TPU v7x, 32 devices: a whole 2x2x4 slice. The times are simulated.
32 devices in a mesh: rep: 2 (over y), fsdp: 16 (over z, x, core).
Axes of the slice: x: 2, y: 2, z: 4, core: 2. Of those that a mesh axis runs over, the one named last changes fastest.
Arguments:
- tokens: bfloat16 [32, 1024, 1024], P(('rep', 'fsdp')), may hold values from -6 to 6
- norm_gain: float32 [1024], replicated, may hold values from 0.25 to 1.75
- in_weight: bfloat16 [1024, 4384], P('fsdp'), may hold values from -0.1875 to 0.1875
- conv_weight: float32 [4, 2304], replicated, may hold values from -3 to 3
- conv_bias: float32 [2304], replicated, may hold values from -0.5 to 0.5
- step_bias: float32 [32], replicated, may hold values from -7 to -1
- decay_log: float32 [32], replicated, may hold values from -1 to 2.5
- skip_gain: float32 [32], replicated, may hold values from 0.5 to 1.5
- out_gain: float32 [2048], replicated, may hold values from 0.25 to 1.75
- out_weight: bfloat16 [2048, 1024], P('fsdp'), may hold values from -0.125 to 0.125
- cotangent: bfloat16 [32, 1024, 1024], P(('rep', 'fsdp')), may hold values from -6 to 6
- teacher: bfloat16 [32, 1024, 1024], P(('rep', 'fsdp')), may hold values from -6 to 6
- segment: int32 [32, 1024], P(('rep', 'fsdp')), may hold values from 0 to 3, never falling along the last dimension, each value on 1 to 512 neighbouring positions
- valid_mask: int32 [32, 1024], P(('rep', 'fsdp')), may hold values from 0 to 1, as said below
Outputs:
- output: bfloat16 [32, 1024, 1024], P(('rep', 'fsdp'))
- loss_value: float32 [], replicated
- grad_tokens: bfloat16 [32, 1024, 1024], P(('rep', 'fsdp'))
- grad_norm_gain: float32 [1024], replicated
- grad_in_weight: float32 [1024, 4384], P('fsdp')
- grad_conv_weight: float32 [4, 2304], replicated
- grad_conv_bias: float32 [2304], replicated
- grad_step_bias: float32 [32], replicated
- grad_decay_log: float32 [32], replicated
- grad_skip_gain: float32 [32], replicated
- grad_out_gain: float32 [2048], replicated
- grad_out_weight: float32 [2048, 1024], P('fsdp')
Inputs may be any that keep to these rules, and one draw needn't show every extreme that they name: `segment`: within each sequence the number is 0 at the start and never falls; each document has 1 to 512 positions, one has exactly that many. `valid_mask`: each sequence has 1 on a leading run of 341 positions or more and 0 after it.
All inputs are finite; a program needn't handle non-finite values.
Results may differ from a plain program's by a relative error of at most 0.0078.
Values may be sent and summed in bfloat16 or wider, within the bound.
A program may use at most 320 MiB of HBM per device.

v0:
```python
import jax
import jax.numpy as jnp
from jax import lax
from jax.sharding import PartitionSpec as P

STRETCH = 256


epsilon = 1e-05


def prenorm(values, gain_vector):
    return (
        values
        * lax.rsqrt(jnp.mean(values * values, axis=1, keepdims=True) + epsilon)
        * gain_vector[None, :]
    )


def convolve(conv_in, segment, conv_weight, conv_bias):
    tap_count = conv_weight.shape[0]
    summed = conv_bias[None, :] + conv_weight[0][None, :] * conv_in
    for offset in range(1, tap_count):
        delayed = jnp.concatenate(
            [jnp.zeros((offset, conv_in.shape[1]), conv_in.dtype), conv_in[:-offset]], axis=0
        )
        same_doc = jnp.concatenate(
            [
                jnp.zeros((offset,), conv_in.dtype),
                (segment[offset:] == segment[:-offset]).astype(conv_in.dtype),
            ],
            axis=0,
        )
        summed = summed + conv_weight[offset][None, :] * delayed * same_doc[:, None]
    return jax.nn.silu(summed)


def block_step(carried, block_data):
    state_in, last_doc, decay_rate = carried
    x_heads, step_size, inputs_b, outputs_c, doc_ids = block_data
    highest = lax.Precision.HIGHEST
    kind = step_size.dtype
    decay_sum = jnp.cumsum(step_size * decay_rate[None, :], axis=0)
    decay_heads = decay_sum.T
    step_heads = step_size.T
    positions = jnp.arange(doc_ids.shape[0])
    causal = (positions[:, None] >= positions[None, :]) & (doc_ids[:, None] == doc_ids[None, :])
    spread = decay_heads[:, :, None] - decay_heads[:, None, :]
    weights = jnp.exp(jnp.where(causal[None, :, :], spread, 0.0)) * causal[None, :, :].astype(kind)
    scores = jnp.dot(outputs_c, inputs_b.T, precision=highest)
    mixing = scores[None, :, :] * weights * step_heads[:, None, :]
    within_block = jnp.einsum("hij,jhp->ihp", mixing, x_heads, precision=highest)
    keep_prev = (doc_ids == last_doc).astype(kind)
    from_state = (
        jnp.einsum("in,hpn->ihp", outputs_c, state_in, precision=highest)
        * (jnp.exp(decay_sum) * keep_prev[:, None])[:, :, None]
    )
    end_doc = doc_ids[-1]
    to_end = (
        jnp.exp(decay_sum[-1][None, :] - decay_sum)
        * (doc_ids == end_doc).astype(kind)[:, None]
        * step_size
    )
    carry_on = jnp.exp(decay_sum[-1]) * (end_doc == last_doc).astype(kind)
    state_out = state_in * carry_on[:, None, None] + jnp.einsum(
        "jh,jhp,jn->hpn", to_end, x_heads, inputs_b, precision=highest
    )
    return ((state_out, end_doc, decay_rate), within_block + from_state)


def ssd_mixer(
    projected, segment, conv_weight, conv_bias, step_bias, decay_log, skip_gain, out_gain
):
    length = projected.shape[0]
    inner_width = out_gain.shape[0]
    head_count = step_bias.shape[0]
    conv_width = conv_weight.shape[1]
    state_width = (conv_width - inner_width) // 2
    head_width = inner_width // head_count
    block_rows = min(STRETCH, length)
    blocks = length // block_rows
    gate_part = projected[:, :inner_width]
    conv_out = convolve(
        projected[:, inner_width : inner_width + conv_width], segment, conv_weight, conv_bias
    )
    step_size = jax.nn.softplus(projected[:, inner_width + conv_width :] + step_bias[None, :])
    decay_rate = -jnp.exp(decay_log)
    x_heads = conv_out[:, :inner_width].reshape(length, head_count, head_width)
    inputs_b = conv_out[:, inner_width : inner_width + state_width]
    outputs_c = conv_out[:, inner_width + state_width :]
    block_data = (
        x_heads.reshape(blocks, block_rows, head_count, head_width),
        step_size.reshape(blocks, block_rows, head_count),
        inputs_b.reshape(blocks, block_rows, state_width),
        outputs_c.reshape(blocks, block_rows, state_width),
        segment.reshape(blocks, block_rows),
    )
    start_carry = (
        jnp.zeros((head_count, head_width, state_width), projected.dtype),
        jnp.array(-1, jnp.int32),
        decay_rate,
    )
    ignored, mixed_out = lax.scan(jax.checkpoint(block_step), start_carry, block_data)
    ssd_out = mixed_out.reshape(length, head_count, head_width) + skip_gain[None, :, None] * x_heads
    gated = ssd_out.reshape(length, inner_width) * jax.nn.silu(gate_part)
    return (
        gated
        * lax.rsqrt(jnp.mean(gated * gated, axis=1, keepdims=True) + epsilon)
        * out_gain[None, :]
    )


def on_device(
    tokens,
    norm_gain,
    in_weight,
    conv_weight,
    conv_bias,
    step_bias,
    decay_log,
    skip_gain,
    out_gain,
    out_weight,
    cotangent,
    teacher,
    segment,
    valid_mask,
):
    seq_here, seq_len, model_width = tokens.shape
    token_rows = seq_here * seq_len
    proj_width = in_weight.shape[1]
    rep_count = lax.axis_size("rep")
    fsdp_count = lax.axis_size("fsdp")
    loss_weight = float(token_rows * rep_count * fsdp_count * model_width // 8)
    contract_rows = (((0,), (0,)), ((), ()))
    contract_cols = (((1,), (1,)), ((), ()))
    inputs = tokens.reshape(token_rows, model_width).astype(jnp.float32)
    valid_rows = valid_mask.reshape(token_rows).astype(jnp.float32)
    local_count = jnp.sum(valid_rows)
    normed, prenorm_back = jax.vjp(prenorm, inputs, norm_gain)
    normed_low = normed.astype(jnp.bfloat16)
    columns = normed_low
    projected = jnp.dot(
        columns,
        lax.all_gather(in_weight, "fsdp", axis=0, tiled=True),
        preferred_element_type=jnp.float32,
    )

    def run_mixer(projected_all, conv_taps, conv_shift, bias_step, log_decay, gain_skip, gain_out):
        batched = jax.vmap(ssd_mixer, in_axes=(0, 0, None, None, None, None, None, None))(
            projected_all.reshape(seq_here, seq_len, proj_width),
            segment,
            conv_taps,
            conv_shift,
            bias_step,
            log_decay,
            gain_skip,
            gain_out,
        )
        return batched.reshape(token_rows, batched.shape[2])

    mixed, mixer_back = jax.vjp(
        run_mixer, projected, conv_weight, conv_bias, step_bias, decay_log, skip_gain, out_gain
    )
    mixed_low = mixed.astype(jnp.bfloat16)
    columns = mixed_low
    branch = jnp.dot(
        columns,
        lax.all_gather(out_weight, "fsdp", axis=0, tiled=True),
        preferred_element_type=jnp.float32,
    )
    result = inputs + branch
    target_rows = teacher.reshape(token_rows, model_width).astype(jnp.float32)
    residual_error = result - target_rows
    local_squares = jnp.sum(valid_rows[:, None] * residual_error * residual_error)
    total_count, loss_total = lax.psum((local_count, local_squares), ("rep", "fsdp"))
    denominator = total_count * model_width
    loss_value = loss_total / denominator
    cotan_rows = cotangent.reshape(token_rows, model_width).astype(jnp.float32)
    grad_result = valid_rows[:, None] * (
        cotan_rows + 2.0 * loss_weight * residual_error / denominator
    )
    grad_branch = grad_result.astype(jnp.bfloat16)
    columns = mixed_low
    grad_out_shard = lax.psum_scatter(
        lax.dot_general(columns, grad_branch, contract_rows, preferred_element_type=jnp.float32),
        "fsdp",
        scatter_dimension=0,
        tiled=True,
    )
    grad_mixed = lax.dot_general(
        grad_branch,
        lax.all_gather(out_weight, "fsdp", axis=0, tiled=True),
        contract_cols,
        preferred_element_type=jnp.float32,
    )
    (
        grad_projected,
        grad_conv_weight,
        grad_conv_bias,
        grad_step_bias,
        grad_decay_log,
        grad_skip_gain,
        grad_out_gain,
    ) = mixer_back(grad_mixed)
    grad_projected_low = grad_projected.astype(jnp.bfloat16)
    columns = normed_low
    grad_in_shard = lax.psum_scatter(
        lax.dot_general(
            columns, grad_projected_low, contract_rows, preferred_element_type=jnp.float32
        ),
        "fsdp",
        scatter_dimension=0,
        tiled=True,
    )
    grad_normed = lax.dot_general(
        grad_projected_low,
        lax.all_gather(in_weight, "fsdp", axis=0, tiled=True),
        contract_cols,
        preferred_element_type=jnp.float32,
    )
    grad_inputs, grad_norm_gain = prenorm_back(grad_normed)
    grad_tokens = (grad_result + grad_inputs).astype(jnp.bfloat16).reshape(tokens.shape)
    grad_in_weight, grad_out_weight = (
        lax.psum(grad_in_shard.astype(jnp.bfloat16), "rep").astype(jnp.float32),
        lax.psum(grad_out_shard.astype(jnp.bfloat16), "rep").astype(jnp.float32),
    )
    summed_small = lax.psum(
        (
            grad_norm_gain,
            grad_conv_weight,
            grad_conv_bias,
            grad_step_bias,
            grad_decay_log,
            grad_skip_gain,
            grad_out_gain,
        ),
        ("rep", "fsdp"),
    )
    output = result.astype(jnp.bfloat16).reshape(tokens.shape)
    return (
        output,
        loss_value,
        grad_tokens,
        summed_small[0],
        grad_in_weight,
        summed_small[1],
        summed_small[2],
        summed_small[3],
        summed_small[4],
        summed_small[5],
        summed_small[6],
        grad_out_weight,
    )


def solution(mesh):
    return jax.shard_map(
        on_device,
        mesh=mesh,
        in_specs=(
            P(("rep", "fsdp"), None, None),
            P(),
            P("fsdp", None),
            P(),
            P(),
            P(),
            P(),
            P(),
            P(),
            P("fsdp", None),
            P(("rep", "fsdp"), None, None),
            P(("rep", "fsdp"), None, None),
            P(("rep", "fsdp"), None),
            P(("rep", "fsdp"), None),
        ),
        out_specs=(
            P(("rep", "fsdp"), None, None),
            P(),
            P(("rep", "fsdp"), None, None),
            P(),
            P("fsdp", None),
            P(),
            P(),
            P(),
            P(),
            P(),
            P(),
            P("fsdp", None),
        ),
        check_vma=False,
    )
```

profile of v0, /device:TPU:0, one launch (start us, length us, event | category | flops | bytes accessed | tf_op | source)
XLA Modules:
  0.0 1649.2 jit_solution(16716333693821393875)
XLA Ops:
  18.1 43.1 %psum.78 = f32[]{:T(128)} all-reduce(f32[]{:T(128)} %convert_reduce_fusion), channel_id=1, replica_groups=mesh['rep'=2,'fsdp'=16] {'rep','fsdp'}, use_global_device_ids=true, to_apply=%region_9.10 | all-reduce | flops 1 | bytes 8 | tf_op jit(solution)/shard_map/psum | solution.py:176
  62.0 32.2 %all-gather.3.cloned.1.call-done = bf16[1024,4384]{1,0:T(8,128)(2,1)} async-done(((bf16[64,4384]{1,0:T(8,128)(2,1)}), bf16[1024,4384]{1,0:T(8,128)(2,1)}) %all-gather.3.cloned.1.call-update) | async-done | bytes 8978448 | tf_op jit(solution)/shard_map/all_gather | solution.py:145
  94.2 17.5 %convolution_bitcast_fusion.1 = f32[1,1024,4384]{1,2,0:T(8,128)} fusion(bf16[1024,4384]{1,0:T(8,128)(2,1)} %all-gather.3.cloned.1.call-done, bf16[1,1024,1024]{2,1,0:T(8,128)(2,1)} %param.18, f32[1024]{0:T(1024)} %param.19, f32[1024]{0:T(1024)S(1)} %fusion.168), kind=kOutput, calls=%fused_computation.183 | convolution fusion | flops 9198108672 | bytes 29040640 | tf_op jit(solution)/shard_map/dot_general | solution.py:143
  116.4 12.8 slice.174
  138.5 17.2 %fusion.125 = (f32[1,1024,2304]{1,2,0:T(8,128)S(1)}, f32[1,1024,2304]{1,2,0:T(8,128)}) fusion(f32[1024]{0:T(1024)S(1)} %bitcast.694, f32[1,1021,2304]{1,2,0:T(8,128)} %slice.175, f32[2304]{0:T(1024)S(1)} %get-tuple-element.762, f32[1024]{0:T(1024)S(1)} %bitcast.690, f32[1,1022,2304]{1,2,0:T(8,128)} %slice.174, f32[2304]{0:T(1024)S(1)} %get-tuple-element.763, ...), kind=kLoop, calls=%fused_computation.195 | loop fusion | flops 35389440 | bytes 56626176 | tf_op jit(solution)/shard_map/jvp(vmap(jit(silu)))/mul | solution.py:35
  189.8 307.0 %while.47 = (s32[]{:T(128)}, f32[1,32,64,128]{3,2,1,0:T(8,128)S(1)}, s32[1]{0:T(128)}, f32[4,1,256,32,64]{2,0,4,3,1:T(4,128)}, f32[4,1,32,64,128]{4,3,2,1,0:T(8,...) while((s32[]{:T(128)}, ...), condition=%wide.region_4.5_spmd.clone, body=%wide.region_1.4_spmd.clone.sunk | while | flops 3336619008 | bytes 26952952 | solution.py:103
  211.8 45.6 %dynamic_update_slice.82 = f32[4,1,256,32,64]{2,0,4,3,1:T(4,128)} dynamic-update-slice(f32[4,1,256,32,64]{2,0,4,3,1:T(4,128)} %get-tuple-element.1155, f32[1,1,256,32,64]{2,0,4,3,1:T(1,128)S(1)} %copy.315, s32[]{:T(128)} %get-tuple-element.1152, s32[]{:T(128)} %constant.138.clone.1..sunk, s32[]{:T(128)} %constant.138.clone.1..sunk, s32[]{:T(128)} %constant.138.clone.1..sunk, s32[]{:T(128)} %constant.138.clone.1..sunk) | dynamic-update-slice | bytes 4194308 | tf_op jit(solution)/shard_map/jvp(vmap())/while/body/jit(dynamic_update_index_in_dim)/dynamic_update_slice | solution.py:103
  271.0 11.1 fusion.246
  288.4 45.6 %dynamic_update_slice.82 = f32[4,1,256,32,64]{2,0,4,3,1:T(4,128)} dynamic-update-slice(f32[4,1,256,32,64]{2,0,4,3,1:T(4,128)} %get-tuple-element.1155, f32[1,1,256,32,64]{2,0,4,3,1:T(1,128)S(1)} %copy.315, s32[]{:T(128)} %get-tuple-element.1152, s32[]{:T(128)} %constant.138.clone.1..sunk, s32[]{:T(128)} %constant.138.clone.1..sunk, s32[]{:T(128)} %constant.138.clone.1..sunk, s32[]{:T(128)} %constant.138.clone.1..sunk) | dynamic-update-slice | bytes 4194308 | tf_op jit(solution)/shard_map/jvp(vmap())/while/body/jit(dynamic_update_index_in_dim)/dynamic_update_slice | solution.py:103
  347.7 11.1 fusion.246
  365.1 45.6 %dynamic_update_slice.82 = f32[4,1,256,32,64]{2,0,4,3,1:T(4,128)} dynamic-update-slice(f32[4,1,256,32,64]{2,0,4,3,1:T(4,128)} %get-tuple-element.1155, f32[1,1,256,32,64]{2,0,4,3,1:T(1,128)S(1)} %copy.315, s32[]{:T(128)} %get-tuple-element.1152, s32[]{:T(128)} %constant.138.clone.1..sunk, s32[]{:T(128)} %constant.138.clone.1..sunk, s32[]{:T(128)} %constant.138.clone.1..sunk, s32[]{:T(128)} %constant.138.clone.1..sunk) | dynamic-update-slice | bytes 4194308 | tf_op jit(solution)/shard_map/jvp(vmap())/while/body/jit(dynamic_update_index_in_dim)/dynamic_update_slice | solution.py:103
  441.9 45.6 %dynamic_update_slice.82 = f32[4,1,256,32,64]{2,0,4,3,1:T(4,128)} dynamic-update-slice(f32[4,1,256,32,64]{2,0,4,3,1:T(4,128)} %get-tuple-element.1155, f32[1,1,256,32,64]{2,0,4,3,1:T(1,128)S(1)} %copy.315, s32[]{:T(128)} %get-tuple-element.1152, s32[]{:T(128)} %constant.138.clone.1..sunk, s32[]{:T(128)} %constant.138.clone.1..sunk, s32[]{:T(128)} %constant.138.clone.1..sunk, s32[]{:T(128)} %constant.138.clone.1..sunk) | dynamic-update-slice | bytes 4194308 | tf_op jit(solution)/shard_map/jvp(vmap())/while/body/jit(dynamic_update_index_in_dim)/dynamic_update_slice | solution.py:103
  507.6 13.3 multiply_reduce_fusion.8
  520.9 14.2 fusion.149
  544.4 12.6 fusion.129
  557.0 20.7 %multiply_reduce_fusion.7 = (f32[2048]{0:T(1024)}, f32[1,1024,2048]{1,2,0:T(8,128)}, f32[1,1024,2048]{1,2,0:T(8,128)}) fusion(f32[1,1024,2304]{1,2,0:T(8,128)} %copy-done.1, f32[1,1024,4384]{1,2,0:T(8,128)} %convolution_bitcast_fusion.1, f32[1,1024,2048]{1,2,0:T(8,128)} %get-tuple-element.850, f32[1024]{0:T(1024)S(1)} %multiply_multiply_fusion.2, ...), kind=kLoop, calls=%fused_computation.204 | loop fusion | flops 44038144 | bytes 58753024 | tf_op jit(solution)/shard_map/transpose(jvp(vmap()))/reduce_sum | solution.py:104
  596.0 680.5 %while.48 = (s32[]{:T(128)}, f32[1,32,64,128]{3,2,1,0:T(8,128)}, f32[32]{0:T(128)}, f32[4,1,256,32,64]{2,0,4,3,1:T(4,128)}, f32[4,1,256,32]{3,2,1,0:T(8,128)}, /...) while((s32[]{:T(128)}, f32[1,32,64,128]{3,2,1,0:T(8,128)}, ...), condition=%wide.region_24.25_spmd.clone, body=%wide.region_11.24_spmd.clone.sunk | while | flops 7600292864 | bytes 74608752 | solution.py:103
  653.5 16.3 fusion.269
  730.1 45.8 %dynamic_update_slice.87 = f32[4,1,256,32,64]{2,0,4,3,1:T(4,128)} dynamic-update-slice(f32[4,1,256,32,64]{2,0,4,3,1:T(4,128)} %get-tuple-element.1207, f32[1,1,256,32,64]{2,0,4,3,1:T(1,128)} %copy.334, s32[]{:T(128)S(6)} %sub.239, s32[]{:T(128)} %constant.138.clone.1..sunk.1, s32[]{:T(128)} %constant.138.clone.1..sunk.1, s32[]{:T(128)} %constant.138.clone.1..sunk.1, s32[]{:T(128)} %constant.138.clone.1..sunk.1) | dynamic-update-slice | bytes 4194308 | tf_op jit(solution)/shard_map/transpose(jvp(vmap()))/while/body/jit(dynamic_update_index_in_dim)/dynamic_update_slice | solution.py:103
  819.2 16.3 fusion.269
  895.7 45.8 %dynamic_update_slice.87 = f32[4,1,256,32,64]{2,0,4,3,1:T(4,128)} dynamic-update-slice(f32[4,1,256,32,64]{2,0,4,3,1:T(4,128)} %get-tuple-element.1207, f32[1,1,256,32,64]{2,0,4,3,1:T(1,128)} %copy.334, s32[]{:T(128)S(6)} %sub.239, s32[]{:T(128)} %constant.138.clone.1..sunk.1, s32[]{:T(128)} %constant.138.clone.1..sunk.1, s32[]{:T(128)} %constant.138.clone.1..sunk.1, s32[]{:T(128)} %constant.138.clone.1..sunk.1) | dynamic-update-slice | bytes 4194308 | tf_op jit(solution)/shard_map/transpose(jvp(vmap()))/while/body/jit(dynamic_update_index_in_dim)/dynamic_update_slice | solution.py:103
  984.8 16.3 fusion.269
  1061.3 45.8 %dynamic_update_slice.87 = f32[4,1,256,32,64]{2,0,4,3,1:T(4,128)} dynamic-update-slice(f32[4,1,256,32,64]{2,0,4,3,1:T(4,128)} %get-tuple-element.1207, f32[1,1,256,32,64]{2,0,4,3,1:T(1,128)} %copy.334, s32[]{:T(128)S(6)} %sub.239, s32[]{:T(128)} %constant.138.clone.1..sunk.1, s32[]{:T(128)} %constant.138.clone.1..sunk.1, s32[]{:T(128)} %constant.138.clone.1..sunk.1, s32[]{:T(128)} %constant.138.clone.1..sunk.1) | dynamic-update-slice | bytes 4194308 | tf_op jit(solution)/shard_map/transpose(jvp(vmap()))/while/body/jit(dynamic_update_index_in_dim)/dynamic_update_slice | solution.py:103
  1150.4 16.3 fusion.269
  1227.0 45.8 %dynamic_update_slice.87 = f32[4,1,256,32,64]{2,0,4,3,1:T(4,128)} dynamic-update-slice(f32[4,1,256,32,64]{2,0,4,3,1:T(4,128)} %get-tuple-element.1207, f32[1,1,256,32,64]{2,0,4,3,1:T(1,128)} %copy.334, s32[]{:T(128)S(6)} %sub.239, s32[]{:T(128)} %constant.138.clone.1..sunk.1, s32[]{:T(128)} %constant.138.clone.1..sunk.1, s32[]{:T(128)} %constant.138.clone.1..sunk.1, s32[]{:T(128)} %constant.138.clone.1..sunk.1) | dynamic-update-slice | bytes 4194308 | tf_op jit(solution)/shard_map/transpose(jvp(vmap()))/while/body/jit(dynamic_update_index_in_dim)/dynamic_update_slice | solution.py:103
  1299.3 16.1 multiply_reduce_fusion.6
  1315.5 17.7 %multiply_reduce_fusion.5 = (f32[2304]{0:T(1024)S(1)}, f32[1,1024,2304]{1,2,0:T(8,128)}, f32[2304]{0:T(1024)S(1)}, f32[1,1024,2304]{1,2,0:T(8,128)}) fusion(f32[1,1022,2304]{1,2,0:T(8,128)} %slice.174, f32[1,1024,2304]{1,2,0:T(8,128)S(1)} %get-tuple-element.844, f32[1024]{0:T(1024)S(1)} %bitcast.691, f32[1,1023,2304]{1,2,0:T(8,128)} %copy-done.2, ...), kind=kLoop, calls=%fused_computation.191 | loop fusion | flops 14151168 | bytes 47184896 | tf_op jit(solution)/shard_map/transpose(jvp(vmap()))/reduce_sum | solution.py:34
  1363.6 17.1 %fusion.175 = (f32[2304]{0:T(1024)S(1)}, f32[2304]{0:T(1024)S(1)}, f32[1,1024,2304]{1,2,0:T(8,128)}) fusion(f32[1,1024,2304]{1,2,0:T(8,128)S(1)} %get-tuple-element.844, f32[1,1024,4384]{1,2,0:T(8,128)} %convolution_bitcast_fusion.1, f32[2304]{0:T(1024)S(1)} %copy-done.20, f32[1,1023,2304]{1,2,0:T(8,128)} %slice_multiply_fusion, ...), kind=kLoop, calls=%fused_computation.280 | loop fusion | flops 16510464 | bytes 56595456 | tf_op jit(solution)/shard_map/transpose(jvp(vmap()))/reduce_sum | solution.py:22
  1380.7 18.4 %fusion.153 = f32[1024,4384]{1,0:T(8,128)} fusion(bf16[1,1024,1024]{2,1,0:T(8,128)(2,1)S(1)} %copy-done.8, f32[1024]{0:T(1024)S(1)} %copy-done.42, f32[1024]{0:T(1024)S(1)} %copy-done.38, f32[1,1024,2048]{1,2,0:T(8,128)} %get-tuple-element.871, f32[1,1024,2304]{1,2,0:T(8,128)} %get-tuple-element.872, f32[1,1024,32]{1,2,0:T(8,128)S(1)} %get-tuple-element.841), kind=kOutput, calls=%fused_computation.241 | convolution fusion | flops 9211576320 | bytes 38019072 | tf_op jit(solution)/shard_map/dot_general | solution.py:209
  1399.3 20.1 %fusion.140 = (f32[1024]{0:T(1024)S(1)}, f32[1024]{0:T(1024)S(1)}, f32[1024,1024]{1,0:T(8,128)}) fusion(bf16[1,1024,1024]{2,1,0:T(8,128)(2,1)S(1)} %copy-done.8, f32[1024]{0:T(1024)S(1)} %copy-done.38, f32[1024]{0:T(1024)S(1)} %copy-done.42, bf16[1024,4384]{1,0:T(8,128)(2,1)} %all-gather.3.cloned.1.call-done, f32[1,1024,2048]{1,2,0:T(8,128)} %get-tuple-element.871, ...), kind=kOutput, calls=%fused_computation.226 | convolution fusion | flops 9214720000 | bytes 33243136 | tf_op jit(solution)/shard_map/dot_general | solution.py:216
  1421.2 166.4 %reduce-scatter.3.cloned.1.call-done = f32[64,4384]{1,0:T(8,128)} async-done(((f32[1024,4384]{1,0:T(8,128)}), f32[64,4384]{1,0:T(8,128)}) %reduce-scatter.3.cloned.1.call-update) | async-done | bytes 1122320 | tf_op jit(solution)/shard_map/reduce_scatter | solution.py:208
  1590.7 41.0 %all-reduce.20 = (f32[]{:T(128)}, f32[1024]{0:T(1024)}, f32[4,2304]{1,0:T(4,128)}, f32[2304]{0:T(1024)}, f32[32]{0:T(128)}, /*index=5*/f32[32]{0:T(128)}, f32[32]{0:T(128)}, f32[2048]{0:T(1024)}) all-reduce(f32[]{:T(128)} %get-tuple-element.878, f32[1024]{0:T(1024)S(1)} %get-tuple-element.758, ...), channel_id=1, replica_groups=mesh['rep'=2,'fsdp'=16] {'rep','fsdp'}, use_global_device_ids=true, to_apply=%region_7.8 | all-reduce | flops 14689 | bytes 117512 | tf_op jit(solution)/shard_map/psum | solution.py:176
  (614 shorter events, 667.3 us)
Async XLA Ops:
  7.2 87.0 %all-gather.3.cloned.1.call-start = ((), (), s32[]{:S(2)}) async-start(), calls=%async_computation.2 | async-start | bytes 9748480 | tf_op jit(solution)/shard_map/all_gather | solution.py:145
  7.9 512.9 %all-gather.5.cloned.1.call-start = ((), (), s32[]{:S(2)}) async-start(), calls=%async_computation.3 | async-start | bytes 4456448 | tf_op jit(solution)/shard_map/all_gather | solution.py:169
  8.7 1410.7 %reduce-scatter.5.cloned.1.call-start = ((), (), s32[]{:S(2)}) async-start(), calls=%async_computation.5 | async-start | bytes 8912896 | tf_op jit(solution)/shard_map/reduce_scatter | solution.py:185
  15.4 96.3 %copy-start.37 = (f32[1024]{0:T(1024)}, f32[1024]{0:T(1024)S(1)}, u32[]{:S(2)}) copy-start(f32[1024]{0:T(1024)S(1)} %fusion.168) | copy-start | bytes 12292
  16.4 122.0 %copy-start.19 = (f32[2304]{0:T(1024)}, f32[2304]{0:T(1024)S(1)}, u32[]{:S(2)}) copy-start(f32[2304]{0:T(1024)S(1)} %get-tuple-element.760) | copy-start | bytes 27652
  16.4 122.0 %copy-start.21 = (f32[2304]{0:T(1024)}, f32[2304]{0:T(1024)S(1)}, u32[]{:S(2)}) copy-start(f32[2304]{0:T(1024)S(1)} %get-tuple-element.762) | copy-start | bytes 27652
  16.4 122.0 %copy-start.23 = (f32[2304]{0:T(1024)}, f32[2304]{0:T(1024)S(1)}, u32[]{:S(2)}) copy-start(f32[2304]{0:T(1024)S(1)} %get-tuple-element.761) | copy-start | bytes 27652
  16.5 122.0 %copy-start.25 = (f32[2304]{0:T(1024)}, f32[2304]{0:T(1024)S(1)}, u32[]{:S(2)}) copy-start(f32[2304]{0:T(1024)S(1)} %get-tuple-element.763) | copy-start | bytes 27652
  16.5 121.9 %copy-start.28 = (f32[1,1024]{1,0:T(1,128)}, f32[1,1024]{1,0:T(1,128)S(1)}, u32[]{:S(2)}) copy-start(f32[1,1024]{1,0:T(1,128)S(1)} %pad_convert_fusion.1) | copy-start | bytes 12292
  16.6 121.8 %copy-start.34 = (f32[1,1024]{1,0:T(1,128)}, f32[1,1024]{1,0:T(1,128)S(1)}, u32[]{:S(2)}) copy-start(f32[1,1024]{1,0:T(1,128)S(1)} %pad_convert_fusion) | copy-start | bytes 12292
  18.1 538.9 %copy-start.17 = (f32[2048]{0:T(1024)}, f32[2048]{0:T(1024)S(1)}, u32[]{:S(2)}) copy-start(f32[2048]{0:T(1024)S(1)} %mul.950) | copy-start | bytes 24580
  61.3 77.1 %copy-start.30 = (f32[1,1024]{1,0:T(1,128)}, f32[1,1024]{1,0:T(1,128)S(1)}, u32[]{:S(2)}) copy-start(f32[1,1024]{1,0:T(1,128)S(1)} %add_convert_fusion.1) | copy-start | bytes 12292
  544.0 1043.6 %reduce-scatter.3.cloned.1.call-start = ((), (), s32[]{:S(2)}) async-start(), calls=%async_computation.4 | async-start | bytes 19496960 | tf_op jit(solution)/shard_map/reduce_scatter | solution.py:208
  670.8 29.9 %copy-start.16 = (f32[1,256]{1,0:T(1,128)S(1)}, f32[1,256]{1,0:T(1,128)}, u32[]{:S(2)}) copy-start(f32[1,256]{1,0:T(1,128)} %copy-done.15) | copy-start | bytes 3076 | tf_op jit(solution)/shard_map/transpose(jvp(vmap()))/while
  717.2 58.8 %copy-start.48 = (f32[32]{0:T(128)S(1)}, f32[32]{0:T(128)}, u32[]{:S(2)}) copy-start(f32[32]{0:T(128)} %broadcast_select_fusion.5) | copy-start | bytes 388 | tf_op jit(solution)/shard_map/transpose(jvp(vmap()))/while
  717.2 59.4 %copy-start.9 = (f32[256,32]{0,1:T(8,128)S(1)}, f32[256,32]{0,1:T(8,128)}, u32[]{:S(2)}) copy-start(f32[256,32]{0,1:T(8,128)} %copy.322) | copy-start | bytes 98308 | tf_op jit(solution)/shard_map/transpose(jvp(vmap()))/while
  726.6 52.7 %copy-start.47 = (s32[4,1]{0,1:T(1,128)S(1)}, s32[4,1]{0,1:T(1,128)}, u32[]{:S(2)}) copy-start(s32[4,1]{0,1:T(1,128)} %copy-done.46) | copy-start | bytes 52 | tf_op jit(solution)/shard_map/transpose(jvp(vmap()))/while
  882.8 58.8 %copy-start.48 = (f32[32]{0:T(128)S(1)}, f32[32]{0:T(128)}, u32[]{:S(2)}) copy-start(f32[32]{0:T(128)} %broadcast_select_fusion.5) | copy-start | bytes 388 | tf_op jit(solution)/shard_map/transpose(jvp(vmap()))/while
  882.8 59.4 %copy-start.9 = (f32[256,32]{0,1:T(8,128)S(1)}, f32[256,32]{0,1:T(8,128)}, u32[]{:S(2)}) copy-start(f32[256,32]{0,1:T(8,128)} %copy.322) | copy-start | bytes 98308 | tf_op jit(solution)/shard_map/transpose(jvp(vmap()))/while
  892.2 52.7 %copy-start.47 = (s32[4,1]{0,1:T(1,128)S(1)}, s32[4,1]{0,1:T(1,128)}, u32[]{:S(2)}) copy-start(s32[4,1]{0,1:T(1,128)} %copy-done.46) | copy-start | bytes 52 | tf_op jit(solution)/shard_map/transpose(jvp(vmap()))/while
  1002.1 29.9 %copy-start.16 = (f32[1,256]{1,0:T(1,128)S(1)}, f32[1,256]{1,0:T(1,128)}, u32[]{:S(2)}) copy-start(f32[1,256]{1,0:T(1,128)} %copy-done.15) | copy-start | bytes 3076 | tf_op jit(solution)/shard_map/transpose(jvp(vmap()))/while
  1048.4 58.8 %copy-start.48 = (f32[32]{0:T(128)S(1)}, f32[32]{0:T(128)}, u32[]{:S(2)}) copy-start(f32[32]{0:T(128)} %broadcast_select_fusion.5) | copy-start | bytes 388 | tf_op jit(solution)/shard_map/transpose(jvp(vmap()))/while
  1048.4 59.4 %copy-start.9 = (f32[256,32]{0,1:T(8,128)S(1)}, f32[256,32]{0,1:T(8,128)}, u32[]{:S(2)}) copy-start(f32[256,32]{0,1:T(8,128)} %copy.322) | copy-start | bytes 98308 | tf_op jit(solution)/shard_map/transpose(jvp(vmap()))/while
  1057.9 52.7 %copy-start.47 = (s32[4,1]{0,1:T(1,128)S(1)}, s32[4,1]{0,1:T(1,128)}, u32[]{:S(2)}) copy-start(s32[4,1]{0,1:T(1,128)} %copy-done.46) | copy-start | bytes 52 | tf_op jit(solution)/shard_map/transpose(jvp(vmap()))/while
  1214.0 58.8 %copy-start.48 = (f32[32]{0:T(128)S(1)}, f32[32]{0:T(128)}, u32[]{:S(2)}) copy-start(f32[32]{0:T(128)} %broadcast_select_fusion.5) | copy-start | bytes 388 | tf_op jit(solution)/shard_map/transpose(jvp(vmap()))/while
  1214.0 59.4 %copy-start.9 = (f32[256,32]{0,1:T(8,128)S(1)}, f32[256,32]{0,1:T(8,128)}, u32[]{:S(2)}) copy-start(f32[256,32]{0,1:T(8,128)} %copy.322) | copy-start | bytes 98308 | tf_op jit(solution)/shard_map/transpose(jvp(vmap()))/while
  1223.5 52.7 %copy-start.47 = (s32[4,1]{0,1:T(1,128)S(1)}, s32[4,1]{0,1:T(1,128)}, u32[]{:S(2)}) copy-start(s32[4,1]{0,1:T(1,128)} %copy-done.46) | copy-start | bytes 52 | tf_op jit(solution)/shard_map/transpose(jvp(vmap()))/while
  1399.1 238.3 %all-reduce.24.cloned.1.call-start = ((), (), s32[]{:S(2)}) async-start(), calls=%async_computation.6 | async-start | bytes 1671168 | tf_op jit(solution)/shard_map/psum | solution.py:225
  1399.3 190.5 %copy-start.45 = (f32[32]{0:T(128)S(1)}, f32[32]{0:T(128)}, u32[]{:S(2)}) copy-start(f32[32]{0:T(128)} %param.24) | copy-start | bytes 388
  1399.3 191.2 %copy-start.36 = (f32[2048]{0:T(1024)S(1)}, f32[2048]{0:T(1024)}, u32[]{:S(2)}) copy-start(f32[2048]{0:T(1024)} %get-tuple-element.838) | copy-start | bytes 24580
  1399.3 191.4 %copy-start.41 = (f32[2048]{0:T(1024)S(1)}, f32[2048]{0:T(1024)}, u32[]{:S(2)}) copy-start(f32[2048]{0:T(1024)} %get-tuple-element.754) | copy-start | bytes 24580
  1399.3 233.0 %copy-start.33 = (f32[1024]{0:T(1024)S(1)}, f32[1024]{0:T(1024)}, u32[]{:S(2)}) copy-start(f32[1024]{0:T(1024)} %copy-done.32) | copy-start | bytes 12292
  (55 other events, 655.0 us)
Sparse Core Ops, SparseCore 0:
  10.3 83.8 all-gather.2
  96.3 48.6 all-gather.4
  544.1 103.1 reduce-scatter.4
  1399.2 188.3 reduce-scatter.2
  1591.0 35.2 all-reduce.23
where the time goes:
time: 1680 us; the launch traced here: 1650 us
  local copies, waits for them, and re-layouts  678 us (40%)
  matrix products  361 us (21%)
  other arithmetic  277 us (16%)
  waiting for transfers between devices  200 us (12%)
  blocking collectives  84.1 us (5%)
  loops' own time  31.6 us (2%)
  between operations  17 us (1%)
    dynamic_update_slice x32, local copies, waits for them, and re-layouts, ssd_mixer(): lax.scan(jax.checkpoint(block_step), start_carry, block_data)  413 us
    reduce_scatter x1, waiting for transfers between devices, on_device(): lax.psum_scatter(lax.dot_general(columns, grad_projected_low, contract_ro...  166 us
    dot_general x12, matrix products, block_step(): jnp.einsum('hij,jhp->ihp', mixing, x_heads, precision=highest)  147 us
    psum x2, blocking collectives, on_device(): lax.psum((local_count, local_squares), ('rep', 'fsdp'))  84.1 us
    another operation x88, local copies, waits for them, and re-layouts  62.4 us
    dot_general x16, matrix products, block_step(): jnp.einsum('in,hpn->ihp', outputs_c, state_in, precision=highest)  57.9 us
    dot_general x12, matrix products, block_step(): jnp.einsum('jh,jhp,jn->hpn', to_end, x_heads, inputs_b, precision=highest)  44.2 us
    another operation x37, other arithmetic  40.2 us
  transfers between devices with their start and end apart: 5, of which 2 were waited for; matrix products, arithmetic and copies ran while one was open for 78% of the time, Pallas kernels for 0%

commit v1 on v0

v1 whole, which is shorter than its diff:
```python
import functools

import jax
import jax.numpy as jnp
from jax import lax
from jax.experimental import pallas as pl
from jax.experimental.pallas import tpu as pltpu
from jax.sharding import PartitionSpec as P

CHUNK = 128
LANES = 128
EPS = 1e-05
F32 = jnp.float32
BF16 = jnp.bfloat16
NT = (((1,), (1,)), ((), ()))
TN = (((0,), (0,)), ((), ()))


def mm(a, b):
    return jnp.dot(a, b, preferred_element_type=F32)


def mm_nt(a, b):
    return lax.dot_general(a, b, NT, preferred_element_type=F32)


def mm_tn(a, b):
    return lax.dot_general(a, b, TN, preferred_element_type=F32)


def split2(v):
    high = v.astype(BF16)
    return high, (v - high.astype(F32)).astype(BF16)


def split3(v):
    high = v.astype(BF16)
    rest = v - high.astype(F32)
    mid = rest.astype(BF16)
    return high, mid, (rest - mid.astype(F32)).astype(BF16)


def tri_sum(tri, v):
    heads = v.shape[1]
    parts = mm(tri, jnp.concatenate(split3(v), axis=1))
    return parts[:, :heads] + parts[:, heads : 2 * heads] + parts[:, 2 * heads :]


def sigmoid(v):
    return 0.5 * jnp.tanh(0.5 * v) + 0.5


def softplus(v):
    return jnp.maximum(v, 0.0) + jnp.log1p(jnp.exp(-jnp.abs(v)))


def iota(shape, dim):
    return lax.broadcasted_iota(jnp.int32, shape, dim)


def small_terms(step_raw, step_bias, decay_rate, keep, to_end, rows):
    shifted = step_raw + step_bias
    step = softplus(shifted)
    lower = (iota((rows, rows), 0) >= iota((rows, rows), 1)).astype(BF16)
    cum = tri_sum(lower, step * decay_rate)
    last = cum[rows - 1 : rows, :]
    return shifted, step, cum, jnp.exp(cum) * keep, jnp.exp(last - cum) * to_end


def expand(e_ref, out_ref, step, from_prev, to_end):
    stacked = jnp.concatenate(
        [jnp.concatenate(split2(v), axis=1) for v in (step, from_prev, to_end)], axis=0
    )
    out_ref[...] = mm(stacked, e_ref[...])


def conv_tile(xbuf, cw_ref, cb_ref, marks, cols, rows):
    taps = cw_ref.shape[0]
    pre = cb_ref[:, cols] + cw_ref[0:1, cols] * xbuf[8 : 8 + rows, cols]
    for k in range(1, taps):
        pre = pre + (cw_ref[k : k + 1, cols] * xbuf[8 - k : 8 - k + rows, cols]) * marks[k]
    return pre


def forward_kernel(
    p_ref, prev_ref, aux_ref, seg_ref, cw_ref, cb_ref, bias_ref, rate_ref, skip_ref, gain_ref, e_ref,
    mixed_ref, y_ref, state_out_ref,
    xbuf, ex, state, xs, xdt, xe, bc, yin, gs,
    *, inner, conv_width, heads, width, per_seq,
):
    rows = p_ref.shape[0]
    n = (conv_width - inner) // 2
    tiles = inner // LANES
    conv_tiles = conv_width // LANES

    @pl.when(lax.rem(pl.program_id(0), per_seq) == 0)
    def _():
        state[...] = jnp.zeros_like(state)

    aux = aux_ref[...]
    keep, to_end_mask = aux[:, 7:8], aux[:, 8:9]
    shifted, step, cum, from_prev, to_end = small_terms(
        p_ref[:, inner + conv_width :], bias_ref[...], rate_ref[...], keep, to_end_mask, rows
    )
    expand(e_ref, ex, step, from_prev, to_end)
    cum_t = cum.T
    xbuf[0:8, :] = prev_ref[:, inner : inner + conv_width]
    xbuf[8 : 8 + rows, :] = p_ref[:, inner : inner + conv_width]
    marks = [None] + [jnp.broadcast_to(aux[:, k : k + 1], (rows, LANES)) for k in range(1, cw_ref.shape[0])]
    for c in range(conv_tiles):
        cols = slice(c * LANES, (c + 1) * LANES)
        pre = conv_tile(xbuf, cw_ref, cb_ref, marks, cols, rows)
        act = pre * sigmoid(pre)
        if c < tiles:
            xs[:, cols] = act
            scaled = act * ex[0:rows, cols]
            xdt[:, cols] = scaled.astype(BF16)
            xe[:, cols] = (scaled * ex[2 * rows : 3 * rows, cols]).astype(BF16)
        else:
            bc[:, (c - tiles) * LANES : (c - tiles + 1) * LANES] = act.astype(BF16)
    b, cc = bc[:, :n], bc[:, n:]
    causal = (iota((rows, rows), 0) >= iota((rows, rows), 1)) & (aux[:, 0:1] == seg_ref[0])
    scores = jnp.where(causal, mm_nt(cc, b), 0.0)
    state_low = state[...].astype(BF16)
    state_out_ref[...] = state_low
    yin[...] = mm(cc, state_low)
    state[...] = state[...] * ex[2 * rows - 1 : 2 * rows, :] + mm_tn(b, xe[...])
    lane = iota((1, LANES), 1)
    masks = [(lane < width).astype(BF16), (lane >= width).astype(BF16)]
    total = jnp.zeros((rows, LANES), F32)
    for c in range(tiles):
        cols = slice(c * LANES, (c + 1) * LANES)
        mixing = []
        for h in (2 * c, 2 * c + 1):
            spread = jnp.minimum(cum[:, h : h + 1] - cum_t[h : h + 1, :], 0.0)
            mixing.append((scores * jnp.exp(spread)).astype(BF16))
        x_low = xdt[:, cols]
        y = mm(
            jnp.concatenate(mixing, axis=1), jnp.concatenate([x_low * masks[0], x_low * masks[1]], axis=0)
        ) + ex[rows : 2 * rows, cols] * yin[:, cols]
        y_ref[:, cols] = y
        gate = p_ref[:, cols]
        gated = (y + skip_ref[:, cols] * xs[:, cols]) * (gate * sigmoid(gate))
        gs[:, cols] = gated
        total = total + gated * gated
    inverse = lax.rsqrt(jnp.sum(total, axis=1, keepdims=True) / inner + EPS)
    for c in range(tiles):
        cols = slice(c * LANES, (c + 1) * LANES)
        mixed_ref[:, cols] = (gs[:, cols] * inverse * gain_ref[:, cols]).astype(BF16)


def backward_kernel(
    p_ref, prev_ref, aux_ref, seg_ref, y_ref, state_ref, gm_ref,
    cw_ref, cb_ref, bias_ref, rate_ref, skip_ref, gain_ref, e_ref, et_ref,
    gp_ref, dcw_ref, dcb_ref, dgain_ref, dskip_ref, dsmall_ref,
    xbuf, ex, adj, xs, xdt, xe, bc, slope, dy, dye, dxi, dbuf, r1, r1l, r2, r3,
    *, inner, conv_width, heads, width, per_seq,
):
    rows = p_ref.shape[0]
    n = (conv_width - inner) // 2
    tiles = inner // LANES
    conv_tiles = conv_width // LANES
    taps = cw_ref.shape[0]

    @pl.when(pl.program_id(0) == 0)
    def _():
        for ref in (dcw_ref, dcb_ref, dgain_ref, dskip_ref, dsmall_ref):
            ref[...] = jnp.zeros_like(ref)

    @pl.when(lax.rem(pl.program_id(0), per_seq) == 0)
    def _():
        adj[...] = jnp.zeros_like(adj)
        dbuf[rows : rows + 8, :] = jnp.zeros((8, conv_width), F32)

    def fold(v):
        return jnp.sum(v.reshape(rows // 8, 8, v.shape[1]), axis=0)

    aux = aux_ref[...]
    keep, to_end_mask = aux[:, 7:8], aux[:, 8:9]
    rate = rate_ref[...]
    shifted, step, cum, from_prev, to_end = small_terms(
        p_ref[:, inner + conv_width :], bias_ref[...], rate, keep, to_end_mask, rows
    )
    expand(e_ref, ex, step, from_prev, to_end)
    cum_t = cum.T
    xbuf[0:8, :] = prev_ref[:, inner : inner + conv_width]
    xbuf[8 : 8 + rows, :] = p_ref[:, inner : inner + conv_width]
    marks = [None] + [jnp.broadcast_to(aux[:, k : k + 1], (rows, LANES)) for k in range(1, taps)]
    for c in range(conv_tiles):
        cols = slice(c * LANES, (c + 1) * LANES)
        pre = conv_tile(xbuf, cw_ref, cb_ref, marks, cols, rows)
        sig = sigmoid(pre)
        act = pre * sig
        slope[:, cols] = sig + act * (1.0 - sig)
        if c < tiles:
            xs[:, cols] = act
            scaled = act * ex[0:rows, cols]
            xdt[:, cols] = scaled.astype(BF16)
            xe[:, cols] = (scaled * ex[2 * rows : 3 * rows, cols]).astype(BF16)
        else:
            bc[:, (c - tiles) * LANES : (c - tiles + 1) * LANES] = act.astype(BF16)
    squares = jnp.zeros((rows, LANES), F32)
    cross = jnp.zeros((rows, LANES), F32)
    for c in range(tiles):
        cols = slice(c * LANES, (c + 1) * LANES)
        gate = p_ref[:, cols]
        gated = (y_ref[:, cols] + skip_ref[:, cols] * xs[:, cols]) * (gate * sigmoid(gate))
        squares = squares + gated * gated
        cross = cross + gm_ref[:, cols] * gain_ref[:, cols] * gated
    inverse = lax.rsqrt(jnp.sum(squares, axis=1, keepdims=True) / inner + EPS)
    mean_cross = jnp.sum(cross, axis=1, keepdims=True) / inner * inverse
    for c in range(tiles):
        cols = slice(c * LANES, (c + 1) * LANES)
        gate = p_ref[:, cols]
        sig = sigmoid(gate)
        silu = gate * sig
        x = xs[:, cols]
        y = y_ref[:, cols]
        ssd = y + skip_ref[:, cols] * x
        unit = ssd * silu * inverse
        grad_mixed = gm_ref[:, cols]
        dgain_ref[:, cols] += fold(grad_mixed * unit)
        grad_gated = inverse * (grad_mixed * gain_ref[:, cols] - unit * mean_cross)
        grad_ssd = grad_gated * silu
        gp_ref[:, cols] = (grad_gated * ssd * (sig + silu * (1.0 - sig))).astype(BF16)
        dskip_ref[:, cols] += fold(grad_ssd * x)
        low = grad_ssd.astype(BF16)
        dy[:, cols] = low
        dye[:, cols] = (grad_ssd * ex[rows : 2 * rows, cols]).astype(BF16)
        r1[:, cols] = low
    b, cc = bc[:, :n], bc[:, n:]
    state_low = state_ref[...]
    adj_low = adj[...].astype(BF16)
    carry = ex[2 * rows - 1 : 2 * rows, :]
    grad_c = mm_nt(dye[...], state_low)
    grad_b = mm_nt(xe[...], adj_low)
    dxi[...] = mm(b, adj_low)
    through = jnp.sum(adj[...] * state_low.astype(F32), axis=0, keepdims=True) * carry
    adj[...] = adj[...] * carry + mm_tn(cc, dye[...])
    causal_t = (iota((rows, rows), 0) <= iota((rows, rows), 1)) & (aux[:, 0:1] == seg_ref[0])
    scores_t = jnp.where(causal_t, mm_nt(b, cc), 0.0)
    lane = iota((1, LANES), 1)
    masks = [(lane < width).astype(BF16), (lane >= width).astype(BF16)]
    grad_scores_t = jnp.zeros((rows, rows), F32)
    for c in range(tiles):
        cols = slice(c * LANES, (c + 1) * LANES)
        x_low, dy_low = xdt[:, cols], dy[:, cols]
        grad_mix = mm_nt(jnp.concatenate([x_low * masks[0], x_low * masks[1]], axis=0), dy_low)
        mixing = []
        for i, h in enumerate((2 * c, 2 * c + 1)):
            decay = jnp.exp(jnp.minimum(cum_t[h : h + 1, :] - cum[:, h : h + 1], 0.0))
            mixing.append((scores_t * decay).astype(BF16))
            grad_scores_t = grad_scores_t + grad_mix[i * rows : (i + 1) * rows] * decay
        within = mm(
            jnp.concatenate(mixing, axis=1), jnp.concatenate([dy_low * masks[0], dy_low * masks[1]], axis=0)
        )
        x = xs[:, cols]
        across = ex[2 * rows : 3 * rows, cols] * dxi[:, cols]
        both = within + across
        grad_ssd = dy_low.astype(F32)
        x_scaled = x_low.astype(F32)
        r1[:, cols], r1l[:, cols] = split2(grad_ssd * y_ref[:, cols] - within * x_scaled)
        r2[:, cols] = (across * x_scaled).astype(BF16)
        r3[:, cols] = (both * x).astype(BF16)
        grad_x = skip_ref[:, cols] * grad_ssd + ex[0:rows, cols] * both
        dbuf[0:rows, cols] = grad_x * slope[:, cols]
    grad_scores_t = jnp.where(causal_t, grad_scores_t, 0.0).astype(BF16)
    grad_b = grad_b + mm(grad_scores_t, cc)
    grad_c = grad_c + mm_tn(grad_scores_t, b)
    dbuf[0:rows, inner : inner + n] = grad_b * slope[:, inner : inner + n]
    dbuf[0:rows, inner + n :] = grad_c * slope[:, inner + n :]
    et = et_ref[...]
    sum1 = (mm(r1[...], et) + mm(r1l[...], et))[:, :heads]
    sum2 = mm(r2[...], et)[:, :heads]
    sum3 = mm(r3[...], et)[:, :heads]
    through8 = jnp.broadcast_to(through, (8, inner))
    high, rest = split2(through8)
    const = (mm(high, et) + mm(rest, et))[0:1, :heads]
    upper = (iota((rows, rows), 0) <= iota((rows, rows), 1)).astype(BF16)
    strict = (iota((rows, rows), 0) > iota((rows, rows), 1)).astype(BF16)
    grad_log = (tri_sum(upper, sum1) + tri_sum(strict, sum2) + const) * aux[:, 1:2]
    grad_raw = (sum3 + rate * grad_log) * sigmoid(shifted)
    gp_ref[:, inner + conv_width :] = grad_raw.astype(BF16)
    dsmall_ref[0:8, :] += fold(grad_raw)
    dsmall_ref[8:16, :] += fold(step * grad_log * rate)
    marks_next = [None] + [jnp.broadcast_to(aux[:, 3 + k : 4 + k], (rows, LANES)) for k in range(1, taps)]
    for c in range(conv_tiles):
        cols = slice(c * LANES, (c + 1) * LANES)
        here = dbuf[0:rows, cols]
        out = cw_ref[0:1, cols] * here
        dcb_ref[:, cols] += fold(here)
        dcw_ref[0:8, cols] += fold(here * xbuf[8 : 8 + rows, cols])
        for k in range(1, taps):
            out = out + (cw_ref[k : k + 1, cols] * dbuf[k : k + rows, cols]) * marks_next[k]
            dcw_ref[8 * k : 8 * k + 8, cols] += fold(here * (xbuf[8 - k : 8 - k + rows, cols] * marks[k]))
        gp_ref[:, inner + c * LANES : inner + (c + 1) * LANES] = out.astype(BF16)
    dbuf[rows : rows + 8, :] = dbuf[0:8, :]


def helpers(segment, chunk):
    seqs, length = segment.shape
    blocks = length // chunk
    def same(shift):
        return (segment[:, shift:] == segment[:, :-shift]).astype(F32)
    back = [jnp.pad(same(k), ((0, 0), (k, 0))) for k in (1, 2, 3)]
    ahead = [jnp.pad(same(k), ((0, 0), (0, k))) for k in (1, 2, 3)]
    by_block = segment.reshape(seqs, blocks, chunk)
    ends = by_block[:, :, -1]
    before = jnp.pad(ends[:, :-1], ((0, 0), (1, 0)), constant_values=-1)
    keep = (by_block == before[:, :, None]).astype(F32).reshape(seqs, length)
    to_end = (by_block == ends[:, :, None]).astype(F32).reshape(seqs, length)
    docs = segment.astype(F32)
    columns = [docs, *back, *ahead, keep, to_end] + [jnp.zeros_like(docs)] * 7
    aux = jnp.stack(columns, axis=-1).reshape(seqs * length, 16)
    return aux, docs.reshape(seqs * blocks, 1, chunk)


def head_maps(heads, width):
    inner = heads * width
    owner = jnp.arange(inner) // width
    one = (jnp.arange(heads)[:, None] == owner[None, :]).astype(BF16)
    down = (owner[:, None] == jnp.arange(LANES)[None, :]).astype(BF16)
    return jnp.concatenate([one, one], axis=0), down


def full(shape):
    return pl.BlockSpec(shape, lambda i: (0,) * len(shape))


def scan_forward(p, aux, seg_rows, conv_w, conv_b, bias, rate, skip_row, gain_row, e, per_seq):
    tokens, proj = p.shape
    inner, conv_width, heads = gain_row.shape[1], conv_w.shape[1], bias.shape[1]
    n = (conv_width - inner) // 2
    r = CHUNK
    chunks = tokens // r
    return pl.pallas_call(
        functools.partial(
            forward_kernel, inner=inner, conv_width=conv_width, heads=heads, width=inner // heads, per_seq=per_seq
        ),
        grid=(chunks,),
        in_specs=[
            pl.BlockSpec((r, proj), lambda i: (i, 0)),
            pl.BlockSpec((8, proj), lambda i: (jnp.maximum(i * (r // 8) - 1, 0), 0)),
            pl.BlockSpec((r, 16), lambda i: (i, 0)),
            pl.BlockSpec((1, 1, r), lambda i: (i, 0, 0)),
            full(conv_w.shape), full(conv_b.shape), full(bias.shape), full(rate.shape),
            full(skip_row.shape), full(gain_row.shape), full(e.shape),
        ],
        out_specs=[
            pl.BlockSpec((r, inner), lambda i: (i, 0)),
            pl.BlockSpec((r, inner), lambda i: (i, 0)),
            pl.BlockSpec((n, inner), lambda i: (i, 0)),
        ],
        out_shape=[
            jax.ShapeDtypeStruct((tokens, inner), BF16),
            jax.ShapeDtypeStruct((tokens, inner), F32),
            jax.ShapeDtypeStruct((chunks * n, inner), BF16),
        ],
        scratch_shapes=[
            pltpu.VMEM((r + 8, conv_width), F32),
            pltpu.VMEM((3 * r, inner), F32),
            pltpu.VMEM((n, inner), F32),
            pltpu.VMEM((r, inner), F32),
            pltpu.VMEM((r, inner), BF16),
            pltpu.VMEM((r, inner), BF16),
            pltpu.VMEM((r, 2 * n), BF16),
            pltpu.VMEM((r, inner), F32),
            pltpu.VMEM((r, inner), F32),
        ],
        compiler_params=pltpu.CompilerParams(
            dimension_semantics=("arbitrary",), vmem_limit_bytes=48 * 2**20
        ),
        name="scan_forward",
    )(p, p, aux, seg_rows, conv_w, conv_b, bias, rate, skip_row, gain_row, e)


def scan_backward(p, aux, seg_rows, y, states, grad_mixed, conv_w, conv_b, bias, rate, skip_row, gain_row, e, et, per_seq):
    tokens, proj = p.shape
    inner, conv_width, heads = gain_row.shape[1], conv_w.shape[1], bias.shape[1]
    taps = conv_w.shape[0]
    n = (conv_width - inner) // 2
    r = CHUNK
    chunks = tokens // r
    back = lambda i: (chunks - 1 - i, 0)
    return pl.pallas_call(
        functools.partial(
            backward_kernel, inner=inner, conv_width=conv_width, heads=heads, width=inner // heads, per_seq=per_seq
        ),
        grid=(chunks,),
        in_specs=[
            pl.BlockSpec((r, proj), back),
            pl.BlockSpec((8, proj), lambda i: (jnp.maximum((chunks - 1 - i) * (r // 8) - 1, 0), 0)),
            pl.BlockSpec((r, 16), back),
            pl.BlockSpec((1, 1, r), lambda i: (chunks - 1 - i, 0, 0)),
            pl.BlockSpec((r, inner), back),
            pl.BlockSpec((n, inner), back),
            pl.BlockSpec((r, inner), back),
            full(conv_w.shape), full(conv_b.shape), full(bias.shape), full(rate.shape),
            full(skip_row.shape), full(gain_row.shape), full(e.shape), full(et.shape),
        ],
        out_specs=[
            pl.BlockSpec((r, proj), back),
            full((8 * taps, conv_width)), full((8, conv_width)), full((8, inner)), full((8, inner)), full((16, heads)),
        ],
        out_shape=[
            jax.ShapeDtypeStruct((tokens, proj), BF16),
            jax.ShapeDtypeStruct((8 * taps, conv_width), F32),
            jax.ShapeDtypeStruct((8, conv_width), F32),
            jax.ShapeDtypeStruct((8, inner), F32),
            jax.ShapeDtypeStruct((8, inner), F32),
            jax.ShapeDtypeStruct((16, heads), F32),
        ],
        scratch_shapes=[
            pltpu.VMEM((r + 8, conv_width), F32),
            pltpu.VMEM((3 * r, inner), F32),
            pltpu.VMEM((n, inner), F32),
            pltpu.VMEM((r, inner), F32),
            pltpu.VMEM((r, inner), BF16),
            pltpu.VMEM((r, inner), BF16),
            pltpu.VMEM((r, 2 * n), BF16),
            pltpu.VMEM((r, conv_width), F32),
            pltpu.VMEM((r, inner), BF16),
            pltpu.VMEM((r, inner), BF16),
            pltpu.VMEM((r, inner), F32),
            pltpu.VMEM((r + 8, conv_width), F32),
            pltpu.VMEM((r, inner), BF16),
            pltpu.VMEM((r, inner), BF16),
            pltpu.VMEM((r, inner), BF16),
            pltpu.VMEM((r, inner), BF16),
        ],
        compiler_params=pltpu.CompilerParams(
            dimension_semantics=("arbitrary",), vmem_limit_bytes=56 * 2**20
        ),
        name="scan_backward",
    )(p, p, aux, seg_rows, y, states, grad_mixed, conv_w, conv_b, bias, rate, skip_row, gain_row, e, et)


def rms_scale(values):
    return lax.rsqrt(jnp.mean(values * values, axis=1, keepdims=True) + EPS)


def on_device(
    tokens,
    norm_gain,
    in_weight,
    conv_weight,
    conv_bias,
    step_bias,
    decay_log,
    skip_gain,
    out_gain,
    out_weight,
    cotangent,
    teacher,
    segment,
    valid_mask,
):
    seqs, length, width = tokens.shape
    rows = seqs * length
    every = ("rep", "fsdp")
    devices = lax.axis_size("rep") * lax.axis_size("fsdp")
    loss_weight = float(rows * devices * width // 8)
    valid = valid_mask.reshape(rows, 1).astype(F32)
    total_count = lax.psum(jnp.sum(valid), every)
    denominator = total_count * width

    inputs = tokens.reshape(rows, width).astype(F32)
    scaled = inputs * rms_scale(inputs)
    normed = (scaled * norm_gain[None, :]).astype(BF16)
    w_in = lax.all_gather(in_weight, "fsdp", axis=0, tiled=True)
    w_out = lax.all_gather(out_weight, "fsdp", axis=0, tiled=True)
    projected = mm(normed, w_in)

    heads = step_bias.shape[0]
    head_width = out_gain.shape[0] // heads
    aux, seg_rows = helpers(segment, CHUNK)
    e, et = head_maps(heads, head_width)
    rate = -jnp.exp(decay_log)[None, :]
    skip_row = jnp.repeat(skip_gain, head_width)[None, :]
    per_seq = length // CHUNK
    params = (conv_weight, conv_bias[None, :], step_bias[None, :], rate, skip_row, out_gain[None, :])
    mixed, y, states = scan_forward(projected, aux, seg_rows, *params, e, per_seq)

    result = inputs + mm(mixed, w_out)
    error = result - teacher.reshape(rows, width).astype(F32)
    squares = jnp.sum(valid * error * error)
    cotan = cotangent.reshape(rows, width).astype(F32)
    grad_result = valid * (cotan + 2.0 * loss_weight * error / denominator)
    grad_branch = grad_result.astype(BF16)
    grad_out = mm_tn(mixed, grad_branch).astype(BF16)
    grad_mixed = mm_nt(grad_branch, w_out)
    grad_projected, dcw, dcb, dgain, dskip, dsmall = scan_backward(
        projected, aux, seg_rows, y, states, grad_mixed, *params, e, et, per_seq
    )
    grad_in = mm_tn(normed, grad_projected).astype(BF16)
    grad_normed = mm_nt(grad_projected, w_in)
    grad_scaled = grad_normed * norm_gain[None, :]
    grad_inputs = rms_scale(inputs) * (
        grad_scaled - scaled * jnp.mean(grad_scaled * scaled, axis=1, keepdims=True)
    )
    grad_tokens = (grad_result + grad_inputs).astype(BF16).reshape(tokens.shape)

    def reduce(grad):
        shard = lax.psum_scatter(grad, "fsdp", scatter_dimension=0, tiled=True)
        return lax.psum(shard, "rep").astype(F32)

    small = (
        jnp.sum(grad_normed * scaled, axis=0),
        jnp.sum(dcw.reshape(conv_weight.shape[0], 8, -1), axis=1),
        jnp.sum(dcb, axis=0),
        jnp.sum(dsmall[:8], axis=0),
        jnp.sum(dsmall[8:], axis=0),
        jnp.sum(dskip, axis=0).reshape(heads, head_width).sum(axis=1),
        jnp.sum(dgain, axis=0),
        squares,
    )
    summed = lax.psum(small, every)
    return (
        result.astype(BF16).reshape(tokens.shape),
        summed[7] / denominator,
        grad_tokens,
        summed[0],
        reduce(grad_in),
        summed[1],
        summed[2],
        summed[3],
        summed[4],
        summed[5],
        summed[6],
        reduce(grad_out),
    )


def solution(mesh):
    tokens = P(("rep", "fsdp"), None, None)
    marks = P(("rep", "fsdp"), None)
    shard = P("fsdp", None)
    return jax.shard_map(
        on_device,
        mesh=mesh,
        in_specs=(tokens, P(), shard, P(), P(), P(), P(), P(), P(), shard, tokens, tokens, marks, marks),
        out_specs=(tokens, P(), tokens, P(), shard, P(), P(), P(), P(), P(), P(), shard),
        check_vma=False,
    )
```

time: 1680 us -> 442 us (0.26); the launches traced: 1650 us -> 435 us
  local copies, waits for them, and re-layouts: 678 us -> 8.02 us
  matrix products: 361 us -> 79.8 us
  other arithmetic: 277 us -> 19.1 us
  Pallas kernels: 0 us -> 101 us
  waiting for transfers between devices: 200 us -> 124 us
  loops' own time: 31.6 us -> 0 us
    dynamic_update_slice x32 -> x0, local copies, waits for them, and re-layouts: 413 us -> none  [ssd_mixer(): lax.scan(jax.checkpoint(block_step), start_carry, block_data)]
    dot_general x62 -> x6, matrix products: 361 us -> 79.8 us  [the longest x2 29.3 us: mm_nt(): return lax.dot_general(a, b, NT, preferred_element_type=F32)]
    pallas_call x0 -> x2, Pallas kernels: none -> 101 us  [the longest x1 71.9 us: scan_backward(): pl.pallas_call(functools.partial(backward_kernel, inner=inner, conv_width...]
    reduce_sum x17 -> x8, other arithmetic: 102 us -> 3.67 us  [the longest x1 2.07 us: rms_scale(): return lax.rsqrt(jnp.mean(values * values, axis=1, keepdims=True) + EPS)]
    reduce_scatter x2, waiting for transfers between devices: 166 us -> 89.2 us  [reduce(): shard = lax.psum_scatter(grad, 'fsdp', scatter_dimension=0, tiled=True)]
    mul x44 -> x0, other arithmetic: 71 us -> none  [the longest x6 30.7 us: convolve(): summed = summed + conv_weight[offset][None, :] * delayed * same_doc[:, None]]
    another operation x88 -> x8, local copies, waits for them, and re-layouts: 62.4 us -> 0.55 us  [the longest x7 0.47 us: helpers(): aux = jnp.stack(columns, axis=-1).reshape(seqs * length, 16)]
    another operation x45 -> x0, other arithmetic: 48.3 us -> none
  transfers between devices with their start and end apart: 5 -> 5, of which waited for: 2 -> 3; matrix products, arithmetic and copies ran while one was open for 78% -> 18% of each run, Pallas kernels for 0% -> 23%
where the time goes in v1:
time: 442 us; the launch traced here: 435 us
  waiting for transfers between devices  124 us (28%)
  Pallas kernels  101 us (23%)
  blocking collectives  85.6 us (19%)
  matrix products  79.8 us (18%)
  other arithmetic  19.1 us (4%)
  between operations  17 us (4%)
  local copies, waits for them, and re-layouts  8.02 us (2%)
    reduce_scatter x2, waiting for transfers between devices, reduce(): shard = lax.psum_scatter(grad, 'fsdp', scatter_dimension=0, tiled=True)  89.2 us
    pallas_call x1, Pallas kernels, scan_backward(): pl.pallas_call(functools.partial(backward_kernel, inner=inner, conv_width...  71.9 us
    psum x1, blocking collectives, on_device(): total_count = lax.psum(jnp.sum(valid), every)  43.7 us
    psum x1, blocking collectives, on_device(): summed = lax.psum(small, every)  41.9 us
    all_gather x1, waiting for transfers between devices, on_device(): w_in = lax.all_gather(in_weight, 'fsdp', axis=0, tiled=True)  29.4 us
    dot_general x2, matrix products, mm_nt(): return lax.dot_general(a, b, NT, preferred_element_type=F32)  29.3 us
    pallas_call x1, Pallas kernels, scan_forward(): pl.pallas_call(functools.partial(forward_kernel, inner=inner, conv_width=...  28.8 us
    dot_general x2, matrix products, mm(): return jnp.dot(a, b, preferred_element_type=F32)  28.2 us
  transfers between devices with their start and end apart: 5, of which 3 were waited for; matrix products, arithmetic and copies ran while one was open for 18% of the time, Pallas kernels for 23%

profile of v1, /device:TPU:0, one launch (start us, length us, event | category | flops | bytes accessed | tf_op | source)
XLA Modules:
  0.0 434.7 jit_solution(17868429242040772086)
XLA Ops:
  8.0 0.7 all-gather.5.cloned.1.call-update
  8.7 1.3 convert_reduce_fusion
  10.0 43.7 %psum.78 = f32[]{:T(128)} all-reduce(f32[]{:T(128)} %convert_reduce_fusion), channel_id=1, replica_groups=mesh['rep'=2,'fsdp'=16] {'rep','fsdp'}, use_global_device_ids=true, to_apply=%region_4.5 | all-reduce | flops 1 | bytes 8 | tf_op jit(solution)/shard_map/psum | solution.py:464
  53.7 0.7 convert_element_type.123
  54.4 0.8 slice.44
  55.2 0.7 broadcast_in_dim.8.cb_ref
  56.0 0.7 broadcast_in_dim.10
  56.8 0.8 compare_convert_fusion.4
  57.8 0.8 compare_convert_fusion.2
  58.6 0.8 compare_convert_fusion.3
  59.5 0.7 convert_bitcast_fusion.1
  60.4 0.7 compare_convert_fusion
  62.7 2.1 fusion.12
  65.0 29.4 %all-gather.3.cloned.1.call-done = bf16[1024,4384]{1,0:T(8,128)(2,1)} async-done(((bf16[64,4384]{1,0:T(8,128)(2,1)}), bf16[1024,4384]{1,0:T(8,128)(2,1)}) %all-gather.3.cloned.1.call-update) | async-done | bytes 8978448 | tf_op jit(solution)/shard_map/all_gather | solution.py:470
  94.3 16.0 %fusion.20.p_ref.prev_ref = f32[1024,4384]{1,0:T(8,128)} fusion(bf16[1024,4384]{1,0:T(8,128)(2,1)} %all-gather.3.cloned.1.call-done, bf16[1,1024,1024]{2,1,0:T(8,128)(2,1)S(1)} %copy-done.11, f32[1024]{0:T(1024)S(1)} %copy-done.18, f32[1024]{0:T(1024)S(1)} %add_rsqrt_fusion), kind=kOutput, calls=%fused_computation.29 | convolution fusion | flops 9198108672 | bytes 29040640 | tf_op jit(solution)/shard_map/dot_general | solution.py:20
  110.5 28.8 %scan_forward.1 = (bf16[1024,2048]{1,0:T(8,128)(2,1)S(1)}, f32[1024,2048]{1,0:T(8,128)}, bf16[1024,2048]{1,0:T(8,128)(2,1)}) custom-call(f32[1024,4384]{1,0:T(8,128)} %fusion.20.p_ref.prev_ref, f32[1024,4384]{1,0:T(8,128)} %fusion.20.p_ref.prev_ref, f32[1024,16]{1,0:T(8,128)S(1)} %bitcast.66, f32[8,1,128]{2,1,0:T(1,128)S(1)} %get-tuple-element.47.seg_ref, ...), custom_call_target="tpu_custom_call" | custom-call | tf_op jit(solution)/shard_map/scan_forward/pallas_call | solution.py:336
  139.3 2.0 copy-done.9
  141.2 4.3 all-gather.5.cloned.1.call-done
  145.5 12.2 %fusion.13 = (f32[1024,1024]{1,0:T(8,128)S(1)}, f32[]{:T(128)}, bf16[1,1024,1024]{2,1,0:T(8,128)(2,1)}) fusion(bf16[1,1024,1024]{2,1,0:T(8,128)(2,1)} %param.24, bf16[1,1024,1024]{2,1,0:T(8,128)(2,1)} %param.25, f32[]{:T(128)S(6)} %mul.80, f32[1024]{0:T(1024)S(1)} %bitcast.75, bf16[1024,2048]{1,0:T(8,128)(2,1)} %copy-done.9, ...), kind=kOutput, calls=%fused_computation.19 | convolution fusion | flops 4308598784 | bytes 20975624 | tf_op jit(solution)/shard_map/dot_general | solution.py:20
  157.6 2.0 copy-done.12
  159.6 6.3 %convolution_convert_fusion.1 = bf16[2048,1024]{1,0:T(8,128)(2,1)} fusion(bf16[1024,2048]{1,0:T(8,128)(2,1)S(1)} %copy-done.10, f32[1024,1024]{1,0:T(8,128)S(1)} %get-tuple-element.44), kind=kOutput, calls=%fused_computation.21 | convolution fusion | flops 4298113024 | bytes 12582912 | tf_op jit(solution)/shard_map/dot_general | solution.py:28
  166.0 1.1 fusion.18.et_ref
  167.1 11.5 %fusion.16.gm_ref = f32[1024,2048]{1,0:T(8,128)} fusion(bf16[2048,1024]{1,0:T(8,128)(2,1)} %all-gather.5.cloned.1.call-done, f32[1024,1024]{1,0:T(8,128)} %copy-done.12), kind=kOutput, calls=%fused_computation.26 | convolution fusion | flops 4296015872 | bytes 16777216 | tf_op jit(solution)/shard_map/dot_general | solution.py:24
  178.6 71.9 %scan_backward.1 = (bf16[1024,4384]{1,0:T(8,128)(2,1)}, f32[32,2304]{1,0:T(8,128)}, f32[8,2304]{1,0:T(8,128)}, f32[8,2048]{1,0:T(8,128)}, f32[8,2048]{1,0:T(8,128)}, /*index=5*/f32[16,32]{1,0:T(8,128)}) custom-call(f32[1024,4384]{1,0:T(8,128)} %fusion.20.p_ref.prev_ref, f32[1024,4384]{1,0:T(8,128)} %fusion.20.p_ref.prev_ref, f32[1024,16]{1,0:T(8,128)} %bitcast.67, ...), custom_call_target="tpu_custom_call" | custom-call | tf_op jit(solution)/shard_map/scan_backward/pallas_call | solution.py:385
  250.5 16.1 %convolution_convert_fusion = bf16[1024,4384]{1,0:T(8,128)(2,1)} fusion(bf16[1024,4384]{1,0:T(8,128)(2,1)} %get-tuple-element.24, bf16[1,1024,1024]{2,1,0:T(8,128)(2,1)S(1)} %copy-done.11, f32[1024]{0:T(1024)S(1)} %copy-done.18, f32[1024]{0:T(1024)S(1)} %add_rsqrt_fusion), kind=kOutput, calls=%fused_computation | convolution fusion | flops 9202597888 | bytes 20062208 | tf_op jit(solution)/shard_map/dot_general | solution.py:28
  266.6 0.9 copy-done.13
  267.6 17.8 %fusion.11 = (f32[1024]{0:T(1024)S(1)}, f32[1024]{0:T(1024)S(1)}, f32[1024,1024]{1,0:T(8,128)}) fusion(bf16[1,1024,1024]{2,1,0:T(8,128)(2,1)S(1)} %copy-done.11, f32[1024]{0:T(1024)S(1)} %add_rsqrt_fusion, f32[1024]{0:T(1024)S(1)} %copy-done.18, bf16[1024,4384]{1,0:T(8,128)(2,1)} %get-tuple-element.24, bf16[1024,4384]{1,0:T(8,128)(2,1)} %all-gather.3.cloned.1.call-done), kind=kOutput, calls=%fused_computation.16 | convolution fusion | flops 9201252352 | bytes 24264704 | tf_op jit(solution)/shard_map/dot_general | solution.py:24
  285.4 89.2 %reduce-scatter.3.cloned.1.call-done = bf16[64,4384]{1,0:T(8,128)(2,1)} async-done(((bf16[1024,4384]{1,0:T(8,128)(2,1)}), bf16[64,4384]{1,0:T(8,128)(2,1)}) %reduce-scatter.3.cloned.1.call-update) | async-done | bytes 561168 | tf_op jit(solution)/shard_map/reduce_scatter | solution.py:504
  375.0 41.9 %all-reduce.7 = (f32[]{:T(128)}, f32[1024]{0:T(1024)}, f32[4,2304]{1,0:T(4,128)}, f32[2304]{0:T(1024)}, f32[32]{0:T(128)}, /*index=5*/f32[32]{0:T(128)}, f32[32]{0:T(128)}, f32[2048]{0:T(1024)}) all-reduce(f32[]{:T(128)} %get-tuple-element.45, f32[1024]{0:T(1024)S(1)} %get-tuple-element.30, ...), channel_id=1, replica_groups=mesh['rep'=2,'fsdp'=16] {'rep','fsdp'}, use_global_device_ids=true, to_apply=%region_2.0 | all-reduce | flops 14689 | bytes 117512 | tf_op jit(solution)/shard_map/psum | solution.py:517
  417.6 5.1 %fusion.14 = bf16[1,1024,1024]{2,1,0:T(8,128)(2,1)} fusion(f32[1024,1024]{1,0:T(8,128)} %copy-done.12, f32[1024,1024]{1,0:T(8,128)} %get-tuple-element.57, bf16[1,1024,1024]{2,1,0:T(8,128)(2,1)S(1)} %copy-done.11, f32[1024]{0:T(1024)S(1)} %broadcast_multiply_fusion, f32[1024]{0:T(1024)S(1)} %copy-done.18, f32[1024]{0:T(1024)S(1)} %add_rsqrt_fusion), kind=kLoop, calls=%fused_computation.22 | loop fusion | flops 8388608 | bytes 12595200 | tf_op jit(solution)/shard_map/reshape | solution.py:501
  422.7 1.8 convert_element_type.135
  424.4 2.1 convert_element_type.133
  (71 shorter events, 3.0 us)
Async XLA Ops:
  7.2 87.2 %copy-start.11 = (bf16[1,1024,1024]{2,1,0:T(8,128)(2,1)S(1)}, bf16[1,1024,1024]{2,1,0:T(8,128)(2,1)}, u32[]{:S(2)}) copy-start(bf16[1,1024,1024]{2,1,0:T(8,128)(2,1)} %param.14) | copy-start | bytes 6291460
  7.2 87.2 %copy-start.18 = (f32[1024]{0:T(1024)S(1)}, f32[1024]{0:T(1024)}, u32[]{:S(2)}) copy-start(f32[1024]{0:T(1024)} %param.15) | copy-start | bytes 12292
  7.2 87.1 %all-gather.3.cloned.1.call-start = ((), (), s32[]{:S(2)}) async-start(), calls=%async_computation.2 | async-start | bytes 9748480 | tf_op jit(solution)/shard_map/all_gather | solution.py:470
  7.9 137.5 %all-gather.5.cloned.1.call-start = ((), (), s32[]{:S(2)}) async-start(), calls=%async_computation.3 | async-start | bytes 4456448 | tf_op jit(solution)/shard_map/all_gather | solution.py:471
  8.7 276.8 %reduce-scatter.5.cloned.1.call-start = ((), (), s32[]{:S(2)}) async-start(), calls=%async_computation.5 | async-start | bytes 4456448 | tf_op jit(solution)/shard_map/reduce_scatter | solution.py:504
  56.0 54.4 %copy-start.3 = (f32[1,2304]{1,0:T(1,128)}, f32[1,2304]{1,0:T(1,128)S(1)}, u32[]{:S(2)}) copy-start(f32[1,2304]{1,0:T(1,128)S(1)} %broadcast_in_dim.8.cb_ref) | copy-start | bytes 27652
  56.8 53.6 %copy-start.4 = (f32[1,2048]{1,0:T(1,128)}, f32[1,2048]{1,0:T(1,128)S(1)}, u32[]{:S(2)}) copy-start(f32[1,2048]{1,0:T(1,128)S(1)} %broadcast_in_dim_reshape.3.skip_ref) | copy-start | bytes 24580
  60.2 50.2 %copy-start.5 = (f32[8,1,128]{2,1,0:T(1,128)}, f32[8,1,128]{2,1,0:T(1,128)S(1)}, u32[]{:S(2)}) copy-start(f32[8,1,128]{2,1,0:T(1,128)S(1)} %get-tuple-element.47.seg_ref) | copy-start | bytes 12292
  61.4 49.0 %copy-start = (f32[1,1024,16]{2,1,0:T(8,128)}, f32[1,1024,16]{2,1,0:T(8,128)S(1)}, u32[]{:S(2)}) copy-start(f32[1,1024,16]{2,1,0:T(8,128)S(1)} %copy.54) | copy-start | bytes 196612
  62.7 47.7 %copy-start.8 = (f32[1,32]{1,0:T(1,128)}, f32[1,32]{1,0:T(1,128)S(1)}, u32[]{:S(2)}) copy-start(f32[1,32]{1,0:T(1,128)S(1)} %negate_bitcast_fusion.rate_ref) | copy-start | bytes 388
  64.9 45.5 %copy-start.1 = (bf16[64,2048]{1,0:T(8,128)(2,1)}, bf16[64,2048]{1,0:T(8,128)(2,1)S(1)}, u32[]{:S(2)}) copy-start(bf16[64,2048]{1,0:T(8,128)(2,1)S(1)} %add_convert_fusion.e_ref) | copy-start | bytes 786436
  64.9 45.5 %copy-start.2 = (f32[4,2304]{1,0:T(4,128)S(1)}, f32[4,2304]{1,0:T(4,128)}, u32[]{:S(2)}) copy-start(f32[4,2304]{1,0:T(4,128)} %cw_ref.3) | copy-start | bytes 110596
  64.9 45.5 %copy-start.6 = (f32[2048]{0:T(1024)S(1)}, f32[2048]{0:T(1024)}, u32[]{:S(2)}) copy-start(f32[2048]{0:T(1024)} %param.22) | copy-start | bytes 24580
  64.9 45.5 %copy-start.7 = (f32[32]{0:T(128)S(1)}, f32[32]{0:T(128)}, u32[]{:S(2)}) copy-start(f32[32]{0:T(128)} %param.19) | copy-start | bytes 388
  139.2 2.0 copy-start.9
  145.5 14.2 %copy-start.10 = (bf16[1024,2048]{1,0:T(8,128)(2,1)S(1)}, bf16[1024,2048]{1,0:T(8,128)(2,1)}, u32[]{:S(2)}) copy-start(bf16[1024,2048]{1,0:T(8,128)(2,1)} %copy-done.9) | copy-start | bytes 12582916
  157.6 2.0 copy-start.12
  165.9 208.7 %reduce-scatter.3.cloned.1.call-start = ((), (), s32[]{:S(2)}) async-start(), calls=%async_computation.4 | async-start | bytes 9748480 | tf_op jit(solution)/shard_map/reduce_scatter | solution.py:504
  266.6 1.0 copy-start.13
  266.6 156.1 %all-reduce.11.cloned.1.call-start = ((), (), s32[]{:S(2)}) async-start(), calls=%async_computation.6 | async-start | bytes 1671168 | tf_op jit(solution)/shard_map/psum | solution.py:505
  267.6 107.0 %copy-start.17 = (f32[16,32]{1,0:T(8,128)S(1)}, f32[16,32]{1,0:T(8,128)}, u32[]{:S(2)}) copy-start(f32[16,32]{1,0:T(8,128)} %get-tuple-element.27) | copy-start | bytes 6148
  267.6 107.0 %copy-start.16 = (f32[8,2048]{1,0:T(8,128)S(1)}, f32[8,2048]{1,0:T(8,128)}, u32[]{:S(2)}) copy-start(f32[8,2048]{1,0:T(8,128)} %get-tuple-element.28) | copy-start | bytes 196612
  267.6 107.3 %copy-start.15 = (f32[8,2048]{1,0:T(8,128)S(1)}, f32[8,2048]{1,0:T(8,128)}, u32[]{:S(2)}) copy-start(f32[8,2048]{1,0:T(8,128)} %get-tuple-element.29) | copy-start | bytes 196612
  267.6 107.3 %copy-start.14 = (f32[8,2304]{1,0:T(8,128)S(1)}, f32[8,2304]{1,0:T(8,128)}, u32[]{:S(2)}) copy-start(f32[8,2304]{1,0:T(8,128)} %get-tuple-element.26) | copy-start | bytes 221188
Sparse Core Ops, SparseCore 0:
  10.3 83.9 all-gather.2
  96.5 48.9 all-gather.4
  166.1 71.2 reduce-scatter.4
  266.7 107.8 reduce-scatter.2
  376.9 35.7 all-reduce.10

commit v2 on v1

v2 whole, which is shorter than its diff:
```python
import functools

import jax
import jax.numpy as jnp
from jax import lax
from jax.experimental import pallas as pl
from jax.experimental.pallas import tpu as pltpu
from jax.sharding import PartitionSpec as P

CHUNK = 128
LANES = 128
EPS = 1e-05
F32 = jnp.float32
BF16 = jnp.bfloat16
NT = (((1,), (1,)), ((), ()))
TN = (((0,), (0,)), ((), ()))


def mm(a, b):
    return jnp.dot(a, b, preferred_element_type=F32)


def mm_nt(a, b):
    return lax.dot_general(a, b, NT, preferred_element_type=F32)


def mm_tn(a, b):
    return lax.dot_general(a, b, TN, preferred_element_type=F32)


def split2(v):
    high = v.astype(BF16)
    return high, (v - high.astype(F32)).astype(BF16)


def split3(v):
    high = v.astype(BF16)
    rest = v - high.astype(F32)
    mid = rest.astype(BF16)
    return high, mid, (rest - mid.astype(F32)).astype(BF16)


def tri_sum(tri, v):
    heads = v.shape[1]
    parts = mm(tri, jnp.concatenate(split3(v), axis=1))
    return parts[:, :heads] + parts[:, heads : 2 * heads] + parts[:, 2 * heads :]


def sigmoid(v):
    return 0.5 * jnp.tanh(0.5 * v) + 0.5


def softplus(v):
    return jnp.maximum(v, 0.0) + jnp.log1p(jnp.exp(-jnp.abs(v)))


def iota(shape, dim):
    return lax.broadcasted_iota(jnp.int32, shape, dim)


def small_terms(step_raw, step_bias, decay_rate, keep, to_end, rows):
    shifted = step_raw + step_bias
    step = softplus(shifted)
    lower = (iota((rows, rows), 0) >= iota((rows, rows), 1)).astype(BF16)
    cum = tri_sum(lower, step * decay_rate)
    last = cum[rows - 1 : rows, :]
    return shifted, step, cum, jnp.exp(cum) * keep, jnp.exp(last - cum) * to_end


def expand(e_ref, out_ref, step, from_prev, to_end):
    stacked = jnp.concatenate(
        [jnp.concatenate(split2(v), axis=1) for v in (step, from_prev, to_end)], axis=0
    )
    out_ref[...] = mm(stacked, e_ref[...])


def conv_tile(xbuf, cw_ref, cb_ref, marks, cols, rows):
    taps = cw_ref.shape[0]
    pre = cb_ref[:, cols] + cw_ref[0:1, cols] * xbuf[8 : 8 + rows, cols]
    for k in range(1, taps):
        pre = pre + (cw_ref[k : k + 1, cols] * xbuf[8 - k : 8 - k + rows, cols]) * marks[k]
    return pre


def forward_kernel(
    p_ref, prev_ref, aux_ref, seg_ref, cw_ref, cb_ref, bias_ref, rate_ref, skip_ref, gain_ref, e_ref,
    mixed_ref, y_ref, state_out_ref,
    xbuf, ex, state, xs, xdt, xe, bc, yin, gs,
    *, inner, conv_width, heads, width, per_seq,
):
    rows = p_ref.shape[0]
    n = (conv_width - inner) // 2
    tiles = inner // LANES
    conv_tiles = conv_width // LANES

    @pl.when(lax.rem(pl.program_id(0), per_seq) == 0)
    def _():
        state[...] = jnp.zeros_like(state)

    aux = aux_ref[...]
    keep, to_end_mask = aux[:, 7:8], aux[:, 8:9]
    shifted, step, cum, from_prev, to_end = small_terms(
        p_ref[:, inner + conv_width :], bias_ref[...], rate_ref[...], keep, to_end_mask, rows
    )
    expand(e_ref, ex, step, from_prev, to_end)
    cum_t = cum.T
    xbuf[0:8, :] = prev_ref[:, inner : inner + conv_width]
    xbuf[8 : 8 + rows, :] = p_ref[:, inner : inner + conv_width]
    marks = [None] + [jnp.broadcast_to(aux[:, k : k + 1], (rows, LANES)) for k in range(1, cw_ref.shape[0])]
    for c in range(conv_tiles):
        cols = slice(c * LANES, (c + 1) * LANES)
        pre = conv_tile(xbuf, cw_ref, cb_ref, marks, cols, rows)
        act = pre * sigmoid(pre)
        if c < tiles:
            xs[:, cols] = act
            scaled = act * ex[0:rows, cols]
            xdt[:, cols] = scaled.astype(BF16)
            xe[:, cols] = (scaled * ex[2 * rows : 3 * rows, cols]).astype(BF16)
        else:
            bc[:, (c - tiles) * LANES : (c - tiles + 1) * LANES] = act.astype(BF16)
    b, cc = bc[:, :n], bc[:, n:]
    causal = (iota((rows, rows), 0) >= iota((rows, rows), 1)) & (aux[:, 0:1] == seg_ref[0])
    scores = jnp.where(causal, mm_nt(cc, b), 0.0)
    state_low = state[...].astype(BF16)
    state_out_ref[...] = state_low
    yin[...] = mm(cc, state_low)
    state[...] = state[...] * ex[2 * rows - 1 : 2 * rows, :] + mm_tn(b, xe[...])
    lane = iota((1, LANES), 1)
    masks = [(lane < width).astype(BF16), (lane >= width).astype(BF16)]
    total = jnp.zeros((rows, LANES), F32)
    for c in range(tiles):
        cols = slice(c * LANES, (c + 1) * LANES)
        mixing = []
        for h in (2 * c, 2 * c + 1):
            spread = jnp.minimum(cum[:, h : h + 1] - cum_t[h : h + 1, :], 0.0)
            mixing.append((scores * jnp.exp(spread)).astype(BF16))
        x_low = xdt[:, cols]
        y = mm(
            jnp.concatenate(mixing, axis=1), jnp.concatenate([x_low * masks[0], x_low * masks[1]], axis=0)
        ) + ex[rows : 2 * rows, cols] * yin[:, cols]
        y = y + skip_ref[:, cols] * xs[:, cols]
        y_ref[:, cols] = y
        gate = p_ref[:, cols]
        gated = y * (gate * sigmoid(gate))
        gs[:, cols] = gated
        total = total + gated * gated
    inverse = lax.rsqrt(jnp.sum(total, axis=1, keepdims=True) / inner + EPS)
    for c in range(tiles):
        cols = slice(c * LANES, (c + 1) * LANES)
        mixed_ref[:, cols] = (gs[:, cols] * inverse * gain_ref[:, cols]).astype(BF16)


def helpers(segment, chunk):
    seqs, length = segment.shape
    blocks = length // chunk
    def same(shift):
        return (segment[:, shift:] == segment[:, :-shift]).astype(F32)
    back = [jnp.pad(same(k), ((0, 0), (k, 0))) for k in (1, 2, 3)]
    ahead = [jnp.pad(same(k), ((0, 0), (0, k))) for k in (1, 2, 3)]
    by_block = segment.reshape(seqs, blocks, chunk)
    ends = by_block[:, :, -1]
    before = jnp.pad(ends[:, :-1], ((0, 0), (1, 0)), constant_values=-1)
    keep = (by_block == before[:, :, None]).astype(F32).reshape(seqs, length)
    to_end = (by_block == ends[:, :, None]).astype(F32).reshape(seqs, length)
    docs = segment.astype(F32)
    columns = [docs, *back, *ahead, keep, to_end] + [jnp.zeros_like(docs)] * 7
    aux = jnp.stack(columns, axis=-1).reshape(seqs * length, 16)
    return aux, docs.reshape(seqs * blocks, 1, chunk)


def head_maps(heads, width):
    inner = heads * width
    owner = jnp.arange(inner) // width
    one = (jnp.arange(heads)[:, None] == owner[None, :]).astype(BF16)
    down = (owner[:, None] == jnp.arange(LANES)[None, :]).astype(BF16)
    return jnp.concatenate([one, one], axis=0), down


def full(shape):
    return pl.BlockSpec(shape, lambda i: (0,) * len(shape))


def scan_forward(p, aux, seg_rows, conv_w, conv_b, bias, rate, skip_row, gain_row, e, per_seq):
    tokens, proj = p.shape
    inner, conv_width, heads = gain_row.shape[1], conv_w.shape[1], bias.shape[1]
    n = (conv_width - inner) // 2
    r = CHUNK
    chunks = tokens // r
    return pl.pallas_call(
        functools.partial(
            forward_kernel, inner=inner, conv_width=conv_width, heads=heads, width=inner // heads, per_seq=per_seq
        ),
        grid=(chunks,),
        in_specs=[
            pl.BlockSpec((r, proj), lambda i: (i, 0)),
            pl.BlockSpec((8, proj), lambda i: (jnp.maximum(i * (r // 8) - 1, 0), 0)),
            pl.BlockSpec((r, 16), lambda i: (i, 0)),
            pl.BlockSpec((1, 1, r), lambda i: (i, 0, 0)),
            full(conv_w.shape), full(conv_b.shape), full(bias.shape), full(rate.shape),
            full(skip_row.shape), full(gain_row.shape), full(e.shape),
        ],
        out_specs=[
            pl.BlockSpec((r, inner), lambda i: (i, 0)),
            pl.BlockSpec((r, inner), lambda i: (i, 0)),
            pl.BlockSpec((n, inner), lambda i: (i, 0)),
        ],
        out_shape=[
            jax.ShapeDtypeStruct((tokens, inner), BF16),
            jax.ShapeDtypeStruct((tokens, inner), F32),
            jax.ShapeDtypeStruct((chunks * n, inner), BF16),
        ],
        scratch_shapes=[
            pltpu.VMEM((r + 8, conv_width), F32),
            pltpu.VMEM((3 * r, inner), F32),
            pltpu.VMEM((n, inner), F32),
            pltpu.VMEM((r, inner), F32),
            pltpu.VMEM((r, inner), BF16),
            pltpu.VMEM((r, inner), BF16),
            pltpu.VMEM((r, 2 * n), BF16),
            pltpu.VMEM((r, inner), F32),
            pltpu.VMEM((r, inner), F32),
        ],
        compiler_params=pltpu.CompilerParams(
            dimension_semantics=("arbitrary",), vmem_limit_bytes=48 * 2**20
        ),
        name="scan_forward",
    )(p, p, aux, seg_rows, conv_w, conv_b, bias, rate, skip_row, gain_row, e)


def gate_kernel(gate_ref, ssd_ref, gm_ref, gain_ref, dy_ref, dz_ref, dgain_ref):
    rows, inner = gate_ref.shape

    @pl.when(pl.program_id(0) == 0)
    def _():
        dgain_ref[...] = jnp.zeros_like(dgain_ref)

    squares = jnp.zeros((rows, LANES), F32)
    cross = jnp.zeros((rows, LANES), F32)
    for c in range(inner // LANES):
        cols = slice(c * LANES, (c + 1) * LANES)
        gate = gate_ref[:, cols]
        gated = ssd_ref[:, cols] * (gate * sigmoid(gate))
        squares = squares + gated * gated
        cross = cross + gm_ref[:, cols] * gain_ref[:, cols] * gated
    inverse = lax.rsqrt(jnp.sum(squares, axis=1, keepdims=True) / inner + EPS)
    mean_cross = jnp.sum(cross, axis=1, keepdims=True) / inner * inverse
    for c in range(inner // LANES):
        cols = slice(c * LANES, (c + 1) * LANES)
        gate = gate_ref[:, cols]
        sig = sigmoid(gate)
        silu = gate * sig
        ssd = ssd_ref[:, cols]
        unit = ssd * silu * inverse
        grad_mixed = gm_ref[:, cols]
        dgain_ref[:, cols] += jnp.sum((grad_mixed * unit).reshape(rows // 8, 8, LANES), axis=0)
        grad_gated = inverse * (grad_mixed * gain_ref[:, cols] - unit * mean_cross)
        dy_ref[:, cols] = (grad_gated * silu).astype(BF16)
        dz_ref[:, cols] = (grad_gated * ssd * (sig + silu * (1.0 - sig))).astype(BF16)


def gate_back(p, ssd, gm, gain_row):
    tokens, inner = ssd.shape
    r = CHUNK
    block = pl.BlockSpec((r, inner), lambda i: (i, 0))
    return pl.pallas_call(
        gate_kernel,
        grid=(tokens // r,),
        in_specs=[block, block, block, full(gain_row.shape)],
        out_specs=[block, block, full((8, inner))],
        out_shape=[
            jax.ShapeDtypeStruct((tokens, inner), BF16),
            jax.ShapeDtypeStruct((tokens, inner), BF16),
            jax.ShapeDtypeStruct((8, inner), F32),
        ],
        compiler_params=pltpu.CompilerParams(dimension_semantics=("arbitrary",), vmem_limit_bytes=32 * 2**20),
        name="gate_backward",
    )(p, ssd, gm, gain_row)


MESH = pl.DeviceIdType.MESH


class Spot:
    def __init__(self, levels):
        self.rep, self.at = lax.axis_index("rep"), lax.axis_index("fsdp")
        self.core, self.side, self.level = self.at % 2, (self.at // 2) % 2, self.at // 4
        self.levels = levels
        self.sibling = (self.rep, self.at + 1 - 2 * self.core)
        self.across = (self.rep, self.at + 2 - 4 * self.side)
        self.twin = (1 - self.rep, self.at)

    def far(self, step):
        return (self.rep, ((self.level + step) % self.levels) * 4 + self.at % 4)

    def greet(self):
        barrier = pltpu.get_barrier_semaphore()
        partners = [self.sibling, self.across, self.twin] + [self.far(d) for d in range(1, self.levels)]
        for one in partners:
            pl.semaphore_signal(barrier, inc=1, device_id=one, device_id_type=MESH)
        pl.semaphore_wait(barrier, len(partners))


def send(src, dst, send_sem, recv_sem, device):
    return pltpu.make_async_remote_copy(
        src_ref=src, dst_ref=dst, send_sem=send_sem, recv_sem=recv_sem, device_id=device, device_id_type=MESH
    )


class Unit:
    def __init__(self, spot, whole, own, from_core, from_side, from_level, mine, from_twin, sems, local, write):
        self.spot, self.whole, self.own, self.local, self.write = spot, whole, own, local, write
        self.from_core, self.from_side, self.from_level = from_core, from_side, from_level
        self.mine, self.from_twin = mine, from_twin
        self.sems = sems

    @property
    def c0(self):
        return pltpu.make_async_copy(self.whole.at[:, :, self.spot.core], self.own, self.sems.at[6])

    @property
    def c1(self):
        spot, sems = self.spot, self.sems
        return send(self.whole.at[:, :, 1 - spot.core], self.from_core, sems.at[0], sems.at[1], spot.sibling)

    @property
    def c2(self):
        spot, sems = self.spot, self.sems
        return send(self.own.at[:, 1 - spot.side], self.from_side, sems.at[2], sems.at[3], spot.across)

    @property
    def c3(self):
        spot, sems = self.spot, self.sems
        return [
            send(
                self.from_side.at[(spot.level + d) % spot.levels], self.from_level.at[d - 1],
                sems.at[5 + 2 * d], sems.at[6 + 2 * d], spot.far(d),
            )
            for d in range(1, spot.levels)
        ]

    @property
    def c4(self):
        spot, sems = self.spot, self.sems
        return send(self.mine, self.from_twin, sems.at[4], sems.at[5], spot.twin)

    def stage(self, number):
        spot, levels = self.spot, self.spot.levels
        if number == 1:
            self.c1.start()
            self.c0.start()
        elif number == 2:
            self.c0.wait()
            self.c1.wait()

            def add(i, carry):
                for side in range(2):
                    self.own[i, side] = (
                        self.own[i, side].astype(F32) + self.from_core[i, side].astype(F32)
                    ).astype(BF16)
                return carry

            lax.fori_loop(0, levels, add, 0)
            self.c2.start()
        elif number == 3:
            self.c2.wait()

            def add(i, carry):
                self.from_side[i] = (
                    self.from_side[i].astype(F32) + self.own[i, spot.side].astype(F32)
                ).astype(BF16)
                return carry

            lax.fori_loop(0, levels, add, 0)
            for copy in self.c3:
                copy.start()
        elif number == 4:
            for copy in self.c3:
                copy.wait()
            total = self.from_side[spot.level].astype(F32)
            for d in range(levels - 1):
                total = total + self.from_level[d].astype(F32)
            self.mine[...] = total.astype(BF16)
            self.c4.start()
        else:
            self.c4.wait()
            self.write(self.mine[...].astype(F32) + self.from_twin[...].astype(F32))


GROUPS = 4
BACKGROUND_STARTS = (0, 2, 5, 7, 11, 13, 18, 21)


def back_kernel(
    px_ref, prev_ref, ssd_ref, dy_ref, state_ref,
    tail_ref, aux_ref, seg_ref, cw_ref, cb_ref, bias_ref, rate_ref, skip_ref, e_ref, et_ref,
    ngain_ref, dgain_ref, square_ref,
    normed_t_hbm, wx_hbm, gn_hbm, tokens_hbm, gb_hbm, ggate_hbm, gout_hbm,
    gi_ref, go_ref, gt_ref, small_ref,
    xbuf, ex, adj, xs, xdt, xe, bc, slope, dye, dxi, dbuf, r1, r1l, r2, r3,
    tbuf, consts, stacks, raws, cums, scores, dscores, gbs, gcs, sums, tslope, gp, gpt, accum, taccum,
    normed_t, wx, gn, tokens, gb,
    own, part, part_t, own_t, from_core, from_core_t, from_side, from_side_t, from_level, from_level_t,
    mine, mine_t, twin, twin_t, sm, smr, smz, sems, small_sems, load_sems,
    *, inner, heads, width, levels, seq_chunks,
):
    group, turn = pl.program_id(0), pl.program_id(1)
    step = group * seq_chunks + turn
    chunk = seq_chunks - 1 - turn
    rows, cols_g = px_ref.shape
    n = bc.shape[2] // 2
    tiles = cols_g // LANES
    per_group = cols_g // width
    taps = cw_ref.shape[0]
    tail_cols = tail_ref.shape[1]
    conv_tail = 2 * n
    here = pl.ds(pl.multiple_of(chunk * rows, rows), rows)
    spot = Spot(levels)
    gcol = pl.multiple_of(group * cols_g, cols_g)
    rows_f = mine.shape[1]

    def loads():
        pairs = ((normed_t_hbm, normed_t), (wx_hbm, wx), (gn_hbm, gn), (tokens_hbm, tokens), (gb_hbm, gb))
        return [pltpu.make_async_copy(a, b, load_sems.at[i]) for i, (a, b) in enumerate(pairs)]

    units = []

    def writer(ref, row, col, wide):
        def write(v):
            ref[row : row + rows_f, col : col + wide] = v[:, :wide]
        return write

    for u in range(GROUPS * 2):
        if u < GROUPS:
            hbm = gout_hbm.at[:, :, :, pl.ds((u // 2) * rows_f, rows_f), pl.ds((u % 2) * cols_g, cols_g)]
            write = writer(go_ref, (u // 2) * rows_f, (u % 2) * cols_g, cols_g)
        else:
            hbm = ggate_hbm.at[:, :, :, :, pl.ds((u - GROUPS) * cols_g, cols_g)]
            write = writer(gi_ref, 0, (u - GROUPS) * cols_g, cols_g)
        units.append((u, hbm, own.at[u], write))
    for g in range(GROUPS):
        u = 2 * GROUPS + g
        units.append((u, part.at[g % 2], own.at[u], writer(gi_ref, 0, inner + g * cols_g, cols_g)))
    units = [
        Unit(
            spot, whole, mine_half, from_core.at[u], from_side.at[u], from_level.at[u], mine.at[u], twin.at[u],
            sems.at[u], True, write,
        )
        for u, whole, mine_half, write in units
    ]
    tail_wide = gi_ref.shape[1] - 2 * inner
    tail_unit = Unit(
        spot, part_t, own_t, from_core_t, from_side_t, from_level_t, mine_t, twin_t, sems.at[3 * GROUPS], True,
        writer(gi_ref, 0, 2 * inner, tail_wide),
    )

    events = {}
    last_step = GROUPS * seq_chunks - 1
    late = []
    plan = [(s * seq_chunks // 8, units[u]) for u, s in enumerate(BACKGROUND_STARTS)]
    plan += [((g + 1) * seq_chunks, units[2 * GROUPS + g]) for g in range(GROUPS - 1)]
    for begin, unit in plan:
        for number, delay in ((1, 0), (2, 1), (3, 4), (4, 7), (5, 8)):
            events.setdefault(min(begin + delay, last_step), []).append((unit, number))

    @pl.when(step == 0)
    def _():
        for copy in loads():
            copy.start()
        spot.greet()
        accum[...] = jnp.zeros_like(accum)
        taccum[...] = jnp.zeros_like(taccum)
        cums[...] = jnp.zeros_like(cums)

    for at, happen in sorted(events.items()):
        if at == last_step:
            late += happen
            continue

        @pl.when(step == at)
        def _(happen=happen):
            for unit, number in sorted(happen, key=lambda pair: -pair[1]):
                unit.stage(number)

    def fold(v):
        return jnp.sum(v.reshape(rows // 8, 8, v.shape[1]), axis=0)

    aux = aux_ref[here, :]
    marks = [None] + [jnp.broadcast_to(aux[:, k : k + 1], (rows, LANES)) for k in range(1, taps)]
    marks_next = [None] + [jnp.broadcast_to(aux[:, 3 + k : 4 + k], (rows, LANES)) for k in range(1, taps)]
    lower = iota((rows, rows), 0) >= iota((rows, rows), 1)
    upper = iota((rows, rows), 0) <= iota((rows, rows), 1)
    rate = rate_ref[...]

    def conv_pre(buffer, cols, wcols):
        pre = cb_ref[:, wcols] + cw_ref[0:1, wcols] * buffer[8 : 8 + rows, cols]
        for k in range(1, taps):
            pre = pre + (cw_ref[k : k + 1, wcols] * buffer[8 - k : 8 - k + rows, cols]) * marks[k]
        return pre

    def conv_back(buffer, cols, wcols, acc, acc_cols):
        grad = buffer[0:rows, cols]
        out = cw_ref[0:1, wcols] * grad
        acc[8 * taps : 8 * taps + 8, acc_cols] += fold(grad)
        acc[0:8, acc_cols] += fold(grad * xbuf[8 : 8 + rows, cols])
        for k in range(1, taps):
            out = out + (cw_ref[k : k + 1, wcols] * buffer[k : k + rows, cols]) * marks_next[k]
            acc[8 * k : 8 * k + 8, acc_cols] += fold(grad * (xbuf[8 - k : 8 - k + rows, cols] * marks[k]))
        return out

    def fill_tail():
        xbuf[8 : 8 + rows, 0:conv_tail] = tail_ref[here, 0:conv_tail]
        before = pl.ds(pl.multiple_of(jnp.maximum(chunk * rows - 8, 0), 8), 8)
        xbuf[0:8, 0:conv_tail] = tail_ref[before, 0:conv_tail]

    @pl.when(group == 0)
    def _():
        shifted, step_size, cum, from_prev, to_end = small_terms(
            tail_ref[here, conv_tail : conv_tail + heads], bias_ref[...], rate, aux[:, 7:8], aux[:, 8:9], rows
        )
        raws[here, 0:heads] = shifted
        raws[here, heads : 2 * heads] = step_size
        cums[chunk, :, 0:heads] = cum
        stacks[chunk] = jnp.concatenate(
            [jnp.concatenate(split2(v), axis=1) for v in (step_size, from_prev, to_end)], axis=0
        )
        fill_tail()
        for c in range(conv_tail // LANES):
            cols = slice(c * LANES, (c + 1) * LANES)
            pre = conv_pre(xbuf, cols, slice(inner + c * LANES, inner + (c + 1) * LANES))
            sig = sigmoid(pre)
            act = pre * sig
            tslope[here, cols] = sig + act * (1.0 - sig)
            bc[chunk, :, cols] = act.astype(BF16)
        same = upper & (aux[:, 0:1] == seg_ref[chunk])
        scores[chunk] = jnp.where(same, mm_nt(bc[chunk, :, 0:n], bc[chunk, :, n:]), 0.0)
        dscores[chunk] = jnp.zeros((rows, rows), F32)
        gbs[here, :] = jnp.zeros((rows, n), F32)
        gcs[here, :] = jnp.zeros((rows, n), F32)
        consts[chunk] = jnp.zeros((8, LANES), F32)
        for i in range(3):
            sums[i, here, :] = jnp.zeros((rows, LANES), F32)

    @pl.when(turn == 0)
    def _():
        adj[...] = jnp.zeros_like(adj)
        dbuf[rows : rows + 8, :] = jnp.zeros((8, cols_g), F32)

    ex[...] = mm(stacks[chunk], e_ref[:, pl.ds(gcol, cols_g)])
    head0 = group * per_group
    pick = (iota((LANES, LANES), 0) == iota((LANES, LANES), 1) + head0).astype(BF16)
    cum_all = cums[chunk]
    moved = [mm(v, pick) for v in split3(cum_all)]
    cum = moved[0] + moved[1] + moved[2]
    cum_t = cum.T
    xbuf[0:8, :] = prev_ref[...]
    xbuf[8 : 8 + rows, :] = px_ref[...]
    for c in range(tiles):
        cols = slice(c * LANES, (c + 1) * LANES)
        wcols = pl.ds(gcol + c * LANES, LANES)
        pre = conv_pre(xbuf, cols, wcols)
        sig = sigmoid(pre)
        act = pre * sig
        slope[:, cols] = sig + act * (1.0 - sig)
        xs[:, cols] = act
        scaled = act * ex[0:rows, cols]
        xdt[:, cols] = scaled.astype(BF16)
        xe[:, cols] = (scaled * ex[2 * rows : 3 * rows, cols]).astype(BF16)
        dye[:, cols] = (dy_ref[:, cols].astype(F32) * ex[rows : 2 * rows, cols]).astype(BF16)
    b, cc = bc[chunk, :, 0:n], bc[chunk, :, n:]
    state_low = state_ref[...]
    adj_low = adj[...].astype(BF16)
    carry = ex[2 * rows - 1 : 2 * rows, :]
    gcs[here, :] += mm_nt(dye[...], state_low)
    gbs[here, :] += mm_nt(xe[...], adj_low)
    dxi[...] = mm(b, adj_low)
    through = jnp.sum(adj[...] * state_low.astype(F32), axis=0, keepdims=True) * carry
    adj[...] = adj[...] * carry + mm_tn(cc, dye[...])
    scores_t = scores[chunk]
    lane = iota((1, LANES), 1)
    masks = [(lane < width).astype(BF16), (lane >= width).astype(BF16)]
    grad_scores_t = jnp.zeros((rows, rows), F32)
    for c in range(tiles):
        cols = slice(c * LANES, (c + 1) * LANES)
        acols = pl.ds(gcol + c * LANES, LANES)
        x_low, dy_low = xdt[:, cols], dy_ref[:, cols]
        grad_mix = mm_nt(jnp.concatenate([x_low * masks[0], x_low * masks[1]], axis=0), dy_low)
        mixing = []
        for i, h in enumerate((2 * c, 2 * c + 1)):
            decay = jnp.exp(jnp.minimum(cum_t[h : h + 1, :] - cum[:, h : h + 1], 0.0))
            mixing.append((scores_t * decay).astype(BF16))
            grad_scores_t = grad_scores_t + grad_mix[i * rows : (i + 1) * rows] * decay
        within = mm(
            jnp.concatenate(mixing, axis=1), jnp.concatenate([dy_low * masks[0], dy_low * masks[1]], axis=0)
        )
        x = xs[:, cols]
        skip = skip_ref[:, acols]
        across = ex[2 * rows : 3 * rows, cols] * dxi[:, cols]
        both = within + across
        grad_ssd = dy_low.astype(F32)
        x_scaled = x_low.astype(F32)
        r1[:, cols], r1l[:, cols] = split2(grad_ssd * (ssd_ref[:, cols] - skip * x) - within * x_scaled)
        r2[:, cols] = (across * x_scaled).astype(BF16)
        r3[:, cols] = (both * x).astype(BF16)
        accum[8 * taps + 8 : 8 * taps + 16, acols] += fold(grad_ssd * x)
        grad_x = skip * grad_ssd + ex[0:rows, cols] * both
        dbuf[0:rows, cols] = grad_x * slope[:, cols]
    dscores[chunk] += grad_scores_t
    et = et_ref[pl.ds(gcol, cols_g), :]
    sums[0, here, :] += mm(r1[...], et) + mm(r1l[...], et)
    sums[1, here, :] += mm(r2[...], et)
    sums[2, here, :] += mm(r3[...], et)
    high, rest = split2(jnp.broadcast_to(through, (8, cols_g)))
    consts[chunk] += mm(high, et) + mm(rest, et)
    for c in range(tiles):
        cols = slice(c * LANES, (c + 1) * LANES)
        acols = pl.ds(gcol + c * LANES, LANES)
        gp[here, cols] = conv_back(dbuf, cols, acols, accum, acols).astype(BF16)
    dbuf[rows : rows + 8, :] = dbuf[0:8, :]

    @pl.when(group == GROUPS - 1)
    def _():
        same = upper & (aux[:, 0:1] == seg_ref[chunk])
        grad_scores = jnp.where(same, dscores[chunk], 0.0).astype(BF16)
        grad_b = gbs[here, :] + mm(grad_scores, cc)
        grad_c = gcs[here, :] + mm_tn(grad_scores, b)
        fill_tail()

        @pl.when(turn == 0)
        def _():
            tbuf[rows : rows + 8, :] = jnp.zeros((8, 2 * n), F32)

        tbuf[0:rows, 0:n] = grad_b * tslope[here, 0:n]
        tbuf[0:rows, n : 2 * n] = grad_c * tslope[here, n : 2 * n]
        for c in range(conv_tail // LANES):
            cols = slice(c * LANES, (c + 1) * LANES)
            gpt[here, cols] = conv_back(
                tbuf, cols, slice(inner + c * LANES, inner + (c + 1) * LANES), taccum, cols
            ).astype(BF16)
        tbuf[rows : rows + 8, :] = tbuf[0:8, :]
        shifted = raws[here, 0:heads]
        step_size = raws[here, heads : 2 * heads]
        const = consts[chunk, 0:1, 0:heads]
        grad_log = (
            tri_sum(upper.astype(BF16), sums[0, here, 0:heads])
            + tri_sum((iota((rows, rows), 0) > iota((rows, rows), 1)).astype(BF16), sums[1, here, 0:heads])
            + const
        ) * aux[:, 1:2]
        grad_raw = (sums[2, here, 0:heads] + rate * grad_log) * sigmoid(shifted)
        gpt[here, conv_tail:] = jnp.concatenate(
            [grad_raw, jnp.zeros((rows, tail_cols - conv_tail - heads), F32)], axis=1
        ).astype(BF16)
        small = 8 * taps + 8
        taccum[small : small + 8, 0:heads] += fold(grad_raw)
        taccum[small : small + 8, LANES : LANES + heads] += fold(step_size * grad_log * rate)

    def weight_grad(low, out):
        def one(i, carry):
            block = pl.ds(pl.multiple_of(i * 4 * rows_f, 4 * rows_f), 4 * rows_f)
            v = mm(normed_t[block, :], low[...]).astype(BF16)
            for side in range(2):
                for core in range(2):
                    at = (2 * side + core) * rows_f
                    out[i, side, core] = v[at : at + rows_f]
            return carry

        lax.fori_loop(0, levels, one, 0)

    def input_grad(low, weights):
        def one(i, carry):
            block = pl.ds(pl.multiple_of(i * 256, 256), 256)
            gn[block, :] += mm_nt(low[block, :], weights[...])
            return carry

        lax.fori_loop(0, gn.shape[0] // 256, one, 0)

    for g in range(GROUPS - 1):

        @pl.when(step == (g + 1) * seq_chunks - 1)
        def _(g=g):
            if g == 0:
                for copy in loads():
                    copy.wait()
            weight_grad(gp, part.at[g % 2])
            input_grad(gp, wx.at[:, g * cols_g : (g + 1) * cols_g])

    @pl.when(step == last_step)
    def _():
        for unit, number in sorted(late, key=lambda pair: pair[1]):
            unit.stage(number)
        last = units[3 * GROUPS - 1]
        weight_grad(gpt, part_t)
        tail_unit.stage(1)
        weight_grad(gp, part.at[(GROUPS - 1) % 2])
        last.stage(1)
        input_grad(gpt, wx.at[:, inner : inner + tail_cols])
        tail_unit.stage(2)
        input_grad(gp, wx.at[:, (GROUPS - 1) * cols_g : GROUPS * cols_g])
        last.stage(2)
        d = gn.shape[1]
        ngain = ngain_ref[...]

        def block_norm(i, total):
            block = pl.ds(pl.multiple_of(i * 64, 64), 64)
            v = tokens[block, :].astype(F32)
            rinv = lax.rsqrt(jnp.sum(v * v, axis=1, keepdims=True) / d + EPS)
            scaled = v * rinv
            grad = gn[block, :]
            total = total + jnp.sum((grad * scaled).reshape(8, 8, d), axis=0)
            grad = grad * ngain
            mean = jnp.sum(grad * scaled, axis=1, keepdims=True) / d
            gb[block, :] = (gb[block, :].astype(F32) + rinv * (grad - scaled * mean)).astype(BF16)
            return total

        dnorm = lax.fori_loop(0, gn.shape[0] // 64, block_norm, jnp.zeros((8, d), F32))
        leave = pltpu.make_async_copy(gb, gt_ref, load_sems.at[5])
        leave.start()

        def one_row(v):
            return jnp.sum(v, axis=0, keepdims=True)

        local = sm.at[0]
        local[...] = jnp.zeros(local.shape, F32)
        for k in range(taps + 1):
            local[k : k + 1, 0:inner] = one_row(accum[8 * k : 8 * k + 8, :])
            local[k : k + 1, inner : inner + conv_tail] = one_row(taccum[8 * k : 8 * k + 8, 0:conv_tail])
        local[5:6, 0:inner] = one_row(dgain_ref[...])
        local[6:7, 0:inner] = one_row(accum[8 * taps + 8 : 8 * taps + 16, :])
        local[7:8, 0:d] = one_row(dnorm)
        small = 8 * taps + 8
        local[7:8, d : d + conv_tail] = one_row(taccum[small : small + 8, 0:conv_tail])
        local[7:8, d + conv_tail : d + conv_tail + LANES] = one_row(square_ref[...])
        exchange = [
            send(sm.at[i], smr.at[i], small_sems.at[2 * i], small_sems.at[2 * i + 1], device)
            for i, device in enumerate((spot.sibling, spot.across, spot.twin))
        ]
        spread = [
            send(sm.at[3], smz.at[spot.level], small_sems.at[4 + 2 * d], small_sems.at[5 + 2 * d], spot.far(d))
            for d in range(1, levels)
        ]

        def fold_small(i):
            exchange[i].wait()
            sm[i + 1] = sm[i] + smr[i]

        exchange[0].start()
        tail_unit.stage(3)
        fold_small(0)
        exchange[1].start()
        last.stage(3)
        fold_small(1)
        exchange[2].start()
        tail_unit.stage(4)
        fold_small(2)
        for copy in spread:
            copy.start()
        smz[spot.level] = sm[3]
        last.stage(4)
        tail_unit.stage(5)
        for copy in spread:
            copy.wait()
        total = smz[0]
        for i in range(1, levels):
            total = total + smz[i]
        small_ref[...] = total
        last.stage(5)
        leave.wait()


def back(
    px, px_block, tail, ssd, dy, states, aux, seg_rows, conv_w, conv_b, bias, rate, skip_row, e, et,
    norm_gain, dgain, squares, normed_t, wx, gn, tokens, gb, ggate, gout, proj,
):
    length, inner = ssd.shape
    heads = bias.shape[1]
    levels, rows_f = ggate.shape[0], ggate.shape[3]
    taps = conv_w.shape[0]
    n = (conv_w.shape[1] - inner) // 2
    r = CHUNK
    chunks = length // r
    wide = inner // GROUPS
    tcols = tail.shape[1]
    d = normed_t.shape[0]
    small_cols = inner + tcols
    units = 3 * GROUPS
    back_at = lambda off: lambda g, c: (chunks - 1 - c, g + off)
    whole = lambda a: pl.BlockSpec(a.shape, lambda g, c: (0,) * a.ndim, pipeline_mode=pl.Buffered(1))
    anywhere = pl.BlockSpec(memory_space=pl.ANY)
    vm = pltpu.VMEM
    out = lambda s: pl.BlockSpec(s, lambda g, c: (0,) * len(s))
    return pl.pallas_call(
        functools.partial(
            back_kernel, inner=inner, heads=heads, width=inner // heads, levels=levels, seq_chunks=chunks
        ),
        grid=(GROUPS, chunks),
        in_specs=[
            pl.BlockSpec((r, wide), back_at(px_block)),
            pl.BlockSpec((8, wide), lambda g, c: (jnp.maximum((chunks - 1 - c) * (r // 8) - 1, 0), g + px_block)),
            pl.BlockSpec((r, wide), back_at(0)),
            pl.BlockSpec((r, wide), back_at(0)),
            pl.BlockSpec((n, wide), back_at(0)),
            *[whole(a) for a in (tail, aux, seg_rows, conv_w, conv_b, bias, rate, skip_row, e, et, norm_gain, dgain, squares)],
            *[anywhere] * 7,
        ],
        out_specs=[out((rows_f, proj)), out((2 * rows_f, d)), anywhere, out((8, small_cols))],
        out_shape=[
            jax.ShapeDtypeStruct((rows_f, proj), F32),
            jax.ShapeDtypeStruct((2 * rows_f, d), F32),
            jax.ShapeDtypeStruct((length, d), BF16),
            jax.ShapeDtypeStruct((8, small_cols), F32),
        ],
        scratch_shapes=[
            vm((r + 8, wide), F32), vm((3 * r, wide), F32), vm((n, wide), F32), vm((r, wide), F32),
            vm((r, wide), BF16), vm((r, wide), BF16), vm((chunks, r, 2 * n), BF16), vm((r, wide), F32),
            vm((r, wide), BF16), vm((r, wide), F32), vm((r + 8, wide), F32),
            vm((r, wide), BF16), vm((r, wide), BF16), vm((r, wide), BF16), vm((r, wide), BF16),
            vm((r + 8, 2 * n), F32), vm((chunks, 8, LANES), F32),
            vm((chunks, 3 * r, 2 * heads), BF16), vm((length, LANES), F32), vm((chunks, r, LANES), F32),
            vm((chunks, r, r), F32), vm((chunks, r, r), F32), vm((length, n), F32), vm((length, n), F32),
            vm((3, length, LANES), F32), vm((length, 2 * n), F32), vm((length, wide), BF16), vm((length, tcols), BF16),
            vm((8 * taps + 16, inner), F32), vm((8 * taps + 16, 2 * n), F32),
            vm(normed_t.shape, BF16), vm(wx.shape, BF16), vm(gn.shape, F32), vm(tokens.shape, BF16), vm(gb.shape, BF16),
            vm((units, levels, 2, rows_f, wide), BF16), vm((2, levels, 2, 2, rows_f, wide), BF16),
            vm((levels, 2, 2, rows_f, tcols), BF16), vm((levels, 2, rows_f, tcols), BF16),
            vm((units, levels, 2, rows_f, wide), BF16), vm((levels, 2, rows_f, tcols), BF16),
            vm((units, levels, rows_f, wide), BF16), vm((levels, rows_f, tcols), BF16),
            vm((units, levels - 1, rows_f, wide), BF16), vm((levels - 1, rows_f, tcols), BF16),
            vm((units, rows_f, wide), BF16), vm((rows_f, tcols), BF16),
            vm((units, rows_f, wide), BF16), vm((rows_f, tcols), BF16),
            vm((4, 8, small_cols), F32), vm((3, 8, small_cols), F32), vm((levels, 8, small_cols), F32),
            pltpu.SemaphoreType.DMA((units + 1, 5 + 2 * levels)),
            pltpu.SemaphoreType.DMA((4 + 2 * levels,)),
            pltpu.SemaphoreType.DMA((6,)),
        ],
        compiler_params=pltpu.CompilerParams(
            dimension_semantics=("arbitrary", "arbitrary"), vmem_limit_bytes=60 * 2**20,
            collective_id=1, has_side_effects=True,
        ),
        name="scan_backward",
    )(
        px, px, ssd, dy, states, tail, aux, seg_rows, conv_w, conv_b, bias, rate, skip_row, e, et,
        norm_gain, dgain, squares, normed_t, wx, gn, tokens, gb, ggate, gout,
    )


def rms_scale(values):
    return lax.rsqrt(jnp.mean(values * values, axis=1, keepdims=True) + EPS)


def on_device(
    tokens,
    norm_gain,
    in_weight,
    conv_weight,
    conv_bias,
    step_bias,
    decay_log,
    skip_gain,
    out_gain,
    out_weight,
    cotangent,
    teacher,
    segment,
    valid_mask,
):
    seqs, length, width = tokens.shape
    rows = seqs * length
    every = ("rep", "fsdp")
    shards = lax.axis_size("fsdp")
    devices = lax.axis_size("rep") * shards
    loss_weight = float(rows * devices * width // 8)
    valid = valid_mask.reshape(rows, 1).astype(F32)
    total_count = lax.psum(jnp.sum(valid), every)
    denominator = total_count * width

    flat = tokens.reshape(rows, width)
    inputs = flat.astype(F32)
    normed = (inputs * rms_scale(inputs) * norm_gain[None, :]).astype(BF16)
    w_in = lax.all_gather(in_weight, "fsdp", axis=0, tiled=True)
    w_out = lax.all_gather(out_weight, "fsdp", axis=0, tiled=True)
    projected = mm(normed, w_in)

    heads = step_bias.shape[0]
    inner = out_gain.shape[0]
    head_width = inner // heads
    aux, seg_rows = helpers(segment, CHUNK)
    e, et = head_maps(heads, head_width)
    rate = -jnp.exp(decay_log)[None, :]
    skip_row = jnp.repeat(skip_gain, head_width)[None, :]
    per_seq = length // CHUNK
    params = (conv_weight, conv_bias[None, :], step_bias[None, :], rate, skip_row)
    gain_row = out_gain[None, :]
    mixed, ssd, states = scan_forward(projected, aux, seg_rows, *params, gain_row, e, per_seq)

    result = inputs + mm(mixed, w_out)
    error = result - teacher.reshape(rows, width).astype(F32)
    squares = jnp.sum((valid * error * error).reshape(rows, width // LANES, LANES), axis=(0, 1))
    cotan = cotangent.reshape(rows, width).astype(F32)
    grad_result = valid * (cotan + 2.0 * loss_weight * error / denominator)
    grad_branch = grad_result.astype(BF16)
    grad_out = mm_tn(mixed, grad_branch).astype(BF16)
    grad_mixed = mm_nt(grad_branch, w_out)
    dy, dz, dgain = gate_back(projected, ssd, grad_mixed, gain_row)
    grad_gate = mm_tn(normed, dz).astype(BF16)
    gn = mm_nt(dz, w_in[:, :inner])
    levels = shards // 4
    tail_at = 2 * inner
    tail_pad = -(in_weight.shape[1] - tail_at) % LANES
    tail = jnp.pad(projected[:, tail_at:], ((0, 0), (0, tail_pad)))
    wx = jnp.pad(w_in[:, inner:], ((0, 0), (0, tail_pad)))
    squares8 = jnp.pad(squares[None, :], ((0, 7), (0, 0)))
    grad_in, grad_out, grad_tokens, small = back(
        projected, inner // (inner // GROUPS), tail, ssd, dy, states, aux, seg_rows, *params, e, et,
        norm_gain[None, :], dgain, squares8, normed.T, wx, gn, flat, grad_branch,
        grad_gate.reshape(levels, 2, 2, width // shards, inner),
        grad_out.reshape(levels, 2, 2, inner // shards, width), in_weight.shape[1],
    )
    taps, conv_width = conv_weight.shape
    extra = small[7, width:]
    loss = jnp.sum(extra[2 * LANES : 3 * LANES]) / denominator
    return (
        result.astype(BF16).reshape(tokens.shape),
        loss,
        grad_tokens.reshape(tokens.shape),
        small[7, :width],
        grad_in,
        small[:taps, :conv_width],
        small[taps, :conv_width],
        extra[:heads],
        extra[LANES : LANES + heads],
        small[6, :inner].reshape(heads, head_width).sum(axis=1),
        small[5, :inner],
        grad_out,
    )


def solution(mesh):
    tokens = P(("rep", "fsdp"), None, None)
    marks = P(("rep", "fsdp"), None)
    shard = P("fsdp", None)
    return jax.shard_map(
        on_device,
        mesh=mesh,
        in_specs=(tokens, P(), shard, P(), P(), P(), P(), P(), P(), shard, tokens, tokens, marks, marks),
        out_specs=(tokens, P(), tokens, P(), shard, P(), P(), P(), P(), P(), P(), shard),
        check_vma=False,
    )
```

time: 442 us -> 372 us (0.84); the launches traced: 435 us -> 371 us
  waiting for transfers between devices: 124 us -> 24.7 us
  Pallas kernels: 101 us -> 188 us
  blocking collectives: 85.6 us -> 43.7 us
  matrix products: 79.8 us -> 50.3 us
  local copies, waits for them, and re-layouts: 8.02 us -> 34.4 us
  other arithmetic: 19.1 us -> 13.7 us
    reduce_scatter x2 -> x0, waiting for transfers between devices: 89.2 us -> none  [reduce(): shard = lax.psum_scatter(grad, 'fsdp', scatter_dimension=0, tiled=True)]
    pallas_call x1 -> x2, Pallas kernels: 71.9 us -> 159 us  [the longest x1 145 us: back(): pl.pallas_call(functools.partial(back_kernel, inner=inner, heads=heads, w...]
    psum x1 -> x0, blocking collectives: 41.9 us -> none  [on_device(): summed = lax.psum(small, every)]
    dot_general x2, matrix products: 29.3 us -> 13.1 us  [mm_nt(): return lax.dot_general(a, b, NT, preferred_element_type=F32)]
    slice x0 -> x9, local copies, waits for them, and re-layouts: none -> 9.63 us  [the longest x2 2.41 us: on_device(): wx = jnp.pad(w_in[:, inner:], ((0, 0), (0, tail_pad)))]
    dot_general x2, matrix products: 22.4 us -> 12.7 us  [mm_tn(): return lax.dot_general(a, b, TN, preferred_element_type=F32)]
    unnamed x39 -> x56, local copies, waits for them, and re-layouts: 4.99 us -> 13.4 us
    all_gather x1, waiting for transfers between devices: 29.4 us -> 22.3 us  [on_device(): w_in = lax.all_gather(in_weight, 'fsdp', axis=0, tiled=True)]
  transfers between devices with their start and end apart: 5 -> 2, of which waited for: 3 -> 2; matrix products, arithmetic and copies ran while one was open for 18% -> 8% of each run, Pallas kernels for 23% -> 8%
where the time goes in v2:
time: 372 us; the launch traced here: 371 us
  Pallas kernels  188 us (51%)
  matrix products  50.3 us (14%)
  blocking collectives  43.7 us (12%)
  local copies, waits for them, and re-layouts  34.4 us (9%)
  waiting for transfers between devices  24.7 us (7%)
  between operations  16.8 us (5%)
  other arithmetic  13.7 us (4%)
    pallas_call x1, Pallas kernels, back(): pl.pallas_call(functools.partial(back_kernel, inner=inner, heads=heads, w...  145 us
    psum x1, blocking collectives, on_device(): total_count = lax.psum(jnp.sum(valid), every)  43.7 us
    pallas_call x1, Pallas kernels, scan_forward(): pl.pallas_call(functools.partial(forward_kernel, inner=inner, conv_width=...  28.8 us
    dot_general x2, matrix products, mm(): return jnp.dot(a, b, preferred_element_type=F32)  24.5 us
    all_gather x1, waiting for transfers between devices, on_device(): w_in = lax.all_gather(in_weight, 'fsdp', axis=0, tiled=True)  22.3 us
    unnamed x56, local copies, waits for them, and re-layouts  13.4 us
    pallas_call x1, Pallas kernels, gate_back(): pl.pallas_call(gate_kernel, grid=(tokens // r,), in_specs=[block, block,...  13.4 us
    dot_general x2, matrix products, mm_nt(): return lax.dot_general(a, b, NT, preferred_element_type=F32)  13.1 us
  transfers between devices with their start and end apart: 2, of which 2 were waited for; matrix products, arithmetic and copies ran while one was open for 8% of the time, Pallas kernels for 8%

profile of v2, /device:TPU:0, one launch (start us, length us, event | category | flops | bytes accessed | tf_op | source)
XLA Modules:
  0.0 371.3 jit_solution(2076215102978132045)
XLA Ops:
  8.7 1.3 convert_reduce_fusion
  10.0 43.7 %psum.7 = f32[]{:T(128)} all-reduce(f32[]{:T(128)} %convert_reduce_fusion), channel_id=1, replica_groups=mesh['rep'=2,'fsdp'=16] {'rep','fsdp'}, use_global_device_ids=true, to_apply=%region_2.0 | all-reduce | flops 1 | bytes 8 | tf_op jit(solution)/shard_map/psum | solution.py:872
  56.2 0.8 compare_convert_fusion.2
  57.1 0.8 compare_convert_fusion.3
  61.4 2.1 fusion
  63.6 2.6 fusion.13
  66.2 3.9 %copy.70.normed_t_hbm = bf16[1024,1024]{1,0:T(8,128)(2,1)} copy(bf16[1024,1024]{0,1:T(8,128)(2,1)} %fusion.13) | data formatting | bytes 4194304 | tf_op jit(solution)/shard_map/transpose | solution.py:913
  70.9 1.1 fusion.8.et_ref
  72.0 22.3 %all-gather.3.cloned.1.call-done = bf16[1024,4384]{1,0:T(8,128)(2,1)} async-done(((bf16[64,4384]{1,0:T(8,128)(2,1)}), bf16[1024,4384]{1,0:T(8,128)(2,1)}) %all-gather.3.cloned.1.call-update) | async-done | bytes 8978448 | tf_op jit(solution)/shard_map/all_gather | solution.py:878
  94.4 12.8 %fusion.14.p_ref.prev_ref.gate_ref.px_ref = f32[1024,4384]{1,0:T(8,128)S(1)} fusion(bf16[1024,4384]{1,0:T(8,128)(2,1)} %all-gather.3.cloned.1.call-done, f32[1024]{0:T(1024)S(1)} %copy-done.18, f32[1024]{0:T(1024)S(1)} %add_rsqrt_fusion, bf16[1,1024,1024]{2,1,0:T(8,128)(2,1)S(1)} %copy-done.14), kind=kOutput, calls=%fused_computation.52 | convolution fusion | flops 9198108672 | bytes 29040640 | tf_op jit(solution)/shard_map/dot_general | solution.py:20
  107.1 6.3 %copy-done.13 = f32[1024,4384]{1,0:T(8,128)} copy-done((f32[1024,4384]{1,0:T(8,128)}, f32[1024,4384]{1,0:T(8,128)S(1)}, u32[]{:S(2)}) %copy-start.13) | copy-done | bytes 17956888
  113.5 28.8 %scan_forward.1 = (bf16[1024,2048]{1,0:T(8,128)(2,1)S(1)}, f32[1024,2048]{1,0:T(8,128)}, bf16[1024,2048]{1,0:T(8,128)(2,1)}) custom-call(f32[1024,4384]{1,0:T(8,128)} %copy-done.13, f32[1024,4384]{1,0:T(8,128)} %copy-done.13, f32[1024,16]{1,0:T(8,128)S(1)} %bitcast.78, f32[8,1,128]{2,1,0:T(1,128)S(1)} %get-tuple-element.39.seg_ref, f32[4,2304]{1,0:T(4,128)S(1)} %copy-done.3, ...), custom_call_target="tpu_custom_call" | custom-call | tf_op jit(solution)/shard_map/scan_forward/pallas_call | solution.py:189
  142.3 2.1 copy-done.11
  144.3 1.0 all-gather.5.cloned.1.call-done
  145.3 11.7 %fusion.3 = (f32[1024]{0:T(1024)S(1)}, bf16[1024,1024]{1,0:T(8,128)(2,1)S(1)}, bf16[1,1024,1024]{2,1,0:T(8,128)(2,1)}) fusion(bf16[1,1024,1024]{2,1,0:T(8,128)(2,1)} %param.25, f32[1024]{0:T(1024)S(1)} %bitcast.95, f32[]{:T(128)S(6)} %mul.53, bf16[1,1024,1024]{2,1,0:T(8,128)(2,1)} %param.24, bf16[1024,2048]{1,0:T(8,128)(2,1)} %copy-done.11, ...), kind=kOutput, calls=%fused_computation.7 | convolution fusion | flops 4309646336 | bytes 18882564 | tf_op jit(solution)/shard_map/dot_general | solution.py:20
  157.1 6.3 %convolution_convert_fusion = bf16[2048,1024]{1,0:T(8,128)(2,1)} fusion(bf16[1024,2048]{1,0:T(8,128)(2,1)S(1)} %copy-done.12, bf16[1024,1024]{1,0:T(8,128)(2,1)S(1)} %get-tuple-element.33.gb_hbm), kind=kOutput, calls=%fused_computation.14 | convolution fusion | flops 4297064448 | bytes 10485760 | tf_op jit(solution)/shard_map/dot_general | solution.py:28
  163.4 7.0 %fusion.17.gm_ref = f32[1024,2048]{1,0:T(8,128)} fusion(bf16[1024,1024]{1,0:T(8,128)(2,1)S(1)} %get-tuple-element.33.gb_hbm, bf16[2048,1024]{1,0:T(8,128)(2,1)S(1)} %copy-done.19), kind=kOutput, calls=%fused_computation.54 | convolution fusion | flops 4294967296 | bytes 14680064 | tf_op jit(solution)/shard_map/dot_general | solution.py:24
  170.4 13.4 %gate_backward.1 = (bf16[1024,2048]{1,0:T(8,128)(2,1)S(1)}, bf16[1024,2048]{1,0:T(8,128)(2,1)S(1)}, f32[8,2048]{1,0:T(8,128)S(1)}) custom-call(f32[1024,4384]{1,0:T(8,128)} %copy-done.13, f32[1024,2048]{1,0:T(8,128)S(1)} %bitcast.77, f32[1024,2048]{1,0:T(8,128)} %fusion.17.gm_ref, f32[1,2048]{1,0:T(1,128)S(1)} %bitcast.81), custom_call_target="tpu_custom_call" | custom-call | tf_op jit(solution)/shard_map/gate_backward/pallas_call | solution.py:265
  183.8 6.4 %convolution_convert_fusion.1 = bf16[1024,2048]{1,0:T(8,128)(2,1)} fusion(bf16[1024,2048]{1,0:T(8,128)(2,1)S(1)} %get-tuple-element.27, f32[1024]{0:T(1024)S(1)} %copy-done.18, f32[1024]{0:T(1024)S(1)} %add_rsqrt_fusion, bf16[1,1024,1024]{2,1,0:T(8,128)(2,1)S(1)} %copy-done.14), kind=kOutput, calls=%fused_computation.15 | convolution fusion | flops 4301258752 | bytes 10493952 | tf_op jit(solution)/shard_map/dot_general | solution.py:28
  190.8 1.2 pad.50.tail_ref
  192.1 2.4 slice-done.6
  194.5 2.5 pad.52.wx_hbm
  197.0 6.1 %fusion.4.gn_hbm = f32[1024,1024]{1,0:T(8,128)} fusion(bf16[1024,2048]{1,0:T(8,128)(2,1)S(1)} %get-tuple-element.27, bf16[1024,4384]{1,0:T(8,128)(2,1)S(1)} %bitcast.85), kind=kOutput, calls=%fused_computation.8 | convolution fusion | flops 4294967296 | bytes 12582912 | tf_op jit(solution)/shard_map/dot_general | solution.py:24
  203.1 145.4 %scan_backward.1 = (f32[64,4384]{1,0:T(8,128)}, f32[128,1024]{1,0:T(8,128)}, bf16[1024,1024]{1,0:T(8,128)(2,1)}, f32[8,2432]{1,0:T(8,128)}) custom-call(f32[1024,4384]{1,0:T(8,128)} %copy-done.13, f32[1024,4384]{1,0:T(8,128)} %copy-done.13, f32[1024,2048]{1,0:T(8,128)} %get-tuple-element.23.ssd_ref, bf16[1024,2048]{1,0:T(8,128)(2,1)} %copy-done.1, ...), custom_call_target="tpu_custom_call" | custom-call | tf_op jit(solution)/shard_map/scan_backward/pallas_call | solution.py:790
  348.6 1.6 slice.90
  350.2 1.5 fusion.16
  351.7 1.5 slice_reduce_fusion
  353.2 1.4 slice.89
  354.6 1.2 slice_bitcast_fusion
  355.8 1.3 slice_reduce_fusion.2
  358.4 3.1 copy.76
  361.5 1.0 copy.77
  (88 shorter events, 9.8 us)
Async XLA Ops:
  7.2 56.4 %copy-start.14 = (bf16[1,1024,1024]{2,1,0:T(8,128)(2,1)S(1)}, bf16[1,1024,1024]{2,1,0:T(8,128)(2,1)}, u32[]{:S(2)}) copy-start(bf16[1,1024,1024]{2,1,0:T(8,128)(2,1)} %param.14) | copy-start | bytes 6291460
  7.2 87.2 %all-gather.3.cloned.1.call-start = ((), (), s32[]{:S(2)}) async-start(), calls=%async_computation | async-start | bytes 9748480 | tf_op jit(solution)/shard_map/all_gather | solution.py:878
  7.9 137.4 %all-gather.5.cloned.1.call-start = ((), (), s32[]{:S(2)}) async-start(), calls=%async_computation.1 | async-start | bytes 4456448 | tf_op jit(solution)/shard_map/all_gather | solution.py:879
  58.7 54.7 %copy-start.7 = (f32[8,1,128]{2,1,0:T(1,128)}, f32[8,1,128]{2,1,0:T(1,128)S(1)}, u32[]{:S(2)}) copy-start(f32[8,1,128]{2,1,0:T(1,128)S(1)} %get-tuple-element.39.seg_ref) | copy-start | bytes 12292
  59.9 53.5 %copy-start = (f32[1,1024,16]{2,1,0:T(8,128)}, f32[1,1024,16]{2,1,0:T(8,128)S(1)}, u32[]{:S(2)}) copy-start(f32[1,1024,16]{2,1,0:T(8,128)S(1)} %copy.63) | copy-start | bytes 196612
  60.7 52.7 %copy-start.5 = (f32[1,2048]{1,0:T(1,128)}, f32[1,2048]{1,0:T(1,128)S(1)}, u32[]{:S(2)}) copy-start(f32[1,2048]{1,0:T(1,128)S(1)} %broadcast_in_dim_reshape.3.skip_ref) | copy-start | bytes 24580
  61.4 52.0 %copy-start.4 = (f32[1,2304]{1,0:T(1,128)}, f32[1,2304]{1,0:T(1,128)S(1)}, u32[]{:S(2)}) copy-start(f32[1,2304]{1,0:T(1,128)S(1)} %broadcast_in_dim.12.cb_ref) | copy-start | bytes 27652
  63.5 7.2 %copy-start.20 = (f32[32]{0:T(128)S(1)}, f32[32]{0:T(128)}, u32[]{:S(2)}) copy-start(f32[32]{0:T(128)} %param.20) | copy-start | bytes 388
  63.6 30.8 %copy-start.18 = (f32[1024]{0:T(1024)S(1)}, f32[1024]{0:T(1024)}, u32[]{:S(2)}) copy-start(f32[1024]{0:T(1024)} %param.15) | copy-start | bytes 12292
  70.8 42.6 %copy-start.10 = (f32[1,32]{1,0:T(1,128)}, f32[1,32]{1,0:T(1,128)S(1)}, u32[]{:S(2)}) copy-start(f32[1,32]{1,0:T(1,128)S(1)} %negate_bitcast_fusion.rate_ref) | copy-start | bytes 388
  70.9 42.6 %copy-start.2 = (bf16[64,2048]{1,0:T(8,128)(2,1)}, bf16[64,2048]{1,0:T(8,128)(2,1)S(1)}, u32[]{:S(2)}) copy-start(bf16[64,2048]{1,0:T(8,128)(2,1)S(1)} %add_convert_fusion.e_ref) | copy-start | bytes 786436
  72.0 41.4 %copy-start.3 = (f32[4,2304]{1,0:T(4,128)S(1)}, f32[4,2304]{1,0:T(4,128)}, u32[]{:S(2)}) copy-start(f32[4,2304]{1,0:T(4,128)} %cw_ref.3) | copy-start | bytes 110596
  72.0 41.4 %copy-start.8 = (f32[2048]{0:T(1024)S(1)}, f32[2048]{0:T(1024)}, u32[]{:S(2)}) copy-start(f32[2048]{0:T(1024)} %param.22) | copy-start | bytes 24580
  72.0 41.4 %copy-start.9 = (f32[32]{0:T(128)S(1)}, f32[32]{0:T(128)}, u32[]{:S(2)}) copy-start(f32[32]{0:T(128)} %param.19) | copy-start | bytes 388
  107.1 6.3 %copy-start.13 = (f32[1024,4384]{1,0:T(8,128)}, f32[1024,4384]{1,0:T(8,128)S(1)}, u32[]{:S(2)}) copy-start(f32[1024,4384]{1,0:T(8,128)S(1)} %fusion.14.p_ref.prev_ref.gate_ref.px_ref) | copy-start | bytes 53870596
  142.3 2.1 copy-start.11
  145.3 11.8 %copy-start.12 = (bf16[1024,2048]{1,0:T(8,128)(2,1)S(1)}, bf16[1024,2048]{1,0:T(8,128)(2,1)}, u32[]{:S(2)}) copy-start(bf16[1024,2048]{1,0:T(8,128)(2,1)} %copy-done.11) | copy-start | bytes 12582916
  157.1 6.3 %copy-start.15 = (bf16[1024,1024]{1,0:T(8,128)(2,1)}, bf16[1024,1024]{1,0:T(8,128)(2,1)S(1)}, u32[]{:S(2)}) copy-start(bf16[1024,1024]{1,0:T(8,128)(2,1)S(1)} %get-tuple-element.33.gb_hbm) | copy-start | bytes 6291460
  157.1 6.3 %copy-start.19 = (bf16[2048,1024]{1,0:T(8,128)(2,1)S(1)}, bf16[2048,1024]{1,0:T(8,128)(2,1)}, u32[]{:S(2)}) copy-start(bf16[2048,1024]{1,0:T(8,128)(2,1)} %all-gather.5.cloned.1.call-done) | copy-start | bytes 12582916
  157.1 13.3 %slice-start = ((s8[8388608]{0:T(1024)(128)(4,1)}), s8[4194304]{0:T(1024)(128)(4,1)S(1)}, s32[]{:S(2)}) async-start(s8[8388608]{0:T(1024)(128)(4,1)} %bitcast.76), calls=%async_computation.2 | async-start | bytes 8388608
  163.4 7.0 %slice-start.1 = ((s8[8388608]{0:T(1024)(128)(4,1)}), s8[4194304]{0:T(1024)(128)(4,1)S(1)}, s32[]{:S(2)}) async-start(s8[8388608]{0:T(1024)(128)(4,1)} %bitcast.76), calls=%async_computation.3 | async-start | bytes 8388608
  183.7 6.5 %copy-start.1 = (bf16[1024,2048]{1,0:T(8,128)(2,1)}, bf16[1024,2048]{1,0:T(8,128)(2,1)S(1)}, u32[]{:S(2)}) copy-start(bf16[1024,2048]{1,0:T(8,128)(2,1)S(1)} %get-tuple-element.24.dy_ref) | copy-start | bytes 12582916
  183.7 6.5 %copy-start.6 = (f32[8,2048]{1,0:T(8,128)}, f32[8,2048]{1,0:T(8,128)S(1)}, u32[]{:S(2)}) copy-start(f32[8,2048]{1,0:T(8,128)S(1)} %get-tuple-element.26.dgain_ref) | copy-start | bytes 196612
  183.7 7.1 %slice-start.2 = ((f32[1024,4384]{1,0:T(8,128)}), f32[1024,288]{1,0:T(8,128)S(1)}, s32[]{:S(2)}) async-start(f32[1024,4384]{1,0:T(8,128)} %copy-done.13), calls=%async_computation.4 | async-start | bytes 3145728 | tf_op jit(solution)/shard_map/slice | solution.py:908
  183.7 13.2 %slice-start.3 = ((s8[9175040]{0:T(1024)(128)(4,1)}), s8[4194304]{0:T(1024)(128)(4,1)S(1)}, s32[]{:S(2)}) async-start(s8[9175040]{0:T(1024)(128)(4,1)} %bitcast.84), calls=%async_computation.5 | async-start | bytes 8388608
  183.8 13.2 %slice-start.4 = ((s8[9175040]{0:T(1024)(128)(4,1)}), s8[4194304]{0:T(1024)(128)(4,1)S(1)}, s32[]{:S(2)}) async-start(s8[9175040]{0:T(1024)(128)(4,1)} %bitcast.84), calls=%async_computation.6 | async-start | bytes 8388608
  192.1 2.4 slice-start.6
  192.1 4.9 %slice-start.5 = ((s8[9175040]{0:T(1024)(128)(4,1)}), s8[786432]{0:T(1024)(128)(4,1)S(1)}, s32[]{:S(2)}) async-start(s8[9175040]{0:T(1024)(128)(4,1)} %bitcast.84), calls=%async_computation.7 | async-start | bytes 1572864
  348.5 13.0 %copy-start.16 = (f32[64,4384]{1,0:T(8,128)S(1)}, f32[64,4384]{1,0:T(8,128)}, u32[]{:S(2)}) copy-start(f32[64,4384]{1,0:T(8,128)} %get-tuple-element.67) | copy-start | bytes 3366916
  348.5 14.0 %copy-start.17 = (f32[128,1024]{1,0:T(8,128)S(1)}, f32[128,1024]{1,0:T(8,128)}, u32[]{:S(2)}) copy-start(f32[128,1024]{1,0:T(8,128)} %get-tuple-element.74) | copy-start | bytes 1572868
Sparse Core Ops, SparseCore 0:
  10.3 84.0 all-gather.2
  96.5 48.7 all-gather.4

commit v3 on v2

--- a/solution.py
+++ b/solution.py
@@ -74,83 +74,7 @@
     out_ref[...] = mm(stacked, e_ref[...])
 
 
-def conv_tile(xbuf, cw_ref, cb_ref, marks, cols, rows):
-    taps = cw_ref.shape[0]
-    pre = cb_ref[:, cols] + cw_ref[0:1, cols] * xbuf[8 : 8 + rows, cols]
-    for k in range(1, taps):
-        pre = pre + (cw_ref[k : k + 1, cols] * xbuf[8 - k : 8 - k + rows, cols]) * marks[k]
-    return pre
-
-
-def forward_kernel(
-    p_ref, prev_ref, aux_ref, seg_ref, cw_ref, cb_ref, bias_ref, rate_ref, skip_ref, gain_ref, e_ref,
-    mixed_ref, y_ref, state_out_ref,
-    xbuf, ex, state, xs, xdt, xe, bc, yin, gs,
-    *, inner, conv_width, heads, width, per_seq,
-):
-    rows = p_ref.shape[0]
-    n = (conv_width - inner) // 2
-    tiles = inner // LANES
-    conv_tiles = conv_width // LANES
-
-    @pl.when(lax.rem(pl.program_id(0), per_seq) == 0)
-    def _():
-        state[...] = jnp.zeros_like(state)
-
-    aux = aux_ref[...]
-    keep, to_end_mask = aux[:, 7:8], aux[:, 8:9]
-    shifted, step, cum, from_prev, to_end = small_terms(
-        p_ref[:, inner + conv_width :], bias_ref[...], rate_ref[...], keep, to_end_mask, rows
-    )
-    expand(e_ref, ex, step, from_prev, to_end)
-    cum_t = cum.T
-    xbuf[0:8, :] = prev_ref[:, inner : inner + conv_width]
-    xbuf[8 : 8 + rows, :] = p_ref[:, inner : inner + conv_width]
-    marks = [None] + [jnp.broadcast_to(aux[:, k : k + 1], (rows, LANES)) for k in range(1, cw_ref.shape[0])]
-    for c in range(conv_tiles):
-        cols = slice(c * LANES, (c + 1) * LANES)
-        pre = conv_tile(xbuf, cw_ref, cb_ref, marks, cols, rows)
-        act = pre * sigmoid(pre)
-        if c < tiles:
-            xs[:, cols] = act
-            scaled = act * ex[0:rows, cols]
-            xdt[:, cols] = scaled.astype(BF16)
-            xe[:, cols] = (scaled * ex[2 * rows : 3 * rows, cols]).astype(BF16)
-        else:
-            bc[:, (c - tiles) * LANES : (c - tiles + 1) * LANES] = act.astype(BF16)
-    b, cc = bc[:, :n], bc[:, n:]
-    causal = (iota((rows, rows), 0) >= iota((rows, rows), 1)) & (aux[:, 0:1] == seg_ref[0])
-    scores = jnp.where(causal, mm_nt(cc, b), 0.0)
-    state_low = state[...].astype(BF16)
-    state_out_ref[...] = state_low
-    yin[...] = mm(cc, state_low)
-    state[...] = state[...] * ex[2 * rows - 1 : 2 * rows, :] + mm_tn(b, xe[...])
-    lane = iota((1, LANES), 1)
-    masks = [(lane < width).astype(BF16), (lane >= width).astype(BF16)]
-    total = jnp.zeros((rows, LANES), F32)
-    for c in range(tiles):
-        cols = slice(c * LANES, (c + 1) * LANES)
-        mixing = []
-        for h in (2 * c, 2 * c + 1):
-            spread = jnp.minimum(cum[:, h : h + 1] - cum_t[h : h + 1, :], 0.0)
-            mixing.append((scores * jnp.exp(spread)).astype(BF16))
-        x_low = xdt[:, cols]
-        y = mm(
-            jnp.concatenate(mixing, axis=1), jnp.concatenate([x_low * masks[0], x_low * masks[1]], axis=0)
-        ) + ex[rows : 2 * rows, cols] * yin[:, cols]
-        y = y + skip_ref[:, cols] * xs[:, cols]
-        y_ref[:, cols] = y
-        gate = p_ref[:, cols]
-        gated = y * (gate * sigmoid(gate))
-        gs[:, cols] = gated
-        total = total + gated * gated
-    inverse = lax.rsqrt(jnp.sum(total, axis=1, keepdims=True) / inner + EPS)
-    for c in range(tiles):
-        cols = slice(c * LANES, (c + 1) * LANES)
-        mixed_ref[:, cols] = (gs[:, cols] * inverse * gain_ref[:, cols]).astype(BF16)
-
-
-def helpers(segment, chunk):
+def helpers(segment, valid, chunk):
     seqs, length = segment.shape
     blocks = length // chunk
     def same(shift):
@@ -163,7 +87,7 @@
     keep = (by_block == before[:, :, None]).astype(F32).reshape(seqs, length)
     to_end = (by_block == ends[:, :, None]).astype(F32).reshape(seqs, length)
     docs = segment.astype(F32)
-    columns = [docs, *back, *ahead, keep, to_end] + [jnp.zeros_like(docs)] * 7
+    columns = [docs, *back, *ahead, keep, to_end, valid] + [jnp.zeros_like(docs)] * 6
     aux = jnp.stack(columns, axis=-1).reshape(seqs * length, 16)
     return aux, docs.reshape(seqs * blocks, 1, chunk)
 
@@ -178,103 +102,6 @@
 
 def full(shape):
     return pl.BlockSpec(shape, lambda i: (0,) * len(shape))
-
-
-def scan_forward(p, aux, seg_rows, conv_w, conv_b, bias, rate, skip_row, gain_row, e, per_seq):
-    tokens, proj = p.shape
-    inner, conv_width, heads = gain_row.shape[1], conv_w.shape[1], bias.shape[1]
-    n = (conv_width - inner) // 2
-    r = CHUNK
-    chunks = tokens // r
-    return pl.pallas_call(
-        functools.partial(
-            forward_kernel, inner=inner, conv_width=conv_width, heads=heads, width=inner // heads, per_seq=per_seq
-        ),
-        grid=(chunks,),
-        in_specs=[
-            pl.BlockSpec((r, proj), lambda i: (i, 0)),
-            pl.BlockSpec((8, proj), lambda i: (jnp.maximum(i * (r // 8) - 1, 0), 0)),
-            pl.BlockSpec((r, 16), lambda i: (i, 0)),
-            pl.BlockSpec((1, 1, r), lambda i: (i, 0, 0)),
-            full(conv_w.shape), full(conv_b.shape), full(bias.shape), full(rate.shape),
-            full(skip_row.shape), full(gain_row.shape), full(e.shape),
-        ],
-        out_specs=[
-            pl.BlockSpec((r, inner), lambda i: (i, 0)),
-            pl.BlockSpec((r, inner), lambda i: (i, 0)),
-            pl.BlockSpec((n, inner), lambda i: (i, 0)),
-        ],
-        out_shape=[
-            jax.ShapeDtypeStruct((tokens, inner), BF16),
-            jax.ShapeDtypeStruct((tokens, inner), F32),
-            jax.ShapeDtypeStruct((chunks * n, inner), BF16),
-        ],
-        scratch_shapes=[
-            pltpu.VMEM((r + 8, conv_width), F32),
-            pltpu.VMEM((3 * r, inner), F32),
-            pltpu.VMEM((n, inner), F32),
-            pltpu.VMEM((r, inner), F32),
-            pltpu.VMEM((r, inner), BF16),
-            pltpu.VMEM((r, inner), BF16),
-            pltpu.VMEM((r, 2 * n), BF16),
-            pltpu.VMEM((r, inner), F32),
-            pltpu.VMEM((r, inner), F32),
-        ],
-        compiler_params=pltpu.CompilerParams(
-            dimension_semantics=("arbitrary",), vmem_limit_bytes=48 * 2**20
-        ),
-        name="scan_forward",
-    )(p, p, aux, seg_rows, conv_w, conv_b, bias, rate, skip_row, gain_row, e)
-
-
-def gate_kernel(gate_ref, ssd_ref, gm_ref, gain_ref, dy_ref, dz_ref, dgain_ref):
-    rows, inner = gate_ref.shape
-
-    @pl.when(pl.program_id(0) == 0)
-    def _():
-        dgain_ref[...] = jnp.zeros_like(dgain_ref)
-
-    squares = jnp.zeros((rows, LANES), F32)
-    cross = jnp.zeros((rows, LANES), F32)
-    for c in range(inner // LANES):
-        cols = slice(c * LANES, (c + 1) * LANES)
-        gate = gate_ref[:, cols]
-        gated = ssd_ref[:, cols] * (gate * sigmoid(gate))
-        squares = squares + gated * gated
-        cross = cross + gm_ref[:, cols] * gain_ref[:, cols] * gated
-    inverse = lax.rsqrt(jnp.sum(squares, axis=1, keepdims=True) / inner + EPS)
-    mean_cross = jnp.sum(cross, axis=1, keepdims=True) / inner * inverse
-    for c in range(inner // LANES):
-        cols = slice(c * LANES, (c + 1) * LANES)
-        gate = gate_ref[:, cols]
-        sig = sigmoid(gate)
-        silu = gate * sig
-        ssd = ssd_ref[:, cols]
-        unit = ssd * silu * inverse
-        grad_mixed = gm_ref[:, cols]
-        dgain_ref[:, cols] += jnp.sum((grad_mixed * unit).reshape(rows // 8, 8, LANES), axis=0)
-        grad_gated = inverse * (grad_mixed * gain_ref[:, cols] - unit * mean_cross)
-        dy_ref[:, cols] = (grad_gated * silu).astype(BF16)
-        dz_ref[:, cols] = (grad_gated * ssd * (sig + silu * (1.0 - sig))).astype(BF16)
-
-
-def gate_back(p, ssd, gm, gain_row):
-    tokens, inner = ssd.shape
-    r = CHUNK
-    block = pl.BlockSpec((r, inner), lambda i: (i, 0))
-    return pl.pallas_call(
-        gate_kernel,
-        grid=(tokens // r,),
-        in_specs=[block, block, block, full(gain_row.shape)],
-        out_specs=[block, block, full((8, inner))],
-        out_shape=[
-            jax.ShapeDtypeStruct((tokens, inner), BF16),
-            jax.ShapeDtypeStruct((tokens, inner), BF16),
-            jax.ShapeDtypeStruct((8, inner), F32),
-        ],
-        compiler_params=pltpu.CompilerParams(dimension_semantics=("arbitrary",), vmem_limit_bytes=32 * 2**20),
-        name="gate_backward",
-    )(p, ssd, gm, gain_row)
 
 
 MESH = pl.DeviceIdType.MESH
@@ -394,11 +221,11 @@
     px_ref, prev_ref, ssd_ref, dy_ref, state_ref,
     tail_ref, aux_ref, seg_ref, cw_ref, cb_ref, bias_ref, rate_ref, skip_ref, e_ref, et_ref,
     ngain_ref, dgain_ref, square_ref,
-    normed_t_hbm, wx_hbm, gn_hbm, tokens_hbm, gb_hbm, ggate_hbm, gout_hbm,
+    normed_t_hbm, wx_hbm, wt_hbm, gn_hbm, tokens_hbm, gb_hbm, ggate_hbm, gout_hbm,
     gi_ref, go_ref, gt_ref, small_ref,
     xbuf, ex, adj, xs, xdt, xe, bc, slope, dye, dxi, dbuf, r1, r1l, r2, r3,
     tbuf, consts, stacks, raws, cums, scores, dscores, gbs, gcs, sums, tslope, gp, gpt, accum, taccum,
-    normed_t, wx, gn, tokens, gb,
+    normed_t, wx, wt, gn, tokens, gb,
     own, part, part_t, own_t, from_core, from_core_t, from_side, from_side_t, from_level, from_level_t,
     mine, mine_t, twin, twin_t, sm, smr, smz, sems, small_sems, load_sems,
     *, inner, heads, width, levels, seq_chunks,
@@ -419,7 +246,7 @@
     rows_f = mine.shape[1]
 
     def loads():
-        pairs = ((normed_t_hbm, normed_t), (wx_hbm, wx), (gn_hbm, gn), (tokens_hbm, tokens), (gb_hbm, gb))
+        pairs = ((normed_t_hbm, normed_t), (wx_hbm, wx), (wt_hbm, wt), (gn_hbm, gn), (tokens_hbm, tokens), (gb_hbm, gb))
         return [pltpu.make_async_copy(a, b, load_sems.at[i]) for i, (a, b) in enumerate(pairs)]
 
     units = []
@@ -692,7 +519,7 @@
         tail_unit.stage(1)
         weight_grad(gp, part.at[(GROUPS - 1) % 2])
         last.stage(1)
-        input_grad(gpt, wx.at[:, inner : inner + tail_cols])
+        input_grad(gpt, wt)
         tail_unit.stage(2)
         input_grad(gp, wx.at[:, (GROUPS - 1) * cols_g : GROUPS * cols_g])
         last.stage(2)
@@ -712,7 +539,7 @@
             return total
 
         dnorm = lax.fori_loop(0, gn.shape[0] // 64, block_norm, jnp.zeros((8, d), F32))
-        leave = pltpu.make_async_copy(gb, gt_ref, load_sems.at[5])
+        leave = pltpu.make_async_copy(gb, gt_ref, load_sems.at[6])
         leave.start()
 
         def one_row(v):
@@ -768,7 +595,7 @@
 
 def back(
     px, px_block, tail, ssd, dy, states, aux, seg_rows, conv_w, conv_b, bias, rate, skip_row, e, et,
-    norm_gain, dgain, squares, normed_t, wx, gn, tokens, gb, ggate, gout, proj,
+    norm_gain, dgain, squares, normed_t, wx, wt, gn, tokens, gb, ggate, gout, proj,
 ):
     length, inner = ssd.shape
     heads = bias.shape[1]
@@ -799,7 +626,7 @@
             pl.BlockSpec((r, wide), back_at(0)),
             pl.BlockSpec((n, wide), back_at(0)),
             *[whole(a) for a in (tail, aux, seg_rows, conv_w, conv_b, bias, rate, skip_row, e, et, norm_gain, dgain, squares)],
-            *[anywhere] * 7,
+            *[anywhere] * 8,
         ],
         out_specs=[out((rows_f, proj)), out((2 * rows_f, d)), anywhere, out((8, small_cols))],
         out_shape=[
@@ -818,7 +645,7 @@
             vm((chunks, r, r), F32), vm((chunks, r, r), F32), vm((length, n), F32), vm((length, n), F32),
             vm((3, length, LANES), F32), vm((length, 2 * n), F32), vm((length, wide), BF16), vm((length, tcols), BF16),
             vm((8 * taps + 16, inner), F32), vm((8 * taps + 16, 2 * n), F32),
-            vm(normed_t.shape, BF16), vm(wx.shape, BF16), vm(gn.shape, F32), vm(tokens.shape, BF16), vm(gb.shape, BF16),
+            vm(normed_t.shape, BF16), vm(wx.shape, BF16), vm(wt.shape, BF16), vm(gn.shape, F32), vm(tokens.shape, BF16), vm(gb.shape, BF16),
             vm((units, levels, 2, rows_f, wide), BF16), vm((2, levels, 2, 2, rows_f, wide), BF16),
             vm((levels, 2, 2, rows_f, tcols), BF16), vm((levels, 2, rows_f, tcols), BF16),
             vm((units, levels, 2, rows_f, wide), BF16), vm((levels, 2, rows_f, tcols), BF16),
@@ -829,7 +656,7 @@
             vm((4, 8, small_cols), F32), vm((3, 8, small_cols), F32), vm((levels, 8, small_cols), F32),
             pltpu.SemaphoreType.DMA((units + 1, 5 + 2 * levels)),
             pltpu.SemaphoreType.DMA((4 + 2 * levels,)),
-            pltpu.SemaphoreType.DMA((6,)),
+            pltpu.SemaphoreType.DMA((7,)),
         ],
         compiler_params=pltpu.CompilerParams(
             dimension_semantics=("arbitrary", "arbitrary"), vmem_limit_bytes=60 * 2**20,
@@ -838,12 +665,487 @@
         name="scan_backward",
     )(
         px, px, ssd, dy, states, tail, aux, seg_rows, conv_w, conv_b, bias, rate, skip_row, e, et,
-        norm_gain, dgain, squares, normed_t, wx, gn, tokens, gb, ggate, gout,
+        norm_gain, dgain, squares, normed_t, wx, wt, gn, tokens, gb, ggate, gout,
     )
 
 
-def rms_scale(values):
-    return lax.rsqrt(jnp.mean(values * values, axis=1, keepdims=True) + EPS)
+class Load:
+    def __init__(self, spot, shard, whole, sems, split):
+        self.spot, self.shard, self.whole, self.sems, self.split = spot, shard, whole, sems, split
+
+    def part(self, ref):
+        if not self.split:
+            return ref
+        half = ref.shape[-1] // 2
+        cols = pl.ds(pl.multiple_of(self.spot.rep * half, half), half)
+        return ref.at[(slice(None),) * (len(ref.shape) - 1) + (cols,)]
+
+    @property
+    def a0(self):
+        spot = self.spot
+        here = self.whole.at[spot.level, spot.side, spot.core]
+        return pltpu.make_async_copy(self.part(self.shard), self.part(here), self.sems.at[0])
+
+    @property
+    def a(self):
+        spot, sems = self.spot, self.sems
+        here = self.whole.at[spot.level, spot.side, spot.core]
+        return [
+            send(self.part(self.shard), self.part(here), sems.at[5 + 2 * d], sems.at[6 + 2 * d], spot.far(d))
+            for d in range(1, spot.levels)
+        ]
+
+    @property
+    def b(self):
+        spot, sems = self.spot, self.sems
+        if self.split:
+            block = self.part(self.whole.at[:, spot.side, spot.core])
+        else:
+            half = spot.levels // 2
+            block = self.whole.at[pl.ds(spot.rep * half, half), spot.side, spot.core]
+        return send(block, block, sems.at[1], sems.at[2], spot.across)
+
+    @property
+    def c(self):
+        spot, sems = self.spot, self.sems
+        if self.split:
+            block = self.part(self.whole.at[:, :, spot.core])
+        else:
+            half = spot.levels // 2
+            block = self.whole.at[pl.ds(spot.rep * half, half), 1 - spot.side, spot.core]
+        return send(block, block, sems.at[3], sems.at[4], spot.twin)
+
+    @property
+    def d(self):
+        spot, sems = self.spot, self.sems
+        block = self.whole.at[:, :, spot.core]
+        last = 5 + 2 * spot.levels
+        return send(block, block, sems.at[last], sems.at[last + 1], spot.sibling)
+
+    def stage(self, number):
+        if number == 1:
+            self.a0.start()
+            for copy in self.a:
+                copy.start()
+        elif number == 2:
+            self.a0.wait()
+            for copy in self.a:
+                copy.wait()
+            self.b.start()
+        elif number == 3:
+            self.b.wait()
+            self.c.start()
+        elif number == 4:
+            self.c.wait()
+            self.d.start()
+        else:
+            self.d.wait()
+
+
+LOAD_STEPS = (5, 8, 12)
+
+
+def first_kernel(
+    cotan_ref, teacher_ref,
+    tokens_hbm, ngain_ref, aux_ref, seg_ref, count_ref, cw_ref, cb_ref, bias_ref, rate_ref, skip_ref, gain_ref, e_ref,
+    in_hbm, tail_hbm, out_hbm,
+    px_ref, ssd_ref, state_out_ref, tail_out, normed_out, normed_t_out, wx_out, wtail_out,
+    output_ref, gb_ref, mixed_ref, dy_ref, dz_ref, gn_ref, dgain_ref, small_ref,
+    tokens, normed, normed_t, wx, wg, wo, weight_tail, tail, pbuf, ssd_all, gates, gateds, gms, results, inverses,
+    ex, state, xs, xdt, xe, bc, yin, cums, scores, stacks,
+    counts, countr, countz, sems, count_sems, copy_sems, leave_sems,
+    *, inner, heads, width, levels, seq_chunks, loss_weight,
+):
+    step = pl.program_id(0)
+    group, chunk = step // seq_chunks, step % seq_chunks
+    rows, cols_g = px_ref.shape
+    n = bc.shape[2] // 2
+    tiles = cols_g // LANES
+    per_group = cols_g // width
+    taps = cw_ref.shape[0]
+    rows_f = in_hbm.shape[0]
+    tail_cols = tail.shape[1]
+    conv_tail = 2 * n
+    length, d_model = tokens.shape
+    spot = Spot(levels)
+    here = pl.ds(pl.multiple_of(chunk * rows, rows), rows)
+    gcol = pl.multiple_of(group * cols_g, cols_g)
+    last_step = GROUPS * seq_chunks - 1
+
+    tail_load = Load(spot, tail_hbm, weight_tail, sems.at[0], False)
+    loads = []
+    for k in range(2 * GROUPS):
+        cols = pl.ds((k % GROUPS) * cols_g, cols_g)
+        shard = in_hbm.at[:, pl.ds((inner if k < GROUPS else 0) + (k % GROUPS) * cols_g, cols_g)]
+        loads.append((shard, (wx if k < GROUPS else wg).at[:, :, :, :, cols]))
+    for k in range(GROUPS):
+        cols = pl.ds(k * (d_model // GROUPS), d_model // GROUPS)
+        loads.append((out_hbm.at[:, cols], wo.at[:, :, :, :, cols]))
+    loads = [Load(spot, shard, whole, sems.at[1 + k], k % 2 == 1) for k, (shard, whole) in enumerate(loads)]
+    leaves = [
+        (wx, wx_out), (weight_tail, wtail_out), (normed, normed_out), (normed_t, normed_t_out), (tail.at[8:], tail_out)
+    ]
+
+    def leave(k):
+        return pltpu.make_async_copy(*leaves[k], leave_sems.at[k])
+
+    exchange = lambda i: send(
+        counts.at[i], countr.at[i], count_sems.at[2 * i], count_sems.at[2 * i + 1],
+        (spot.sibling, spot.across, spot.twin)[i],
+    )
+    spread = lambda d: send(
+        counts.at[3], countz.at[spot.level], count_sems.at[4 + 2 * d], count_sems.at[5 + 2 * d], spot.far(d)
+    )
+
+    def marks_of(aux):
+        return [None] + [jnp.broadcast_to(aux[:, k : k + 1], (rows, LANES)) for k in range(1, taps)]
+
+    def conv(buffer, at, cols, wcols, marks):
+        block = buffer[pl.ds(at, rows + 8), cols]
+        pre = cb_ref[:, wcols] + cw_ref[0:1, wcols] * block[8:]
+        for k in range(1, taps):
+            pre = pre + (cw_ref[k : k + 1, wcols] * block[8 - k : 8 - k + rows]) * marks[k]
+        return pre * sigmoid(pre)
+
+    def project(weight, out, cols):
+        for i in range(length // 256):
+            out[8 + i * 256 : 8 + (i + 1) * 256, :] = mm(normed[i * 256 : (i + 1) * 256, :], weight[:, cols])
+
+    @pl.when(step == 0)
+    def _():
+        fetch = pltpu.make_async_copy(tokens_hbm, tokens, copy_sems.at[0])
+        fetch.start()
+        counts[0] = count_ref[...]
+        spot.greet()
+        tail_load.stage(1)
+        exchange(0).start()
+        loads[0].stage(1)
+        loads[1].stage(1)
+        fetch.wait()
+
+        def norm(i, carry):
+            block = pl.ds(pl.multiple_of(i * 64, 64), 64)
+            v = tokens[block, :].astype(F32)
+            v = v * lax.rsqrt(jnp.sum(v * v, axis=1, keepdims=True) / d_model + EPS)
+            normed[block, :] = (v * ngain_ref[...]).astype(BF16)
+            return carry
+
+        lax.fori_loop(0, length // 64, norm, 0)
+        tail[0:8, :] = jnp.zeros((8, tail_cols), F32)
+        pbuf[0:8, :] = jnp.zeros((8, cols_g), F32)
+        tail_load.stage(2)
+        exchange(0).wait()
+        counts[1] = counts[0] + countr[0]
+        exchange(1).start()
+        for i in range(length // 256):
+            block = slice(i * 256, (i + 1) * 256)
+            normed_t[:, block] = normed[block, :].T
+        leave(2).start()
+        leave(3).start()
+        tail_load.stage(3)
+        exchange(1).wait()
+        counts[2] = counts[1] + countr[1]
+        exchange(2).start()
+        loads[0].stage(2)
+        tail_load.stage(4)
+        exchange(2).wait()
+        counts[3] = counts[2] + countr[2]
+        for k in range(1, levels):
+            spread(k).start()
+        countz[spot.level] = counts[3]
+        loads[0].stage(3)
+        tail_load.stage(5)
+        leave(1).start()
+        project(weight_tail.reshape(d_model, tail_cols), tail, slice(0, tail_cols))
+        leave(4).start()
+        loads[0].stage(4)
+        for k in range(1, levels):
+            spread(k).wait()
+        total = countz[0]
+        for k in range(1, levels):
+            total = total + countz[k]
+        counts[4] = total
+        cums[...] = jnp.zeros_like(cums)
+
+        def shared(i, carry):
+            at = pl.ds(pl.multiple_of(i * rows, rows), rows)
+            aux = aux_ref[at, :]
+            marks = marks_of(aux)
+            start = pl.multiple_of(i * rows, rows)
+            raw = tail[pl.ds(start + 8, rows), conv_tail : conv_tail + heads]
+            shifted, size, cum, from_prev, to_end = small_terms(
+                raw, bias_ref[...], rate_ref[...], aux[:, 7:8], aux[:, 8:9], rows
+            )
+            cums[i, :, 0:heads] = cum
+            stacks[i] = jnp.concatenate(
+                [jnp.concatenate(split2(v), axis=1) for v in (size, from_prev, to_end)], axis=0
+            )
+            for c in range(conv_tail // LANES):
+                cols = slice(c * LANES, (c + 1) * LANES)
+                act = conv(tail, start, cols, slice(inner + c * LANES, inner + (c + 1) * LANES), marks)
+                bc[i, :, cols] = act.astype(BF16)
+            causal = (iota((rows, rows), 0) >= iota((rows, rows), 1)) & (aux[:, 0:1] == seg_ref[i])
+            scores[i] = jnp.where(causal, mm_nt(bc[i, :, n:], bc[i, :, 0:n]), 0.0)
+            return carry
+
+        lax.fori_loop(0, seq_chunks, shared, 0)
+
+    scan_steps = GROUPS * seq_chunks
+    events = {}
+    for k in range(1, 3 * GROUPS):
+        begin = max(0, (k - 2) * 3 * seq_chunks // 8)
+        times = [begin, *[begin + 1 + delay * seq_chunks // 8 for delay in LOAD_STEPS]]
+        if k == 1:
+            times = [None, 1, seq_chunks // 2, seq_chunks - 1]
+        need = min(k * seq_chunks, scan_steps)
+        for number, when in enumerate(times):
+            if when is not None:
+                events.setdefault(min(when, need), []).append((k, number + 1))
+        if k < 2 * GROUPS:
+            events.setdefault(need, []).append((k, 5))
+    late = sorted(events.pop(scan_steps), key=lambda pair: (pair[1] + pair[0], pair[0]))
+    for at, happen in sorted(events.items()):
+
+        @pl.when(step == at)
+        def _(happen=sorted(happen, key=lambda pair: (pair[0], pair[1]))):
+            for k, number in happen:
+                loads[k].stage(number)
+
+    @pl.when(step == scan_steps)
+    def _():
+        leave(0).start()
+        for k, number in late:
+            loads[k].stage(number)
+
+    for g in range(GROUPS):
+
+        @pl.when(step == g * seq_chunks)
+        def _(g=g):
+            if g == 0:
+                loads[0].stage(5)
+            project(wx.reshape(d_model, inner), pbuf, slice(g * cols_g, (g + 1) * cols_g))
+
+    @pl.when(step < scan_steps)
+    def _():
+        @pl.when(chunk == 0)
+        def _():
+            state[...] = jnp.zeros_like(state)
+
+        aux = aux_ref[here, :]
+        marks = marks_of(aux)
+        ex[...] = mm(stacks[chunk], e_ref[:, pl.ds(gcol, cols_g)])
+        head0 = group * per_group
+        pick = (iota((LANES, LANES), 0) == iota((LANES, LANES), 1) + head0).astype(BF16)
+        moved = [mm(v, pick) for v in split3(cums[chunk])]
+        cum = moved[0] + moved[1] + moved[2]
+        cum_t = cum.T
+        start = pl.multiple_of(chunk * rows, rows)
+        px_ref[...] = pbuf[pl.ds(start + 8, rows), :]
+        for c in range(tiles):
+            cols = slice(c * LANES, (c + 1) * LANES)
+            act = conv(pbuf, start, cols, pl.ds(gcol + c * LANES, LANES), marks)
+            xs[:, cols] = act
+            scaled = act * ex[0:rows, cols]
+            xdt[:, cols] = scaled.astype(BF16)
+            xe[:, cols] = (scaled * ex[2 * rows : 3 * rows, cols]).astype(BF16)
+        b, cc = bc[chunk, :, 0:n], bc[chunk, :, n:]
+        state_low = state[...].astype(BF16)
+        state_out_ref[...] = state_low
+        yin[...] = mm(cc, state_low)
+        state[...] = state[...] * ex[2 * rows - 1 : 2 * rows, :] + mm_tn(b, xe[...])
+        score = scores[chunk]
+        lane = iota((1, LANES), 1)
+        masks = [(lane < width).astype(BF16), (lane >= width).astype(BF16)]
+        for c in range(tiles):
+            cols = slice(c * LANES, (c + 1) * LANES)
+            mixing = []
+            for h in (2 * c, 2 * c + 1):
+                spread_h = jnp.minimum(cum[:, h : h + 1] - cum_t[h : h + 1, :], 0.0)
+                mixing.append((score * jnp.exp(spread_h)).astype(BF16))
+            x_low = xdt[:, cols]
+            y = mm(
+                jnp.concatenate(mixing, axis=1), jnp.concatenate([x_low * masks[0], x_low * masks[1]], axis=0)
+            ) + ex[rows : 2 * rows, cols] * yin[:, cols]
+            acols = pl.ds(gcol + c * LANES, LANES)
+            y = y + skip_ref[:, acols] * xs[:, cols]
+            ssd_ref[:, cols] = y
+            ssd_all[here, acols] = y
+
+    @pl.when(step >= scan_steps)
+    def _():
+        turn = step - scan_steps
+        block_rows = gates.shape[0]
+        base = pl.multiple_of(turn * block_rows, block_rows)
+        flat_gate = wg.reshape(d_model, inner)
+        flat_out = wo.reshape(inner, d_model)
+        sub = 64
+        own_rows = normed[pl.ds(base, block_rows), :]
+        for k in range(GROUPS):
+            cols = slice(k * cols_g, (k + 1) * cols_g)
+            gates[:, cols] = mm(own_rows, flat_gate[:, cols])
+
+        @pl.when(turn == 0)
+        def _():
+            dgain_ref[...] = jnp.zeros_like(dgain_ref)
+            small_ref[...] = jnp.zeros_like(small_ref)
+            for k in range(2 * GROUPS, 3 * GROUPS):
+                loads[k].stage(5)
+
+        def norm_of(i):
+            at = pl.ds(pl.multiple_of(i * sub, sub), sub)
+            return at, pl.ds(pl.multiple_of(base + i * sub, sub), sub)
+
+        def forward_part(i, carry):
+            at, full_at = norm_of(i)
+            squares = jnp.zeros((sub, LANES), F32)
+            for c in range(inner // LANES):
+                cols = slice(c * LANES, (c + 1) * LANES)
+                gate = gates[at, cols]
+                gated = ssd_all[full_at, cols] * (gate * sigmoid(gate))
+                gateds[at, cols] = gated
+                squares = squares + gated * gated
+            inverse = lax.rsqrt(jnp.sum(squares, axis=1, keepdims=True) / inner + EPS)
+            for c in range(inner // LANES):
+                cols = slice(c * LANES, (c + 1) * LANES)
+                unit = gateds[at, cols] * inverse
+                gateds[at, cols] = unit
+                mixed_ref[at, cols] = (unit * gain_ref[:, cols]).astype(BF16)
+            inverses[at, :] = jnp.broadcast_to(inverse, (sub, LANES))
+            return carry
+
+        lax.fori_loop(0, block_rows // sub, forward_part, 0)
+        results[...] = mm(mixed_ref[...], flat_out[...])
+        scale = 2.0 * loss_weight / (counts[4, 0:1, :] * d_model)
+
+        def loss_part(i, carry):
+            at, full_at = norm_of(i)
+            valid = jnp.broadcast_to(aux_ref[full_at, 9:10], (sub, LANES))
+            squares = jnp.zeros((8, LANES), F32)
+            for c in range(d_model // LANES):
+                cols = slice(c * LANES, (c + 1) * LANES)
+                result = tokens[full_at, cols].astype(F32) + results[at, cols]
+                output_ref[at, cols] = result.astype(BF16)
+                error = result - teacher_ref[at, cols].astype(F32)
+                squares = squares + jnp.sum((valid * error * error).reshape(sub // 8, 8, LANES), axis=0)
+                gb_ref[at, cols] = (valid * (cotan_ref[at, cols].astype(F32) + scale * error)).astype(BF16)
+            small_ref[0:8, :] += squares
+            return carry
+
+        lax.fori_loop(0, block_rows // sub, loss_part, 0)
+        small_ref[8:16, :] = counts[4]
+        grads = gb_ref[...]
+        for k in range(GROUPS):
+            cols = slice(k * cols_g, (k + 1) * cols_g)
+            gms[:, cols] = mm_nt(grads, flat_out[cols, :])
+
+        def backward_part(i, carry):
+            at, full_at = norm_of(i)
+            cross = jnp.zeros((sub, LANES), F32)
+            for c in range(inner // LANES):
+                cols = slice(c * LANES, (c + 1) * LANES)
+                cross = cross + gms[at, cols] * gain_ref[:, cols] * gateds[at, cols]
+            inverse = inverses[at, :]
+            mean_cross = jnp.sum(cross, axis=1, keepdims=True) / inner
+            for c in range(inner // LANES):
+                cols = slice(c * LANES, (c + 1) * LANES)
+                gate = gates[at, cols]
+                sig = sigmoid(gate)
+                silu = gate * sig
+                unit = gateds[at, cols]
+                grad_mixed = gms[at, cols]
+                dgain_ref[:, cols] += jnp.sum((grad_mixed * unit).reshape(sub // 8, 8, LANES), axis=0)
+                grad_gated = inverse * (grad_mixed * gain_ref[:, cols] - unit * mean_cross)
+                dy_ref[at, cols] = (grad_gated * silu).astype(BF16)
+                dz_ref[at, cols] = (
+                    grad_gated * ssd_all[full_at, cols] * (sig + silu * (1.0 - sig))
+                ).astype(BF16)
+            return carry
+
+        lax.fori_loop(0, block_rows // sub, backward_part, 0)
+        gn_ref[...] = mm_nt(dz_ref[...], flat_gate[...])
+
+        @pl.when(turn == length // block_rows - 1)
+        def _():
+            for k in range(len(leaves)):
+                leave(k).wait()
+
+
+def first(
+    tokens, norm_gain, aux, seg_rows, count, conv_w, conv_b, bias, rate, skip_row, gain_row, e,
+    cotangent, teacher, w_in, w_tail, w_out, levels, loss_weight,
+):
+    length, d = tokens.shape
+    heads, inner = bias.shape[1], skip_row.shape[1]
+    rows_f = w_in.shape[0]
+    n = (conv_w.shape[1] - inner) // 2
+    r = CHUNK
+    chunks = length // r
+    wide = inner // GROUPS
+    tcols = w_tail.shape[1]
+    units = 3 * GROUPS
+    tall = 256
+    scan_steps = GROUPS * chunks
+
+    def scan_block(s):
+        s = jnp.minimum(s, scan_steps - 1)
+        return s % chunks, s // chunks
+
+    block = lambda h: pl.BlockSpec((h, wide), scan_block)
+    late = lambda w: pl.BlockSpec((tall, w), lambda s: (jnp.maximum(s - scan_steps, 0), 0))
+    whole = lambda a: pl.BlockSpec(a.shape, lambda s: (0,) * a.ndim, pipeline_mode=pl.Buffered(1))
+    fixed = lambda *dims: pl.BlockSpec(dims, lambda s: (0,) * len(dims))
+    anywhere = pl.BlockSpec(memory_space=pl.ANY)
+    vm = pltpu.VMEM
+    shape = jax.ShapeDtypeStruct
+    wide_shape = (levels, 2, 2, rows_f, inner)
+    return pl.pallas_call(
+        functools.partial(
+            first_kernel, inner=inner, heads=heads, width=inner // heads, levels=levels, seq_chunks=chunks,
+            loss_weight=loss_weight,
+        ),
+        grid=(scan_steps + length // tall,),
+        in_specs=[
+            late(d), late(d), anywhere,
+            *[whole(a) for a in (norm_gain, aux, seg_rows, count, conv_w, conv_b, bias, rate, skip_row, gain_row, e)],
+            anywhere, anywhere, anywhere,
+        ],
+        out_specs=[
+            block(r), block(r), block(n), *[anywhere] * 5,
+            late(d), late(d), late(inner), late(inner), late(inner), late(d), fixed(8, inner), fixed(16, LANES),
+        ],
+        out_shape=[
+            shape((length, inner), F32), shape((length, inner), F32), shape((chunks * n, inner), BF16),
+            shape((length, tcols), F32), shape((length, d), BF16), shape((d, length), BF16),
+            shape(wide_shape, BF16), shape((levels, 2, 2, rows_f, tcols), BF16),
+            shape((length, d), BF16), shape((length, d), BF16), shape((length, inner), BF16),
+            shape((length, inner), BF16), shape((length, inner), BF16), shape((length, d), F32),
+            shape((8, inner), F32), shape((16, LANES), F32),
+        ],
+        scratch_shapes=[
+            vm((length, d), BF16), vm((length, d), BF16), vm((d, length), BF16),
+            vm(wide_shape, BF16), vm(wide_shape, BF16), vm((levels, 2, 2, 2 * rows_f, d), BF16),
+            vm((levels, 2, 2, rows_f, tcols), BF16),
+            vm((length + 8, tcols), F32), vm((length + 8, wide), F32), vm((length, inner), F32),
+            vm((tall, inner), F32), vm((tall, inner), F32), vm((tall, inner), F32), vm((tall, d), F32),
+            vm((tall, LANES), F32),
+            vm((3 * r, wide), F32), vm((n, wide), F32), vm((r, wide), F32), vm((r, wide), BF16), vm((r, wide), BF16),
+            vm((chunks, r, 2 * n), BF16), vm((r, wide), F32), vm((chunks, r, LANES), F32), vm((chunks, r, r), F32),
+            vm((chunks, 3 * r, 2 * heads), BF16),
+            vm((5, 8, LANES), F32), vm((3, 8, LANES), F32), vm((levels, 8, LANES), F32),
+            pltpu.SemaphoreType.DMA((units + 1, 7 + 2 * levels)),
+            pltpu.SemaphoreType.DMA((4 + 2 * levels,)),
+            pltpu.SemaphoreType.DMA((1,)),
+            pltpu.SemaphoreType.DMA((5,)),
+        ],
+        compiler_params=pltpu.CompilerParams(
+            dimension_semantics=("arbitrary",), vmem_limit_bytes=60 * 2**20,
+            collective_id=2, has_side_effects=True,
+        ),
+        name="scan_forward",
+    )(
+        cotangent, teacher, tokens, norm_gain, aux, seg_rows, count, conv_w, conv_b, bias, rate, skip_row, gain_row, e,
+        w_in, w_tail, w_out,
+    )
 
 
 def on_device(
@@ -864,53 +1166,37 @@
 ):
     seqs, length, width = tokens.shape
     rows = seqs * length
-    every = ("rep", "fsdp")
     shards = lax.axis_size("fsdp")
     devices = lax.axis_size("rep") * shards
+    levels = shards // 4
     loss_weight = float(rows * devices * width // 8)
-    valid = valid_mask.reshape(rows, 1).astype(F32)
-    total_count = lax.psum(jnp.sum(valid), every)
-    denominator = total_count * width
-
-    flat = tokens.reshape(rows, width)
-    inputs = flat.astype(F32)
-    normed = (inputs * rms_scale(inputs) * norm_gain[None, :]).astype(BF16)
-    w_in = lax.all_gather(in_weight, "fsdp", axis=0, tiled=True)
-    w_out = lax.all_gather(out_weight, "fsdp", axis=0, tiled=True)
-    projected = mm(normed, w_in)
-
+    valid = valid_mask.astype(F32)
     heads = step_bias.shape[0]
     inner = out_gain.shape[0]
     head_width = inner // heads
-    aux, seg_rows = helpers(segment, CHUNK)
+    aux, seg_rows = helpers(segment, valid, CHUNK)
     e, et = head_maps(heads, head_width)
     rate = -jnp.exp(decay_log)[None, :]
     skip_row = jnp.repeat(skip_gain, head_width)[None, :]
-    per_seq = length // CHUNK
     params = (conv_weight, conv_bias[None, :], step_bias[None, :], rate, skip_row)
-    gain_row = out_gain[None, :]
-    mixed, ssd, states = scan_forward(projected, aux, seg_rows, *params, gain_row, e, per_seq)
-
-    result = inputs + mm(mixed, w_out)
-    error = result - teacher.reshape(rows, width).astype(F32)
-    squares = jnp.sum((valid * error * error).reshape(rows, width // LANES, LANES), axis=(0, 1))
-    cotan = cotangent.reshape(rows, width).astype(F32)
-    grad_result = valid * (cotan + 2.0 * loss_weight * error / denominator)
-    grad_branch = grad_result.astype(BF16)
-    grad_out = mm_tn(mixed, grad_branch).astype(BF16)
-    grad_mixed = mm_nt(grad_branch, w_out)
-    dy, dz, dgain = gate_back(projected, ssd, grad_mixed, gain_row)
-    grad_gate = mm_tn(normed, dz).astype(BF16)
-    gn = mm_nt(dz, w_in[:, :inner])
-    levels = shards // 4
     tail_at = 2 * inner
     tail_pad = -(in_weight.shape[1] - tail_at) % LANES
-    tail = jnp.pad(projected[:, tail_at:], ((0, 0), (0, tail_pad)))
-    wx = jnp.pad(w_in[:, inner:], ((0, 0), (0, tail_pad)))
-    squares8 = jnp.pad(squares[None, :], ((0, 7), (0, 0)))
+    in_tail = jnp.pad(in_weight[:, tail_at:], ((0, 0), (0, tail_pad)))
+    count = jnp.broadcast_to(jnp.sum(valid), (8, LANES))
+    flat, cotan, target = (v.reshape(rows, width) for v in (tokens, cotangent, teacher))
+    (
+        px, ssd, states, tail, normed, normed_t, wx, wt, output, grad_branch, mixed, dy, dz, gn, dgain, sums
+    ) = first(
+        flat, norm_gain[None, :], aux, seg_rows, count, *params, out_gain[None, :], e, cotan, target,
+        in_weight, in_tail, out_weight, levels, loss_weight,
+    )
+    wx, wt = (w.reshape(-1, w.shape[-1]) for w in (wx, wt))
+    denominator = sums[8, 0] * width
+    grad_out = mm_tn(mixed, grad_branch).astype(BF16)
+    grad_gate = mm(normed_t, dz).astype(BF16)
     grad_in, grad_out, grad_tokens, small = back(
-        projected, inner // (inner // GROUPS), tail, ssd, dy, states, aux, seg_rows, *params, e, et,
-        norm_gain[None, :], dgain, squares8, normed.T, wx, gn, flat, grad_branch,
+        px, 0, tail, ssd, dy, states, aux, seg_rows, *params, e, et,
+        norm_gain[None, :], dgain, sums[:8], normed_t, wx, wt, gn, flat, grad_branch,
         grad_gate.reshape(levels, 2, 2, width // shards, inner),
         grad_out.reshape(levels, 2, 2, inner // shards, width), in_weight.shape[1],
     )
@@ -918,7 +1204,7 @@
     extra = small[7, width:]
     loss = jnp.sum(extra[2 * LANES : 3 * LANES]) / denominator
     return (
-        result.astype(BF16).reshape(tokens.shape),
+        output.reshape(tokens.shape),
         loss,
         grad_tokens.reshape(tokens.shape),
         small[7, :width],

time: 372 us -> 341 us (0.917)
  Pallas kernels: 188 us -> 289 us
  blocking collectives: 43.7 us -> 0 us
  matrix products: 50.3 us -> 15.7 us
  waiting for transfers between devices: 24.7 us -> 0 us
  local copies, waits for them, and re-layouts: 34.4 us -> 20.6 us
  between operations: 16.8 us -> 3.17 us
    pallas_call x2 -> x1, Pallas kernels: 42.1 us -> 143 us  [first(): pl.pallas_call(functools.partial(first_kernel, inner=inner, heads=heads,...]
    psum x1 -> x0, blocking collectives: 43.7 us -> none  [on_device(): total_count = lax.psum(jnp.sum(valid), every)]
    all_gather x2 -> x0, waiting for transfers between devices: 23.3 us -> none  [the longest x1 22.3 us: on_device(): w_in = lax.all_gather(in_weight, 'fsdp', axis=0, tiled=True)]
    dot_general x2 -> x1, matrix products: 24.5 us -> 6.1 us  [mm(): return jnp.dot(a, b, preferred_element_type=F32)]
    dot_general x2 -> x0, matrix products: 13.1 us -> none  [mm_nt(): return lax.dot_general(a, b, NT, preferred_element_type=F32)]
    unnamed x56 -> x19, local copies, waits for them, and re-layouts: 13.4 us -> 4.54 us
    transpose x1 -> x0, local copies, waits for them, and re-layouts: 3.93 us -> none  [on_device(): grad_in, grad_out, grad_tokens, small = back(projected, inner // (inner /...]
    dot_general x2 -> x1, matrix products: 12.7 us -> 9.62 us  [mm_tn(): return lax.dot_general(a, b, TN, preferred_element_type=F32)]
  transfers between devices with their start and end apart: 2 -> 0, of which waited for: 2 -> 0; matrix products, arithmetic and copies ran while one was open for 8% -> 0% of each run, Pallas kernels for 8% -> 0%
where the time goes in v3:
time: 341 us; the launch traced here: 340 us
  Pallas kernels  289 us (85%)
  local copies, waits for them, and re-layouts  20.6 us (6%)
  matrix products  15.7 us (5%)
  other arithmetic  11.5 us (3%)
    pallas_call x1, Pallas kernels, back(): pl.pallas_call(functools.partial(back_kernel, inner=inner, heads=heads, w...  146 us
    pallas_call x1, Pallas kernels, first(): pl.pallas_call(functools.partial(first_kernel, inner=inner, heads=heads,...  143 us
    dot_general x1, matrix products, mm_tn(): return lax.dot_general(a, b, TN, preferred_element_type=F32)  9.62 us

profile of v3, /device:TPU:0, one launch (start us, length us, event | category | flops | bytes accessed | tf_op | source)
XLA Modules:
  0.0 340.4 jit_solution(18333445499796281793)
XLA Ops:
  0.6 0.8 slice.82
  1.7 0.7 compare_convert_fusion
  2.4 0.8 compare_convert_fusion.2
  3.2 0.8 compare_convert_fusion.3
  4.2 0.8 compare_convert_fusion.4
  5.1 1.3 convert_bitcast_fusion.1
  6.4 0.7 convert_bitcast_fusion
  7.2 1.0 copy.41
  8.2 0.7 add_convert_fusion.e_ref
  9.0 0.7 broadcast_in_dim.29
  9.7 0.7 broadcast_in_dim_reshape.3.skip_ref
  10.4 1.3 broadcast_in_dim.27.cb_ref
  11.7 1.2 negate_bitcast_fusion.rate_ref
  12.8 0.8 slice.85
  14.3 1.3 convert_reduce_fusion
  15.6 1.2 broadcast_in_dim.26.count_ref
  16.8 143.4 %scan_forward.1 = (f32[1024,2048]{1,0:T(8,128)}, f32[1024,2048]{1,0:T(8,128)}, bf16[1024,2048]{1,0:T(8,128)(2,1)}, f32[1024,384]{1,0:T(8,128)}, bf16[1024,1024]{...) custom-call(bf16[1024,1024]{1,0:T(8,128)(2,1)} %bitcast.64, ...), custom_call_target="tpu_custom_call" | custom-call | tf_op jit(solution)/shard_map/scan_forward/pallas_call | solution.py:1101
  160.3 9.6 %convolution_convert_fusion = bf16[2048,1024]{1,0:T(8,128)(2,1)} fusion(bf16[1024,2048]{1,0:T(8,128)(2,1)} %get-tuple-element.45, bf16[1024,1024]{1,0:T(8,128)(2,1)} %get-tuple-element.43.gb_hbm), kind=kOutput, calls=%fused_computation | convolution fusion | flops 4297064448 | bytes 10485760 | tf_op jit(solution)/shard_map/dot_general | solution.py:28
  169.9 6.1 %convolution_convert_fusion.1 = bf16[1024,2048]{1,0:T(8,128)(2,1)} fusion(bf16[1024,1024]{1,0:T(8,128)(2,1)S(1)} %copy-done, bf16[1024,2048]{1,0:T(8,128)(2,1)S(1)} %copy-done.6), kind=kOutput, calls=%fused_computation.1 | convolution fusion | flops 4297064448 | bytes 10485760 | tf_op jit(solution)/shard_map/dot_general | solution.py:20
  176.6 1.1 fusion.et_ref
  177.7 146.0 %scan_backward.1 = (f32[64,4384]{1,0:T(8,128)}, f32[128,1024]{1,0:T(8,128)}, bf16[1024,1024]{1,0:T(8,128)(2,1)}, f32[8,2432]{1,0:T(8,128)}) custom-call(f32[1024,2048]{1,0:T(8,128)} %get-tuple-element.32.px_ref.prev_ref, f32[1024,2048]{1,0:T(8,128)} %get-tuple-element.32.px_ref.prev_ref, f32[1024,2048]{1,0:T(8,128)} %get-tuple-element.33.ssd_ref, ...), custom_call_target="tpu_custom_call" | custom-call | tf_op jit(solution)/shard_map/scan_backward/pallas_call | solution.py:617
  323.8 1.5 slice.90
  325.3 1.5 fusion.4
  326.9 0.6 reduce_sum.29
  327.5 1.5 slice_reduce_fusion
  329.0 1.4 slice.89
  330.4 1.3 slice_reduce_fusion.2
  333.5 1.3 slice_bitcast_fusion
  334.9 1.3 copy.47
  336.2 1.3 copy.48
  337.5 1.0 copy.49
  338.5 0.8 copy.50
  (29 shorter events, 2.4 us)
Async XLA Ops:
  160.3 9.6 %copy-start = (bf16[1024,1024]{1,0:T(8,128)(2,1)S(1)}, bf16[1024,1024]{1,0:T(8,128)(2,1)}, u32[]{:S(2)}) copy-start(bf16[1024,1024]{1,0:T(8,128)(2,1)} %get-tuple-element.39.normed_t_hbm) | copy-start | bytes 6291460
  160.3 9.6 %copy-start.6 = (bf16[1024,2048]{1,0:T(8,128)(2,1)S(1)}, bf16[1024,2048]{1,0:T(8,128)(2,1)}, u32[]{:S(2)}) copy-start(bf16[1024,2048]{1,0:T(8,128)(2,1)} %get-tuple-element.44) | copy-start | bytes 12582916
  169.9 6.1 %copy-start.5 = (f32[16,128]{1,0:T(8,128)S(1)}, f32[16,128]{1,0:T(8,128)}, u32[]{:S(2)}) copy-start(f32[16,128]{1,0:T(8,128)} %get-tuple-element.38) | copy-start | bytes 24580
  177.7 157.1 %copy-start.1 = (bf16[1024,1024]{1,0:T(8,128)(2,1)S(1)}, bf16[1024,1024]{1,0:T(8,128)(2,1)}, u32[]{:S(2)}) copy-start(bf16[1024,1024]{1,0:T(8,128)(2,1)} %get-tuple-element.31) | copy-start | bytes 6291460
  333.5 2.7 copy-start.2
  334.9 2.6 copy-start.3
  336.2 2.3 copy-start.4

commit v4 on v3

--- a/solution.py
+++ b/solution.py
@@ -46,6 +46,12 @@
     return parts[:, :heads] + parts[:, heads : 2 * heads] + parts[:, 2 * heads :]
 
 
+def sum_tri(v, tri):
+    heads = v.shape[0]
+    parts = mm(jnp.concatenate(split3(v), axis=0), tri)
+    return parts[:heads] + parts[heads : 2 * heads] + parts[2 * heads :]
+
+
 def sigmoid(v):
     return 0.5 * jnp.tanh(0.5 * v) + 0.5
 
@@ -74,34 +80,137 @@
     out_ref[...] = mm(stacked, e_ref[...])
 
 
-def helpers(segment, valid, chunk):
-    seqs, length = segment.shape
-    blocks = length // chunk
-    def same(shift):
-        return (segment[:, shift:] == segment[:, :-shift]).astype(F32)
-    back = [jnp.pad(same(k), ((0, 0), (k, 0))) for k in (1, 2, 3)]
-    ahead = [jnp.pad(same(k), ((0, 0), (0, k))) for k in (1, 2, 3)]
-    by_block = segment.reshape(seqs, blocks, chunk)
-    ends = by_block[:, :, -1]
-    before = jnp.pad(ends[:, :-1], ((0, 0), (1, 0)), constant_values=-1)
-    keep = (by_block == before[:, :, None]).astype(F32).reshape(seqs, length)
-    to_end = (by_block == ends[:, :, None]).astype(F32).reshape(seqs, length)
-    docs = segment.astype(F32)
-    columns = [docs, *back, *ahead, keep, to_end, valid] + [jnp.zeros_like(docs)] * 6
-    aux = jnp.stack(columns, axis=-1).reshape(seqs * length, 16)
-    return aux, docs.reshape(seqs * blocks, 1, chunk)
-
-
-def head_maps(heads, width):
-    inner = heads * width
-    owner = jnp.arange(inner) // width
-    one = (jnp.arange(heads)[:, None] == owner[None, :]).astype(BF16)
-    down = (owner[:, None] == jnp.arange(LANES)[None, :]).astype(BF16)
-    return jnp.concatenate([one, one], axis=0), down
-
-
 def full(shape):
     return pl.BlockSpec(shape, lambda i: (0,) * len(shape))
+
+
+def prepare_kernel(
+    segment_ref, valid_ref, bias_ref, log_ref, skip_ref, cb_ref, ngain_ref, gain_ref, weight_ref,
+    aux_ref, rows_ref, count_ref, bias_out, rate_out, rate_t_out, skip_out, cb_out, ngain_out, gain_out, e_out, tail_out,
+    *, tail_cols,
+):
+    length = segment_ref.shape[1]
+    heads = bias_ref.shape[0]
+    inner = gain_ref.shape[0]
+    width = inner // heads
+    docs = segment_ref[...].astype(F32)
+    valid = valid_ref[...].astype(F32)
+    place = iota((8, length), 1)
+    wide = jnp.broadcast_to(docs, (8, length))
+    marks = []
+    for k in (1, 2, 3):
+        marks.append(jnp.where((wide == pltpu.roll(wide, k, 1)) & (place >= k), 1.0, 0.0)[0:1])
+    for k in (1, 2, 3):
+        marks.append(jnp.where((wide == pltpu.roll(wide, length - k, 1)) & (place < length - k), 1.0, 0.0)[0:1])
+    for c in range(length // CHUNK):
+        cols = slice(c * CHUNK, (c + 1) * CHUNK)
+        own = docs[:, cols]
+        last = docs[:, (c + 1) * CHUNK - 1 : (c + 1) * CHUNK]
+        keep = jnp.zeros_like(own)
+        if c:
+            keep = jnp.where(own == docs[:, c * CHUNK - 1 : c * CHUNK], 1.0, 0.0)
+        stacked = [own, *[v[:, cols] for v in marks], keep, jnp.where(own == last, 1.0, 0.0), valid[:, cols]]
+        stacked.append(jnp.zeros((LANES - len(stacked), CHUNK), F32))
+        aux_ref[cols, :] = jnp.concatenate(stacked, axis=0).T[:, 0:16]
+        rows_ref[c] = own
+    count_ref[...] = jnp.broadcast_to(jnp.sum(valid, axis=1, keepdims=True), count_ref.shape)
+    bias_out[...] = bias_ref[...].reshape(1, heads)
+    rate = -jnp.exp(log_ref[...].reshape(1, heads))
+    rate_out[...] = rate
+    spare = jnp.concatenate([rate, jnp.zeros((1, LANES - heads), F32)], axis=1)
+    rate_t_out[...] = jnp.broadcast_to(spare, (LANES, LANES)).T[0:heads, 0:1]
+    e = (iota((2 * heads, inner), 0) % heads == iota((2 * heads, inner), 1) // width).astype(BF16)
+    e_out[...] = e
+    skip = jnp.broadcast_to(skip_ref[...].reshape(1, heads), (16, heads))
+    parts = [mm(v, e[0:heads]) for v in split3(skip)]
+    skip_out[...] = (parts[0] + parts[1] + parts[2])[0:1]
+    cb_out[...] = cb_ref[...].reshape(1, cb_ref.shape[0])
+    ngain_out[...] = ngain_ref[...].reshape(1, ngain_ref.shape[0])
+    gain_out[...] = gain_ref[...].reshape(1, inner)
+    rows_f = weight_ref.shape[0]
+    tail_out[...] = jnp.concatenate(
+        [weight_ref[:, 0:tail_cols], jnp.zeros((rows_f, tail_out.shape[1] - tail_cols), BF16)], axis=1
+    )
+
+
+def prepare(segment, valid_mask, step_bias, decay_log, skip_gain, conv_bias, norm_gain, out_gain, in_weight):
+    length = segment.shape[1]
+    heads, inner = step_bias.shape[0], out_gain.shape[0]
+    rows_f, proj = in_weight.shape
+    tail_cols = proj - 2 * inner
+    tail_wide = -(-tail_cols // LANES) * LANES
+    shape = jax.ShapeDtypeStruct
+    small = (segment, valid_mask, step_bias, decay_log, skip_gain, conv_bias, norm_gain, out_gain)
+    outs = [
+        shape((length, 16), F32), shape((length // CHUNK, 1, CHUNK), F32), shape((8, LANES), F32),
+        shape((1, heads), F32), shape((1, heads), F32), shape((heads, 1), F32), shape((1, inner), F32),
+        shape((1, conv_bias.shape[0]), F32), shape((1, norm_gain.shape[0]), F32), shape((1, inner), F32),
+        shape((2 * heads, inner), BF16), shape((rows_f, tail_wide), BF16),
+    ]
+    block = 512
+    return pl.pallas_call(
+        functools.partial(prepare_kernel, tail_cols=tail_cols),
+        grid=(1,),
+        in_specs=[*[full(a.shape) for a in small], pl.BlockSpec((rows_f, block), lambda i: (0, 2 * inner // block))],
+        out_specs=[full(o.shape) for o in outs],
+        out_shape=outs,
+        name="prepare",
+    )(*small, in_weight)
+
+
+def finish_kernel(
+    gi_ref, go_ref, gt_ref, output_ref, small_ref, dng_ref, sums_ref, e_ref,
+    out_final, loss_ref, gt_final, ngain_ref, gi_final, cw_ref, cb_ref, bias_ref, log_ref, skip_ref, gain_ref, go_final,
+    gi, go, gt, output, sems,
+):
+    trios = ((gt_ref, gt, gt_final), (output_ref, output, out_final), (gi_ref, gi, gi_final), (go_ref, go, go_final))
+    fetches = [pltpu.make_async_copy(a, b, sems.at[i]) for i, (a, b, c) in enumerate(trios)]
+    stores = [pltpu.make_async_copy(b, c, sems.at[4 + i]) for i, (a, b, c) in enumerate(trios)]
+    for copy in fetches:
+        copy.start()
+    for fetched, stored in zip(fetches, stores):
+        fetched.wait()
+        stored.start()
+    taps, conv_width = cw_ref.shape
+    heads, inner = bias_ref.shape[0], gain_ref.shape[0]
+    d = dng_ref.shape[0] * LANES
+    cw_ref[...] = small_ref[0:taps, 0:conv_width]
+    cb_ref[...] = small_ref[taps : taps + 1, 0:conv_width].reshape(conv_width)
+    gain_ref[...] = small_ref[5:6, 0:inner].reshape(inner)
+    bias_ref[...] = small_ref[7:8, 0:heads].reshape(heads)
+    log_ref[...] = small_ref[7:8, LANES : LANES + heads].reshape(heads)
+    squares = jnp.sum(small_ref[7:8, 2 * LANES : 3 * LANES], axis=1, keepdims=True)
+    loss_ref[...] = squares / (sums_ref[8:9, 0:1] * d)
+    by_head = jnp.zeros((16, 2 * heads), F32)
+    for v in split3(jnp.broadcast_to(small_ref[6:7, 0:inner], (16, inner))):
+        by_head = by_head + mm_nt(v, e_ref[...])
+    skip_ref[...] = by_head[0:1, 0:heads].reshape(heads)
+    ngain_ref[...] = dng_ref[...].reshape(d)
+    for copy in stores:
+        copy.wait()
+
+
+def finish(gi, go, gt, output, small, dng, sums, e, taps, conv_width, heads, inner):
+    shape = jax.ShapeDtypeStruct
+    anywhere = pl.BlockSpec(memory_space=pl.ANY)
+    outs = [
+        shape(output.shape, BF16), shape((1, 1), F32), shape(gt.shape, BF16), shape((dng.size,), F32),
+        shape(gi.shape, F32), shape((taps, conv_width), F32), shape((conv_width,), F32), shape((heads,), F32),
+        shape((heads,), F32), shape((heads,), F32), shape((inner,), F32), shape(go.shape, F32),
+    ]
+    far = (0, 2, 4, 11)
+    return pl.pallas_call(
+        finish_kernel,
+        grid=(1,),
+        in_specs=[*[anywhere] * 4, *[full(a.shape) for a in (small, dng, sums, e)]],
+        out_specs=[anywhere if i in far else full(o.shape) for i, o in enumerate(outs)],
+        out_shape=outs,
+        scratch_shapes=[
+            *[pltpu.VMEM(a.shape, a.dtype) for a in (gi, go, gt, output)], pltpu.SemaphoreType.DMA((8,)),
+        ],
+        compiler_params=pltpu.CompilerParams(vmem_limit_bytes=60 * 2**20),
+        name="finish",
+    )(gi, go, gt, output, small, dng, sums, e)
 
 
 MESH = pl.DeviceIdType.MESH
@@ -119,9 +228,14 @@
     def far(self, step):
         return (self.rep, ((self.level + step) % self.levels) * 4 + self.at % 4)
 
-    def greet(self):
+    def corner(self, j):
+        flip = lambda v, bit: 1 - v if j & bit else v
+        return (flip(self.rep, 4), self.level * 4 + flip(self.side, 2) * 2 + flip(self.core, 1))
+
+    def greet(self, corners=False):
         barrier = pltpu.get_barrier_semaphore()
-        partners = [self.sibling, self.across, self.twin] + [self.far(d) for d in range(1, self.levels)]
+        near = [self.corner(j) for j in range(1, 8)] if corners else [self.sibling, self.across, self.twin]
+        partners = near + [self.far(d) for d in range(1, self.levels)]
         for one in partners:
             pl.semaphore_signal(barrier, inc=1, device_id=one, device_id_type=MESH)
         pl.semaphore_wait(barrier, len(partners))
@@ -133,9 +247,107 @@
     )
 
 
+class Split:
+    def __init__(self, spot, whole, own, from_core, half, from_side, from_level, mine, from_twin, sems, write):
+        self.spot, self.whole, self.own, self.write = spot, whole, own, write
+        self.from_core, self.half, self.from_side, self.from_level = from_core, half, from_side, from_level
+        self.mine, self.from_twin, self.sems = mine, from_twin, sems
+        self.cols = half.shape[-1]
+
+    def columns(self, rep):
+        return pl.ds(pl.multiple_of(rep * self.cols, self.cols), self.cols)
+
+    @property
+    def c0(self):
+        return pltpu.make_async_copy(self.whole.at[:, :, self.spot.core], self.own, self.sems.at[6])
+
+    @property
+    def c1(self):
+        spot, sems = self.spot, self.sems
+        return send(self.whole.at[:, :, 1 - spot.core], self.from_core, sems.at[0], sems.at[1], spot.sibling)
+
+    @property
+    def c2(self):
+        spot, sems = self.spot, self.sems
+        block = self.own.at[:, :, :, self.columns(1 - spot.rep)]
+        return send(block, self.half, sems.at[2], sems.at[3], spot.twin)
+
+    @property
+    def c3(self):
+        spot, sems = self.spot, self.sems
+        last = 5 + 2 * spot.levels
+        return send(self.half.at[:, 1 - spot.side], self.from_side, sems.at[last], sems.at[last + 1], spot.across)
+
+    @property
+    def c4(self):
+        spot, sems = self.spot, self.sems
+        return [
+            send(
+                self.from_side.at[(spot.level + d) % spot.levels], self.from_level.at[d - 1],
+                sems.at[5 + 2 * d], sems.at[6 + 2 * d], spot.far(d),
+            )
+            for d in range(1, spot.levels)
+        ]
+
+    @property
+    def c5(self):
+        spot, sems = self.spot, self.sems
+        return send(self.mine, self.from_twin, sems.at[4], sems.at[5], spot.twin)
+
+    def stage(self, number):
+        spot, levels = self.spot, self.spot.levels
+        if number == 1:
+            self.c1.start()
+            self.c0.start()
+        elif number == 2:
+            self.c0.wait()
+            self.c1.wait()
+
+            def add(i, carry):
+                for side in range(2):
+                    self.own[i, side] = self.own[i, side] + self.from_core[i, side]
+                return carry
+
+            lax.fori_loop(0, levels, add, 0)
+            self.c2.start()
+        elif number == 3:
+            self.c2.wait()
+            columns = self.columns(spot.rep)
+
+            def add(i, carry):
+                for side in range(2):
+                    self.half[i, side] = self.half[i, side] + self.own[i, side, :, columns]
+                return carry
+
+            lax.fori_loop(0, levels, add, 0)
+            self.c3.start()
+        elif number == 4:
+            self.c3.wait()
+
+            def add(i, carry):
+                self.from_side[i] = self.from_side[i] + self.half[i, spot.side]
+                return carry
+
+            lax.fori_loop(0, levels, add, 0)
+            for copy in self.c4:
+                copy.start()
+        elif number == 5:
+            for copy in self.c4:
+                copy.wait()
+            total = self.from_side[spot.level].astype(F32)
+            for d in range(levels - 1):
+                total = total + self.from_level[d].astype(F32)
+            self.mine[...] = total.astype(BF16)
+            self.c5.start()
+        else:
+            self.c5.wait()
+            self.write(self.mine[...].astype(F32), self.columns(spot.rep))
+            self.write(self.from_twin[...].astype(F32), self.columns(1 - spot.rep))
+
+
 class Unit:
-    def __init__(self, spot, whole, own, from_core, from_side, from_level, mine, from_twin, sems, local, write):
-        self.spot, self.whole, self.own, self.local, self.write = spot, whole, own, local, write
+    def __init__(self, spot, whole, own, from_core, from_side, from_level, mine, from_twin, sems, write):
+        self.spot, self.whole, self.own, self.write = spot, whole, own, write
         self.from_core, self.from_side, self.from_level = from_core, from_side, from_level
         self.mine, self.from_twin = mine, from_twin
         self.sems = sems
@@ -181,9 +393,7 @@
 
             def add(i, carry):
                 for side in range(2):
-                    self.own[i, side] = (
-                        self.own[i, side].astype(F32) + self.from_core[i, side].astype(F32)
-                    ).astype(BF16)
+                    self.own[i, side] = self.own[i, side] + self.from_core[i, side]
                 return carry
 
             lax.fori_loop(0, levels, add, 0)
@@ -192,9 +402,7 @@
             self.c2.wait()
 
             def add(i, carry):
-                self.from_side[i] = (
-                    self.from_side[i].astype(F32) + self.own[i, spot.side].astype(F32)
-                ).astype(BF16)
+                self.from_side[i] = self.from_side[i] + self.own[i, spot.side]
                 return carry
 
             lax.fori_loop(0, levels, add, 0)
@@ -214,20 +422,22 @@
 
 
 GROUPS = 4
-BACKGROUND_STARTS = (0, 2, 5, 7, 11, 13, 18, 21)
+STARTS = (0, 2, 4, 6, 8, 11, 13, 16, 18, 20, 24)
+UNIT_DELAYS = (0, 1, 5, 9, 11)
+SPLIT_DELAYS = (0, 1, 5, 8, 11, 13)
 
 
 def back_kernel(
-    px_ref, prev_ref, ssd_ref, dy_ref, state_ref,
-    tail_ref, aux_ref, seg_ref, cw_ref, cb_ref, bias_ref, rate_ref, skip_ref, e_ref, et_ref,
+    px_ref, prev_ref, y_ref, dy_ref, state_ref,
+    tail_ref, aux_ref, seg_ref, cw_ref, cb_ref, bias_ref, rate_ref, skip_ref, e_ref, rate_t_ref,
     ngain_ref, dgain_ref, square_ref,
     normed_t_hbm, wx_hbm, wt_hbm, gn_hbm, tokens_hbm, gb_hbm, ggate_hbm, gout_hbm,
-    gi_ref, go_ref, gt_ref, small_ref,
+    gi_ref, go_ref, gt_ref, small_ref, dng_ref,
     xbuf, ex, adj, xs, xdt, xe, bc, slope, dye, dxi, dbuf, r1, r1l, r2, r3,
-    tbuf, consts, stacks, raws, cums, scores, dscores, gbs, gcs, sums, tslope, gp, gpt, accum, taccum,
+    tbuf, consts, stacks, raws, cums, cum_ts, ones, steps, scores, dscores, gbs, gcs, sums, tslope, gp, gpt, accum, taccum,
     normed_t, wx, wt, gn, tokens, gb,
     own, part, part_t, own_t, from_core, from_core_t, from_side, from_side_t, from_level, from_level_t,
-    mine, mine_t, twin, twin_t, sm, smr, smz, sems, small_sems, load_sems,
+    mine, mine_t, twin, twin_t, half, half_side, half_level, half_mine, half_twin, local, sm, smr, smz, gain_out, gain_near, gain_sum, gain_far, sems, small_sems, gain_sems, load_sems,
     *, inner, heads, width, levels, seq_chunks,
 ):
     group, turn = pl.program_id(0), pl.program_id(1)
@@ -249,54 +459,66 @@
         pairs = ((normed_t_hbm, normed_t), (wx_hbm, wx), (wt_hbm, wt), (gn_hbm, gn), (tokens_hbm, tokens), (gb_hbm, gb))
         return [pltpu.make_async_copy(a, b, load_sems.at[i]) for i, (a, b) in enumerate(pairs)]
 
+    def writer(ref, row, col, wide):
+        def write(v, columns=None):
+            if columns is None:
+                ref[row : row + rows_f, col : col + wide] = v[:, :wide]
+            else:
+                at = pl.multiple_of(col + columns.start, LANES)
+                ref[row : row + rows_f, pl.ds(at, columns.size)] = v
+        return write
+
+    sources = []
+    for u in range(GROUPS):
+        hbm = gout_hbm.at[:, :, :, pl.ds((u // 2) * rows_f, rows_f), pl.ds((u % 2) * cols_g, cols_g)]
+        sources.append((hbm, writer(go_ref, (u // 2) * rows_f, (u % 2) * cols_g, cols_g)))
+    for u in range(GROUPS):
+        hbm = ggate_hbm.at[:, :, :, :, pl.ds(u * cols_g, cols_g)]
+        sources.append((hbm, writer(gi_ref, 0, u * cols_g, cols_g)))
+    for g in range(GROUPS):
+        sources.append((part.at[g % 2], writer(gi_ref, 0, inner + g * cols_g, cols_g)))
+    order = [0, 1, 2, 3, 8, 4, 5, 9, 6, 7, 10, 11]
     units = []
-
-    def writer(ref, row, col, wide):
-        def write(v):
-            ref[row : row + rows_f, col : col + wide] = v[:, :wide]
-        return write
-
-    for u in range(GROUPS * 2):
-        if u < GROUPS:
-            hbm = gout_hbm.at[:, :, :, pl.ds((u // 2) * rows_f, rows_f), pl.ds((u % 2) * cols_g, cols_g)]
-            write = writer(go_ref, (u // 2) * rows_f, (u % 2) * cols_g, cols_g)
+    for i, u in enumerate(order):
+        k = i // 2
+        whole, write = sources[u]
+        if i % 2:
+            units.append(
+                Split(
+                    spot, whole, own.at[u], from_core.at[u], half.at[k], half_side.at[k], half_level.at[k],
+                    half_mine.at[k], half_twin.at[k], sems.at[u], write,
+                )
+            )
         else:
-            hbm = ggate_hbm.at[:, :, :, :, pl.ds((u - GROUPS) * cols_g, cols_g)]
-            write = writer(gi_ref, 0, (u - GROUPS) * cols_g, cols_g)
-        units.append((u, hbm, own.at[u], write))
-    for g in range(GROUPS):
-        u = 2 * GROUPS + g
-        units.append((u, part.at[g % 2], own.at[u], writer(gi_ref, 0, inner + g * cols_g, cols_g)))
-    units = [
-        Unit(
-            spot, whole, mine_half, from_core.at[u], from_side.at[u], from_level.at[u], mine.at[u], twin.at[u],
-            sems.at[u], True, write,
-        )
-        for u, whole, mine_half, write in units
-    ]
+            units.append(
+                Unit(
+                    spot, whole, own.at[u], from_core.at[u], from_side.at[k], from_level.at[k], mine.at[k], twin.at[k],
+                    sems.at[u], write,
+                )
+            )
     tail_wide = gi_ref.shape[1] - 2 * inner
     tail_unit = Unit(
-        spot, part_t, own_t, from_core_t, from_side_t, from_level_t, mine_t, twin_t, sems.at[3 * GROUPS], True,
+        spot, part_t, own_t, from_core_t, from_side_t, from_level_t, mine_t, twin_t, sems.at[3 * GROUPS],
         writer(gi_ref, 0, 2 * inner, tail_wide),
     )
 
     events = {}
     last_step = GROUPS * seq_chunks - 1
     late = []
-    plan = [(s * seq_chunks // 8, units[u]) for u, s in enumerate(BACKGROUND_STARTS)]
-    plan += [((g + 1) * seq_chunks, units[2 * GROUPS + g]) for g in range(GROUPS - 1)]
-    for begin, unit in plan:
-        for number, delay in ((1, 0), (2, 1), (3, 4), (4, 7), (5, 8)):
-            events.setdefault(min(begin + delay, last_step), []).append((unit, number))
+    for i, (begin, unit) in enumerate(zip(STARTS, units)):
+        begin = begin * seq_chunks // 8
+        for number, delay in enumerate(SPLIT_DELAYS if i % 2 else UNIT_DELAYS):
+            events.setdefault(min(begin + delay, last_step), []).append((unit, number + 1))
 
     @pl.when(step == 0)
     def _():
         for copy in loads():
             copy.start()
-        spot.greet()
+        spot.greet(corners=True)
         accum[...] = jnp.zeros_like(accum)
         taccum[...] = jnp.zeros_like(taccum)
-        cums[...] = jnp.zeros_like(cums)
+        steps[...] = jnp.zeros_like(steps)
+        ones[...] = (iota(ones.shape, 0) == iota(ones.shape, 1) // width).astype(BF16)
 
     for at, happen in sorted(events.items()):
         if at == last_step:
@@ -309,7 +531,7 @@
                 unit.stage(number)
 
     def fold(v):
-        return jnp.sum(v.reshape(rows // 8, 8, v.shape[1]), axis=0)
+        return jnp.sum(v.reshape(v.shape[0] // 8, 8, v.shape[1]), axis=0)
 
     aux = aux_ref[here, :]
     marks = [None] + [jnp.broadcast_to(aux[:, k : k + 1], (rows, LANES)) for k in range(1, taps)]
@@ -325,14 +547,23 @@
         return pre
 
     def conv_back(buffer, cols, wcols, acc, acc_cols):
-        grad = buffer[0:rows, cols]
-        out = cw_ref[0:1, wcols] * grad
-        acc[8 * taps : 8 * taps + 8, acc_cols] += fold(grad)
-        acc[0:8, acc_cols] += fold(grad * xbuf[8 : 8 + rows, cols])
-        for k in range(1, taps):
-            out = out + (cw_ref[k : k + 1, wcols] * buffer[k : k + rows, cols]) * marks_next[k]
-            acc[8 * k : 8 * k + 8, acc_cols] += fold(grad * (xbuf[8 - k : 8 - k + rows, cols] * marks[k]))
-        return out
+        outs = []
+        adds = [jnp.zeros((8, LANES), F32) for _ in range(taps + 1)]
+        for at in range(0, rows, 64):
+            inputs = xbuf[8 + at : 72 + at, cols]
+            for k in range(taps):
+                grad = buffer[at + k : at + k + 64, cols]
+                if k == 0:
+                    out = cw_ref[0:1, wcols] * grad
+                    adds[taps] = adds[taps] + fold(grad)
+                else:
+                    grad = grad * marks_next[k][at : at + 64]
+                    out = out + cw_ref[k : k + 1, wcols] * grad
+                adds[k] = adds[k] + fold(grad * inputs)
+            outs.append(out)
+        for k in range(taps + 1):
+            acc[8 * k : 8 * k + 8, acc_cols] += adds[k]
+        return jnp.concatenate(outs, axis=0)
 
     def fill_tail():
         xbuf[8 : 8 + rows, 0:conv_tail] = tail_ref[here, 0:conv_tail]
@@ -344,9 +575,11 @@
         shifted, step_size, cum, from_prev, to_end = small_terms(
             tail_ref[here, conv_tail : conv_tail + heads], bias_ref[...], rate, aux[:, 7:8], aux[:, 8:9], rows
         )
-        raws[here, 0:heads] = shifted
-        raws[here, heads : 2 * heads] = step_size
-        cums[chunk, :, 0:heads] = cum
+        turned = jnp.concatenate([shifted, step_size, cum, jnp.zeros((rows, LANES - 3 * heads), F32)], axis=1).T
+        raws[chunk] = turned[0 : 2 * heads]
+        cum_ts[chunk] = turned[2 * heads : 3 * heads]
+        for g in range(GROUPS):
+            cums[g, here, 0:per_group] = cum[:, g * per_group : (g + 1) * per_group]
         stacks[chunk] = jnp.concatenate(
             [jnp.concatenate(split2(v), axis=1) for v in (step_size, from_prev, to_end)], axis=0
         )
@@ -363,9 +596,6 @@
         dscores[chunk] = jnp.zeros((rows, rows), F32)
         gbs[here, :] = jnp.zeros((rows, n), F32)
         gcs[here, :] = jnp.zeros((rows, n), F32)
-        consts[chunk] = jnp.zeros((8, LANES), F32)
-        for i in range(3):
-            sums[i, here, :] = jnp.zeros((rows, LANES), F32)
 
     @pl.when(turn == 0)
     def _():
@@ -373,12 +603,9 @@
         dbuf[rows : rows + 8, :] = jnp.zeros((8, cols_g), F32)
 
     ex[...] = mm(stacks[chunk], e_ref[:, pl.ds(gcol, cols_g)])
-    head0 = group * per_group
-    pick = (iota((LANES, LANES), 0) == iota((LANES, LANES), 1) + head0).astype(BF16)
-    cum_all = cums[chunk]
-    moved = [mm(v, pick) for v in split3(cum_all)]
-    cum = moved[0] + moved[1] + moved[2]
-    cum_t = cum.T
+    own_heads = pl.ds(pl.multiple_of(group * per_group, per_group), per_group)
+    cum = cums[group, here, :]
+    cum_t = cum_ts[chunk, own_heads, :]
     xbuf[0:8, :] = prev_ref[...]
     xbuf[8 : 8 + rows, :] = px_ref[...]
     for c in range(tiles):
@@ -425,19 +652,20 @@
         both = within + across
         grad_ssd = dy_low.astype(F32)
         x_scaled = x_low.astype(F32)
-        r1[:, cols], r1l[:, cols] = split2(grad_ssd * (ssd_ref[:, cols] - skip * x) - within * x_scaled)
+        r1[:, cols], r1l[:, cols] = split2(grad_ssd * y_ref[:, cols] - within * x_scaled)
         r2[:, cols] = (across * x_scaled).astype(BF16)
         r3[:, cols] = (both * x).astype(BF16)
         accum[8 * taps + 8 : 8 * taps + 16, acols] += fold(grad_ssd * x)
         grad_x = skip * grad_ssd + ex[0:rows, cols] * both
         dbuf[0:rows, cols] = grad_x * slope[:, cols]
     dscores[chunk] += grad_scores_t
-    et = et_ref[pl.ds(gcol, cols_g), :]
-    sums[0, here, :] += mm(r1[...], et) + mm(r1l[...], et)
-    sums[1, here, :] += mm(r2[...], et)
-    sums[2, here, :] += mm(r3[...], et)
-    high, rest = split2(jnp.broadcast_to(through, (8, cols_g)))
-    consts[chunk] += mm(high, et) + mm(rest, et)
+    by_head = ones[...]
+    sums[0, chunk, own_heads, :] = (mm_nt(by_head, r1[...]) + mm_nt(by_head, r1l[...]))[0:per_group]
+    sums[1, chunk, own_heads, :] = mm_nt(by_head, r2[...])[0:per_group]
+    sums[2, chunk, own_heads, :] = mm_nt(by_head, r3[...])[0:per_group]
+    high, rest = split2(jnp.broadcast_to(through, (16, cols_g)))
+    const = (mm_nt(by_head, high) + mm_nt(by_head, rest))[0:per_group, 0:1]
+    consts[chunk, own_heads, :] = jnp.broadcast_to(const, (per_group, LANES))
     for c in range(tiles):
         cols = slice(c * LANES, (c + 1) * LANES)
         acols = pl.ds(gcol + c * LANES, LANES)
@@ -464,41 +692,31 @@
                 tbuf, cols, slice(inner + c * LANES, inner + (c + 1) * LANES), taccum, cols
             ).astype(BF16)
         tbuf[rows : rows + 8, :] = tbuf[0:8, :]
-        shifted = raws[here, 0:heads]
-        step_size = raws[here, heads : 2 * heads]
-        const = consts[chunk, 0:1, 0:heads]
+        shifted, step_size = raws[chunk, 0:heads, :], raws[chunk, heads : 2 * heads, :]
+        turned_aux = jnp.concatenate([aux, jnp.zeros((rows, LANES - aux.shape[1]), F32)], axis=1).T
         grad_log = (
-            tri_sum(upper.astype(BF16), sums[0, here, 0:heads])
-            + tri_sum((iota((rows, rows), 0) > iota((rows, rows), 1)).astype(BF16), sums[1, here, 0:heads])
-            + const
-        ) * aux[:, 1:2]
-        grad_raw = (sums[2, here, 0:heads] + rate * grad_log) * sigmoid(shifted)
-        gpt[here, conv_tail:] = jnp.concatenate(
-            [grad_raw, jnp.zeros((rows, tail_cols - conv_tail - heads), F32)], axis=1
+            sum_tri(sums[0, chunk], lower.astype(BF16))
+            + sum_tri(sums[1, chunk], (iota((rows, rows), 0) < iota((rows, rows), 1)).astype(BF16))
+            + consts[chunk]
+        ) * turned_aux[1:2, :]
+        rate_t = jnp.broadcast_to(rate_t_ref[...], (heads, rows))
+        grad_raw = (sums[2, chunk] + rate_t * grad_log) * sigmoid(shifted)
+        gpt[here, conv_tail:] = (
+            jnp.concatenate([grad_raw, jnp.zeros((tail_cols - conv_tail - heads, rows), F32)], axis=0).T
         ).astype(BF16)
-        small = 8 * taps + 8
-        taccum[small : small + 8, 0:heads] += fold(grad_raw)
-        taccum[small : small + 8, LANES : LANES + heads] += fold(step_size * grad_log * rate)
+        steps[0] += grad_raw
+        steps[1] += step_size * grad_log * rate_t
 
     def weight_grad(low, out):
-        def one(i, carry):
-            block = pl.ds(pl.multiple_of(i * 4 * rows_f, 4 * rows_f), 4 * rows_f)
-            v = mm(normed_t[block, :], low[...]).astype(BF16)
-            for side in range(2):
-                for core in range(2):
-                    at = (2 * side + core) * rows_f
-                    out[i, side, core] = v[at : at + rows_f]
-            return carry
-
-        lax.fori_loop(0, levels, one, 0)
+        flat = out.reshape(normed_t.shape[0], low.shape[1])
+        for k in range(0, low.shape[1], 256):
+            cols = slice(k, min(k + 256, low.shape[1]))
+            flat[:, cols] = mm(normed_t[...], low[:, cols]).astype(BF16)
 
     def input_grad(low, weights):
-        def one(i, carry):
-            block = pl.ds(pl.multiple_of(i * 256, 256), 256)
-            gn[block, :] += mm_nt(low[block, :], weights[...])
-            return carry
-
-        lax.fori_loop(0, gn.shape[0] // 256, one, 0)
+        for k in range(gn.shape[1] // 256):
+            cols = slice(k * 256, (k + 1) * 256)
+            gn[:, cols] += mm_nt(low[...], weights[cols, :])
 
     for g in range(GROUPS - 1):
 
@@ -512,18 +730,59 @@
 
     @pl.when(step == last_step)
     def _():
+        d = gn.shape[1]
+        half_cols = sm.shape[2]
+
+        def half_of(core):
+            return pl.ds(pl.multiple_of(core * half_cols, half_cols), half_cols)
+
+        def exchange(i):
+            src = (local.at[:, half_of(1 - spot.core)], sm.at[0], sm.at[1], sm.at[3])[i]
+            device = (spot.sibling, spot.across, spot.twin, spot.sibling)[i]
+            return send(src, smr.at[i], small_sems.at[2 * i], small_sems.at[2 * i + 1], device)
+
+        spread = lambda k: send(
+            sm.at[2], smz.at[spot.level], small_sems.at[6 + 2 * k], small_sems.at[7 + 2 * k], spot.far(k)
+        )
+
+        def one_row(v):
+            return jnp.sum(v, axis=0, keepdims=True)
+
+        def fold_small(i):
+            exchange(i).wait()
+            sm[i] = (local[:, half_of(spot.core)] if i == 0 else sm[i - 1]) + smr[i]
+
+        local[...] = jnp.zeros(local.shape, F32)
+        for k in range(taps + 1):
+            local[k : k + 1, 0:inner] = one_row(accum[8 * k : 8 * k + 8, :])
+            local[k : k + 1, inner : inner + conv_tail] = one_row(taccum[8 * k : 8 * k + 8, 0:conv_tail])
+        local[5:6, 0:inner] = one_row(dgain_ref[...])
+        local[6:7, 0:inner] = one_row(accum[8 * taps + 8 : 8 * taps + 16, :])
+        for i in range(2):
+            turned = jnp.concatenate([steps[i], jnp.zeros((LANES - heads, LANES), F32)], axis=0).T
+            local[7:8, i * LANES : (i + 1) * LANES] = one_row(turned)
+        local[7:8, 2 * LANES : 3 * LANES] = one_row(square_ref[...])
+        exchange(0).start()
         for unit, number in sorted(late, key=lambda pair: pair[1]):
             unit.stage(number)
-        last = units[3 * GROUPS - 1]
+        last = units[-1]
         weight_grad(gpt, part_t)
         tail_unit.stage(1)
+        fold_small(0)
+        exchange(1).start()
         weight_grad(gp, part.at[(GROUPS - 1) % 2])
         last.stage(1)
+        tail_unit.stage(2)
+        fold_small(1)
+        exchange(2).start()
         input_grad(gpt, wt)
-        tail_unit.stage(2)
+        last.stage(2)
+        fold_small(2)
+        for k in range(1, levels):
+            spread(k).start()
+        smz[spot.level] = sm[2]
         input_grad(gp, wx.at[:, (GROUPS - 1) * cols_g : GROUPS * cols_g])
-        last.stage(2)
-        d = gn.shape[1]
+        tail_unit.stage(3)
         ngain = ngain_ref[...]
 
         def block_norm(i, total):
@@ -538,66 +797,63 @@
             gb[block, :] = (gb[block, :].astype(F32) + rinv * (grad - scaled * mean)).astype(BF16)
             return total
 
-        dnorm = lax.fori_loop(0, gn.shape[0] // 64, block_norm, jnp.zeros((8, d), F32))
+        blocks = gn.shape[0] // 64
+        dnorm = lax.fori_loop(0, blocks // 2, block_norm, jnp.zeros((8, d), F32))
+        last.stage(3)
+        dnorm = lax.fori_loop(blocks // 2, blocks, block_norm, dnorm)
         leave = pltpu.make_async_copy(gb, gt_ref, load_sems.at[6])
         leave.start()
-
-        def one_row(v):
-            return jnp.sum(v, axis=0, keepdims=True)
-
-        local = sm.at[0]
-        local[...] = jnp.zeros(local.shape, F32)
-        for k in range(taps + 1):
-            local[k : k + 1, 0:inner] = one_row(accum[8 * k : 8 * k + 8, :])
-            local[k : k + 1, inner : inner + conv_tail] = one_row(taccum[8 * k : 8 * k + 8, 0:conv_tail])
-        local[5:6, 0:inner] = one_row(dgain_ref[...])
-        local[6:7, 0:inner] = one_row(accum[8 * taps + 8 : 8 * taps + 16, :])
-        local[7:8, 0:d] = one_row(dnorm)
-        small = 8 * taps + 8
-        local[7:8, d : d + conv_tail] = one_row(taccum[small : small + 8, 0:conv_tail])
-        local[7:8, d + conv_tail : d + conv_tail + LANES] = one_row(square_ref[...])
-        exchange = [
-            send(sm.at[i], smr.at[i], small_sems.at[2 * i], small_sems.at[2 * i + 1], device)
-            for i, device in enumerate((spot.sibling, spot.across, spot.twin))
-        ]
-        spread = [
-            send(sm.at[3], smz.at[spot.level], small_sems.at[4 + 2 * d], small_sems.at[5 + 2 * d], spot.far(d))
-            for d in range(1, levels)
-        ]
-
-        def fold_small(i):
-            exchange[i].wait()
-            sm[i + 1] = sm[i] + smr[i]
-
-        exchange[0].start()
-        tail_unit.stage(3)
-        fold_small(0)
-        exchange[1].start()
-        last.stage(3)
-        fold_small(1)
-        exchange[2].start()
+        dnorm = one_row(dnorm)
+        place = spot.rep * 4 + spot.side * 2 + spot.core
+        for k in range(d // LANES):
+            gain_out[k : k + 1, :] = dnorm[:, k * LANES : (k + 1) * LANES]
+        near = lambda k: send(
+            gain_out, gain_near.at[place], gain_sems.at[2 * k - 2], gain_sems.at[2 * k - 1], spot.corner(k)
+        )
+        beyond = lambda k: send(
+            gain_sum, gain_far.at[spot.level], gain_sems.at[12 + 2 * k], gain_sems.at[13 + 2 * k], spot.far(k)
+        )
+        for k in range(1, 8):
+            near(k).start()
+        gain_near[place] = gain_out[...]
+        last.stage(4)
+        for k in range(1, levels):
+            spread(k).wait()
+        total = smz[0]
+        for k in range(1, levels):
+            total = total + smz[k]
+        sm[3] = total
+        exchange(3).start()
+        for k in range(1, 8):
+            near(k).wait()
+        total = gain_near[0]
+        for k in range(1, 8):
+            total = total + gain_near[k]
+        gain_sum[...] = total
+        for k in range(1, levels):
+            beyond(k).start()
+        gain_far[spot.level] = gain_sum[...]
         tail_unit.stage(4)
-        fold_small(2)
-        for copy in spread:
-            copy.start()
-        smz[spot.level] = sm[3]
-        last.stage(4)
+        last.stage(5)
+        for k in range(1, levels):
+            beyond(k).wait()
+        total = gain_far[0]
+        for k in range(1, levels):
+            total = total + gain_far[k]
+        dng_ref[...] = total
+        exchange(3).wait()
+        small_ref[:, half_of(spot.core)] = sm[3]
+        small_ref[:, half_of(1 - spot.core)] = smr[3]
         tail_unit.stage(5)
-        for copy in spread:
-            copy.wait()
-        total = smz[0]
-        for i in range(1, levels):
-            total = total + smz[i]
-        small_ref[...] = total
-        last.stage(5)
+        last.stage(6)
         leave.wait()
 
 
 def back(
-    px, px_block, tail, ssd, dy, states, aux, seg_rows, conv_w, conv_b, bias, rate, skip_row, e, et,
+    px, px_block, tail, y, dy, states, aux, seg_rows, conv_w, conv_b, bias, rate, skip_row, e, rate_t,
     norm_gain, dgain, squares, normed_t, wx, wt, gn, tokens, gb, ggate, gout, proj,
 ):
-    length, inner = ssd.shape
+    length, inner = y.shape
     heads = bias.shape[1]
     levels, rows_f = ggate.shape[0], ggate.shape[3]
     taps = conv_w.shape[0]
@@ -607,7 +863,7 @@
     wide = inner // GROUPS
     tcols = tail.shape[1]
     d = normed_t.shape[0]
-    small_cols = inner + tcols
+    small_cols = inner + tcols + LANES
     units = 3 * GROUPS
     back_at = lambda off: lambda g, c: (chunks - 1 - c, g + off)
     whole = lambda a: pl.BlockSpec(a.shape, lambda g, c: (0,) * a.ndim, pipeline_mode=pl.Buffered(1))
@@ -625,37 +881,46 @@
             pl.BlockSpec((r, wide), back_at(0)),
             pl.BlockSpec((r, wide), back_at(0)),
             pl.BlockSpec((n, wide), back_at(0)),
-            *[whole(a) for a in (tail, aux, seg_rows, conv_w, conv_b, bias, rate, skip_row, e, et, norm_gain, dgain, squares)],
+            *[whole(a) for a in (tail, aux, seg_rows, conv_w, conv_b, bias, rate, skip_row, e, rate_t, norm_gain, dgain, squares)],
             *[anywhere] * 8,
         ],
-        out_specs=[out((rows_f, proj)), out((2 * rows_f, d)), anywhere, out((8, small_cols))],
+        out_specs=[out((rows_f, proj)), out((2 * rows_f, d)), anywhere, out((8, small_cols)), out((d // LANES, LANES))],
         out_shape=[
             jax.ShapeDtypeStruct((rows_f, proj), F32),
             jax.ShapeDtypeStruct((2 * rows_f, d), F32),
             jax.ShapeDtypeStruct((length, d), BF16),
             jax.ShapeDtypeStruct((8, small_cols), F32),
+            jax.ShapeDtypeStruct((d // LANES, LANES), F32),
         ],
         scratch_shapes=[
             vm((r + 8, wide), F32), vm((3 * r, wide), F32), vm((n, wide), F32), vm((r, wide), F32),
             vm((r, wide), BF16), vm((r, wide), BF16), vm((chunks, r, 2 * n), BF16), vm((r, wide), F32),
             vm((r, wide), BF16), vm((r, wide), F32), vm((r + 8, wide), F32),
             vm((r, wide), BF16), vm((r, wide), BF16), vm((r, wide), BF16), vm((r, wide), BF16),
-            vm((r + 8, 2 * n), F32), vm((chunks, 8, LANES), F32),
-            vm((chunks, 3 * r, 2 * heads), BF16), vm((length, LANES), F32), vm((chunks, r, LANES), F32),
+            vm((r + 8, 2 * n), F32), vm((chunks, heads, LANES), F32),
+            vm((chunks, 3 * r, 2 * heads), BF16), vm((chunks, 2 * heads, r), F32), vm((GROUPS, length, LANES), F32),
+            vm((chunks, heads, r), F32), vm((16, wide), BF16), vm((2, heads, r), F32),
             vm((chunks, r, r), F32), vm((chunks, r, r), F32), vm((length, n), F32), vm((length, n), F32),
-            vm((3, length, LANES), F32), vm((length, 2 * n), F32), vm((length, wide), BF16), vm((length, tcols), BF16),
-            vm((8 * taps + 16, inner), F32), vm((8 * taps + 16, 2 * n), F32),
+            vm((3, chunks, heads, r), F32), vm((length, 2 * n), F32), vm((length, wide), BF16), vm((length, tcols), BF16),
+            vm((8 * taps + 16, inner), F32), vm((8 * taps + 8, 2 * n), F32),
             vm(normed_t.shape, BF16), vm(wx.shape, BF16), vm(wt.shape, BF16), vm(gn.shape, F32), vm(tokens.shape, BF16), vm(gb.shape, BF16),
             vm((units, levels, 2, rows_f, wide), BF16), vm((2, levels, 2, 2, rows_f, wide), BF16),
             vm((levels, 2, 2, rows_f, tcols), BF16), vm((levels, 2, rows_f, tcols), BF16),
             vm((units, levels, 2, rows_f, wide), BF16), vm((levels, 2, rows_f, tcols), BF16),
-            vm((units, levels, rows_f, wide), BF16), vm((levels, rows_f, tcols), BF16),
-            vm((units, levels - 1, rows_f, wide), BF16), vm((levels - 1, rows_f, tcols), BF16),
-            vm((units, rows_f, wide), BF16), vm((rows_f, tcols), BF16),
-            vm((units, rows_f, wide), BF16), vm((rows_f, tcols), BF16),
-            vm((4, 8, small_cols), F32), vm((3, 8, small_cols), F32), vm((levels, 8, small_cols), F32),
-            pltpu.SemaphoreType.DMA((units + 1, 5 + 2 * levels)),
-            pltpu.SemaphoreType.DMA((4 + 2 * levels,)),
+            vm((units // 2, levels, rows_f, wide), BF16), vm((levels, rows_f, tcols), BF16),
+            vm((units // 2, levels - 1, rows_f, wide), BF16), vm((levels - 1, rows_f, tcols), BF16),
+            vm((units // 2, rows_f, wide), BF16), vm((rows_f, tcols), BF16),
+            vm((units // 2, rows_f, wide), BF16), vm((rows_f, tcols), BF16),
+            vm((units // 2, levels, 2, rows_f, wide // 2), BF16), vm((units // 2, levels, rows_f, wide // 2), BF16),
+            vm((units // 2, levels - 1, rows_f, wide // 2), BF16),
+            vm((units // 2, rows_f, wide // 2), BF16), vm((units // 2, rows_f, wide // 2), BF16),
+            vm((8, small_cols), F32), vm((4, 8, small_cols // 2), F32), vm((4, 8, small_cols // 2), F32),
+            vm((levels, 8, small_cols // 2), F32),
+            vm((d // LANES, LANES), F32), vm((8, d // LANES, LANES), F32), vm((d // LANES, LANES), F32),
+            vm((levels, d // LANES, LANES), F32),
+            pltpu.SemaphoreType.DMA((units + 1, 7 + 2 * levels)),
+            pltpu.SemaphoreType.DMA((6 + 2 * levels,)),
+            pltpu.SemaphoreType.DMA((12 + 2 * levels,)),
             pltpu.SemaphoreType.DMA((7,)),
         ],
         compiler_params=pltpu.CompilerParams(
@@ -664,7 +929,7 @@
         ),
         name="scan_backward",
     )(
-        px, px, ssd, dy, states, tail, aux, seg_rows, conv_w, conv_b, bias, rate, skip_row, e, et,
+        px, px, y, dy, states, tail, aux, seg_rows, conv_w, conv_b, bias, rate, skip_row, e, rate_t,
         norm_gain, dgain, squares, normed_t, wx, wt, gn, tokens, gb, ggate, gout,
     )
 
@@ -831,41 +1096,10 @@
             return carry
 
         lax.fori_loop(0, length // 64, norm, 0)
-        tail[0:8, :] = jnp.zeros((8, tail_cols), F32)
-        pbuf[0:8, :] = jnp.zeros((8, cols_g), F32)
-        tail_load.stage(2)
-        exchange(0).wait()
-        counts[1] = counts[0] + countr[0]
-        exchange(1).start()
-        for i in range(length // 256):
-            block = slice(i * 256, (i + 1) * 256)
-            normed_t[:, block] = normed[block, :].T
-        leave(2).start()
-        leave(3).start()
-        tail_load.stage(3)
-        exchange(1).wait()
-        counts[2] = counts[1] + countr[1]
-        exchange(2).start()
-        loads[0].stage(2)
-        tail_load.stage(4)
-        exchange(2).wait()
-        counts[3] = counts[2] + countr[2]
-        for k in range(1, levels):
-            spread(k).start()
-        countz[spot.level] = counts[3]
-        loads[0].stage(3)
-        tail_load.stage(5)
-        leave(1).start()
-        project(weight_tail.reshape(d_model, tail_cols), tail, slice(0, tail_cols))
-        leave(4).start()
-        loads[0].stage(4)
-        for k in range(1, levels):
-            spread(k).wait()
-        total = countz[0]
-        for k in range(1, levels):
-            total = total + countz[k]
-        counts[4] = total
-        cums[...] = jnp.zeros_like(cums)
+        def turn_rows(blocks):
+            for i in blocks:
+                block = slice(i * 256, (i + 1) * 256)
+                normed_t[:, block] = normed[block, :].T
 
         def shared(i, carry):
             at = pl.ds(pl.multiple_of(i * rows, rows), rows)
@@ -888,7 +1122,44 @@
             scores[i] = jnp.where(causal, mm_nt(bc[i, :, n:], bc[i, :, 0:n]), 0.0)
             return carry
 
-        lax.fori_loop(0, seq_chunks, shared, 0)
+        tail[0:8, :] = jnp.zeros((8, tail_cols), F32)
+        pbuf[0:8, :] = jnp.zeros((8, cols_g), F32)
+        cums[...] = jnp.zeros_like(cums)
+        tail_load.stage(2)
+        exchange(0).wait()
+        counts[1] = counts[0] + countr[0]
+        exchange(1).start()
+        blocks = length // 256
+        turn_rows(range(blocks // 2))
+        tail_load.stage(3)
+        exchange(1).wait()
+        counts[2] = counts[1] + countr[1]
+        exchange(2).start()
+        turn_rows(range(blocks // 2, blocks))
+        leave(2).start()
+        leave(3).start()
+        tail_load.stage(4)
+        loads[0].stage(2)
+        exchange(2).wait()
+        counts[3] = counts[2] + countr[2]
+        for k in range(1, levels):
+            spread(k).start()
+        countz[spot.level] = counts[3]
+        tail_load.stage(5)
+        leave(1).start()
+        project(weight_tail.reshape(d_model, tail_cols), tail, slice(0, tail_cols))
+        leave(4).start()
+        loads[0].stage(3)
+        lax.fori_loop(0, seq_chunks // 2, shared, 0)
+        loads[0].stage(4)
+        loads[1].stage(2)
+        lax.fori_loop(seq_chunks // 2, seq_chunks, shared, 0)
+        for k in range(1, levels):
+            spread(k).wait()
+        total = countz[0]
+        for k in range(1, levels):
+            total = total + countz[k]
+        counts[4] = total
 
     scan_steps = GROUPS * seq_chunks
     events = {}
@@ -896,7 +1167,7 @@
         begin = max(0, (k - 2) * 3 * seq_chunks // 8)
         times = [begin, *[begin + 1 + delay * seq_chunks // 8 for delay in LOAD_STEPS]]
         if k == 1:
-            times = [None, 1, seq_chunks // 2, seq_chunks - 1]
+            times = [None, None, seq_chunks // 4, 5 * seq_chunks // 8]
         need = min(k * seq_chunks, scan_steps)
         for number, when in enumerate(times):
             if when is not None:
@@ -967,9 +1238,8 @@
                 jnp.concatenate(mixing, axis=1), jnp.concatenate([x_low * masks[0], x_low * masks[1]], axis=0)
             ) + ex[rows : 2 * rows, cols] * yin[:, cols]
             acols = pl.ds(gcol + c * LANES, LANES)
-            y = y + skip_ref[:, acols] * xs[:, cols]
             ssd_ref[:, cols] = y
-            ssd_all[here, acols] = y
+            ssd_all[here, acols] = y + skip_ref[:, acols] * xs[:, cols]
 
     @pl.when(step >= scan_steps)
     def _():
@@ -1170,52 +1440,32 @@
     devices = lax.axis_size("rep") * shards
     levels = shards // 4
     loss_weight = float(rows * devices * width // 8)
-    valid = valid_mask.astype(F32)
-    heads = step_bias.shape[0]
-    inner = out_gain.shape[0]
-    head_width = inner // heads
-    aux, seg_rows = helpers(segment, valid, CHUNK)
-    e, et = head_maps(heads, head_width)
-    rate = -jnp.exp(decay_log)[None, :]
-    skip_row = jnp.repeat(skip_gain, head_width)[None, :]
-    params = (conv_weight, conv_bias[None, :], step_bias[None, :], rate, skip_row)
-    tail_at = 2 * inner
-    tail_pad = -(in_weight.shape[1] - tail_at) % LANES
-    in_tail = jnp.pad(in_weight[:, tail_at:], ((0, 0), (0, tail_pad)))
-    count = jnp.broadcast_to(jnp.sum(valid), (8, LANES))
+    heads, inner = step_bias.shape[0], out_gain.shape[0]
+    aux, seg_rows, count, bias, rate, rate_t, skip_row, conv_row, ngain_row, gain_row, e, in_tail = prepare(
+        segment, valid_mask, step_bias, decay_log, skip_gain, conv_bias, norm_gain, out_gain, in_weight
+    )
+    params = (conv_weight, conv_row, bias, rate, skip_row)
     flat, cotan, target = (v.reshape(rows, width) for v in (tokens, cotangent, teacher))
     (
-        px, ssd, states, tail, normed, normed_t, wx, wt, output, grad_branch, mixed, dy, dz, gn, dgain, sums
+        px, y, states, tail, normed, normed_t, wx, wt, output, grad_branch, mixed, dy, dz, gn, dgain, sums
     ) = first(
-        flat, norm_gain[None, :], aux, seg_rows, count, *params, out_gain[None, :], e, cotan, target,
+        flat, ngain_row, aux, seg_rows, count, *params, gain_row, e, cotan, target,
         in_weight, in_tail, out_weight, levels, loss_weight,
     )
     wx, wt = (w.reshape(-1, w.shape[-1]) for w in (wx, wt))
-    denominator = sums[8, 0] * width
     grad_out = mm_tn(mixed, grad_branch).astype(BF16)
     grad_gate = mm(normed_t, dz).astype(BF16)
-    grad_in, grad_out, grad_tokens, small = back(
-        px, 0, tail, ssd, dy, states, aux, seg_rows, *params, e, et,
-        norm_gain[None, :], dgain, sums[:8], normed_t, wx, wt, gn, flat, grad_branch,
+    grad_in, grad_out, grad_tokens, small, norm_sum = back(
+        px, 0, tail, y, dy, states, aux, seg_rows, *params, e, rate_t,
+        ngain_row, dgain, sums[:8], normed_t, wx, wt, gn, flat, grad_branch,
         grad_gate.reshape(levels, 2, 2, width // shards, inner),
         grad_out.reshape(levels, 2, 2, inner // shards, width), in_weight.shape[1],
     )
-    taps, conv_width = conv_weight.shape
-    extra = small[7, width:]
-    loss = jnp.sum(extra[2 * LANES : 3 * LANES]) / denominator
+    outs = finish(
+        grad_in, grad_out, grad_tokens, output, small, norm_sum, sums, e, *conv_weight.shape, heads, inner
+    )
     return (
-        output.reshape(tokens.shape),
-        loss,
-        grad_tokens.reshape(tokens.shape),
-        small[7, :width],
-        grad_in,
-        small[:taps, :conv_width],
-        small[taps, :conv_width],
-        extra[:heads],
-        extra[LANES : LANES + heads],
-        small[6, :inner].reshape(heads, head_width).sum(axis=1),
-        small[5, :inner],
-        grad_out,
+        outs[0].reshape(tokens.shape), outs[1].reshape(()), outs[2].reshape(tokens.shape), *outs[3:]
     )
 
 

time: 341 us -> 299 us (0.88)
  local copies, waits for them, and re-layouts: 20.6 us -> 0.61 us
  other arithmetic: 11.5 us -> 0 us
  Pallas kernels: 289 us -> 282 us
    pallas_call x1, Pallas kernels: 146 us -> 130 us  [back(): pl.pallas_call(functools.partial(back_kernel, inner=inner, heads=heads, w...]
    slice x8 -> x0, local copies, waits for them, and re-layouts: 9.32 us -> none  [the longest x1 1.53 us: on_device(): small[5, :inner]]
    pallas_call x0 -> x2, Pallas kernels: none -> 7.99 us  [the longest x1 5.84 us: finish(): pl.pallas_call(finish_kernel, grid=(1,), in_specs=[*[anywhere] * 4, *[ful...]
    unnamed x19 -> x6, local copies, waits for them, and re-layouts: 4.54 us -> 0.01 us
    convert_element_type x5 -> x0, other arithmetic: 4.34 us -> none  [the longest x3 2.52 us: same(): return (segment[:, shift:] == segment[:, :-shift]).astype(F32)]
where the time goes in v4:
time: 299 us
  Pallas kernels  282 us (94%)
  matrix products  15.7 us (5%)
    pallas_call x1, Pallas kernels, first(): pl.pallas_call(functools.partial(first_kernel, inner=inner, heads=heads,...  144 us
    pallas_call x1, Pallas kernels, back(): pl.pallas_call(functools.partial(back_kernel, inner=inner, heads=heads, w...  130 us
    dot_general x1, matrix products, mm_tn(): return lax.dot_general(a, b, TN, preferred_element_type=F32)  9.62 us
    dot_general x1, matrix products, mm(): return jnp.dot(a, b, preferred_element_type=F32)  6.08 us

profile of v4, /device:TPU:0, one launch (start us, length us, event | category | flops | bytes accessed | tf_op | source)
XLA Modules:
  0.0 298.8 jit_solution(3784520506839592297)
XLA Ops:
  0.6 2.1 prepare.1
  2.8 144.0 %scan_forward.1 = (f32[1024,2048]{1,0:T(8,128)}, f32[1024,2048]{1,0:T(8,128)}, bf16[1024,2048]{1,0:T(8,128)(2,1)}, f32[1024,384]{1,0:T(8,128)}, bf16[1024,1024]{...) custom-call(bf16[1024,1024]{1,0:T(8,128)(2,1)} %bitcast.19, ...), custom_call_target="tpu_custom_call" | custom-call | tf_op jit(solution)/shard_map/scan_forward/pallas_call | solution.py:1371
  146.8 0.0 copy-start
  146.8 0.0 copy-start.2
  146.8 9.6 %convolution_convert_fusion = bf16[2048,1024]{1,0:T(8,128)(2,1)} fusion(bf16[1024,2048]{1,0:T(8,128)(2,1)} %get-tuple-element.81, bf16[1024,1024]{1,0:T(8,128)(2,1)} %get-tuple-element.79.gb_hbm), kind=kOutput, calls=%fused_computation | convolution fusion | flops 4297064448 | bytes 10485760 | tf_op jit(solution)/shard_map/dot_general | solution.py:28
  156.5 0.0 copy-done
  156.5 0.0 copy-done.2
  156.5 0.0 copy-start.1
  156.5 6.1 %convolution_convert_fusion.1 = bf16[1024,2048]{1,0:T(8,128)(2,1)} fusion(bf16[1024,1024]{1,0:T(8,128)(2,1)S(1)} %copy-done, bf16[1024,2048]{1,0:T(8,128)(2,1)S(1)} %copy-done.2), kind=kOutput, calls=%fused_computation.1 | convolution fusion | flops 4297064448 | bytes 10485760 | tf_op jit(solution)/shard_map/dot_general | solution.py:20
  162.6 0.0 copy-done.1
  162.6 0.6 slice.3.square_ref
  163.2 129.6 %scan_backward.1 = (f32[64,4384]{1,0:T(8,128)}, f32[128,1024]{1,0:T(8,128)}, bf16[1024,1024]{1,0:T(8,128)(2,1)}, f32[8,2560]{1,0:T(8,128)}, f32[8,128]{1,0:T(8,128)}) custom-call(f32[1024,2048]{1,0:T(8,128)} %get-tuple-element.67.px_ref.prev_ref, f32[1024,2048]{1,0:T(8,128)} %get-tuple-element.67.px_ref.prev_ref, f32[1024,2048]{1,0:T(8,128)} %get-tuple-element.68.y_ref, ...), custom_call_target="tpu_custom_call" | custom-call | tf_op jit(solution)/shard_map/scan_backward/pallas_call | solution.py:873
  292.8 5.8 %finish.1 = (bf16[1024,1024]{1,0:T(8,128)(2,1)}, f32[1,1]{1,0:T(1,128)}, bf16[1024,1024]{1,0:T(8,128)(2,1)}, f32[1024]{0:T(1024)}, f32[64,4384]{1,0:T(8,128)}, /...) custom-call(f32[64,4384]{1,0:T(8,128)} %get-tuple-element.82.gi_ref,, ...), custom_call_target="tpu_custom_call" | custom-call | tf_op jit(solution)/shard_map/finish/pallas_call | solution.py:202
Async XLA Ops:
  146.8 9.6 %copy-start = (bf16[1024,1024]{1,0:T(8,128)(2,1)S(1)}, bf16[1024,1024]{1,0:T(8,128)(2,1)}, u32[]{:S(2)}) copy-start(bf16[1024,1024]{1,0:T(8,128)(2,1)} %get-tuple-element.75.normed_t_hbm) | copy-start | bytes 6291460
  146.8 9.6 %copy-start.2 = (bf16[1024,2048]{1,0:T(8,128)(2,1)S(1)}, bf16[1024,2048]{1,0:T(8,128)(2,1)}, u32[]{:S(2)}) copy-start(bf16[1024,2048]{1,0:T(8,128)(2,1)} %get-tuple-element.80) | copy-start | bytes 12582916
  156.5 6.1 %copy-start.1 = (f32[16,128]{1,0:T(8,128)S(1)}, f32[16,128]{1,0:T(8,128)}, u32[]{:S(2)}) copy-start(f32[16,128]{1,0:T(8,128)} %get-tuple-element.74.sums_ref) | copy-start | bytes 24580

commit v5 on v4

--- a/solution.py
+++ b/solution.py
@@ -1007,7 +1007,7 @@
             self.d.wait()
 
 
-LOAD_STEPS = (5, 8, 12)
+LOAD_STEPS = (5, 8, 14)
 
 
 def first_kernel(
@@ -1016,7 +1016,7 @@
     in_hbm, tail_hbm, out_hbm,
     px_ref, ssd_ref, state_out_ref, tail_out, normed_out, normed_t_out, wx_out, wtail_out,
     output_ref, gb_ref, mixed_ref, dy_ref, dz_ref, gn_ref, dgain_ref, small_ref,
-    tokens, normed, normed_t, wx, wg, wo, weight_tail, tail, pbuf, ssd_all, gates, gateds, gms, results, inverses,
+    tokens, normed, normed_t, wx, wg, wo, weight_tail, tail, pbuf, ssd_all, gates, gms, inverses,
     ex, state, xs, xdt, xe, bc, yin, cums, scores, stacks,
     counts, countr, countz, sems, count_sems, copy_sems, leave_sems,
     *, inner, heads, width, levels, seq_chunks, loss_weight,
@@ -1046,7 +1046,7 @@
     for k in range(GROUPS):
         cols = pl.ds(k * (d_model // GROUPS), d_model // GROUPS)
         loads.append((out_hbm.at[:, cols], wo.at[:, :, :, :, cols]))
-    loads = [Load(spot, shard, whole, sems.at[1 + k], k % 2 == 1) for k, (shard, whole) in enumerate(loads)]
+    loads = [Load(spot, shard, whole, sems.at[1 + k], k > 2 and k % 2 == 1) for k, (shard, whole) in enumerate(loads)]
     leaves = [
         (wx, wx_out), (weight_tail, wtail_out), (normed, normed_out), (normed_t, normed_t_out), (tail.at[8:], tail_out)
     ]
@@ -1126,25 +1126,14 @@
         pbuf[0:8, :] = jnp.zeros((8, cols_g), F32)
         cums[...] = jnp.zeros_like(cums)
         tail_load.stage(2)
-        exchange(0).wait()
-        counts[1] = counts[0] + countr[0]
-        exchange(1).start()
         blocks = length // 256
         turn_rows(range(blocks // 2))
         tail_load.stage(3)
-        exchange(1).wait()
-        counts[2] = counts[1] + countr[1]
-        exchange(2).start()
         turn_rows(range(blocks // 2, blocks))
         leave(2).start()
         leave(3).start()
         tail_load.stage(4)
         loads[0].stage(2)
-        exchange(2).wait()
-        counts[3] = counts[2] + countr[2]
-        for k in range(1, levels):
-            spread(k).start()
-        countz[spot.level] = counts[3]
         tail_load.stage(5)
         leave(1).start()
         project(weight_tail.reshape(d_model, tail_cols), tail, slice(0, tail_cols))
@@ -1154,12 +1143,6 @@
         loads[0].stage(4)
         loads[1].stage(2)
         lax.fori_loop(seq_chunks // 2, seq_chunks, shared, 0)
-        for k in range(1, levels):
-            spread(k).wait()
-        total = countz[0]
-        for k in range(1, levels):
-            total = total + countz[k]
-        counts[4] = total
 
     scan_steps = GROUPS * seq_chunks
     events = {}
@@ -1185,8 +1168,59 @@
     @pl.when(step == scan_steps)
     def _():
         leave(0).start()
-        for k, number in late:
-            loads[k].stage(number)
+        rest = list(late)
+        flat_gate = wg.reshape(d_model, inner)
+        for k in range(GROUPS):
+            while True:
+                one = rest.pop(0)
+                loads[one[0]].stage(one[1])
+                if one == (GROUPS + k, 5):
+                    break
+            cols = slice(k * cols_g, (k + 1) * cols_g)
+            gates[:, cols] = mm(normed[...], flat_gate[:, cols])
+
+        def gate_norm(i, carry):
+            at = pl.ds(pl.multiple_of(i * 64, 64), 64)
+            squares = jnp.zeros((64, LANES), F32)
+            for c in range(inner // LANES):
+                cols = slice(c * LANES, (c + 1) * LANES)
+                gate = gates[at, cols]
+                gated = ssd_all[at, cols] * (gate * sigmoid(gate))
+                squares = squares + gated * gated
+            inverse = lax.rsqrt(jnp.sum(squares, axis=1, keepdims=True) / inner + EPS)
+            inverses[at, :] = jnp.broadcast_to(inverse, (64, LANES))
+            return carry
+
+        parts = 4
+        blocks = length // 64
+        share = -(-len(rest) // parts)
+        for i in range(parts):
+            for k, number in rest[i * share : (i + 1) * share]:
+                loads[k].stage(number)
+            lax.fori_loop(i * blocks // parts, (i + 1) * blocks // parts, gate_norm, 0)
+        for k in range(2 * GROUPS, 3 * GROUPS):
+            loads[k].stage(5)
+
+    for i in range(4):
+
+        @pl.when(step == (1 + i) * seq_chunks // 2 + 1)
+        def _(i=i):
+            if i < 3:
+                exchange(i).wait()
+                counts[i + 1] = counts[i] + countr[i]
+            if i < 2:
+                exchange(i + 1).start()
+            elif i == 2:
+                for k in range(1, levels):
+                    spread(k).start()
+                countz[spot.level] = counts[3]
+            else:
+                for k in range(1, levels):
+                    spread(k).wait()
+                total = countz[0]
+                for k in range(1, levels):
+                    total = total + countz[k]
+                counts[4] = total
 
     for g in range(GROUPS):
 
@@ -1244,22 +1278,16 @@
     @pl.when(step >= scan_steps)
     def _():
         turn = step - scan_steps
-        block_rows = gates.shape[0]
+        block_rows = gms.shape[0]
         base = pl.multiple_of(turn * block_rows, block_rows)
         flat_gate = wg.reshape(d_model, inner)
         flat_out = wo.reshape(inner, d_model)
         sub = 64
-        own_rows = normed[pl.ds(base, block_rows), :]
-        for k in range(GROUPS):
-            cols = slice(k * cols_g, (k + 1) * cols_g)
-            gates[:, cols] = mm(own_rows, flat_gate[:, cols])
 
         @pl.when(turn == 0)
         def _():
             dgain_ref[...] = jnp.zeros_like(dgain_ref)
             small_ref[...] = jnp.zeros_like(small_ref)
-            for k in range(2 * GROUPS, 3 * GROUPS):
-                loads[k].stage(5)
 
         def norm_of(i):
             at = pl.ds(pl.multiple_of(i * sub, sub), sub)
@@ -1267,23 +1295,16 @@
 
         def forward_part(i, carry):
             at, full_at = norm_of(i)
-            squares = jnp.zeros((sub, LANES), F32)
+            inverse = inverses[full_at, :]
             for c in range(inner // LANES):
                 cols = slice(c * LANES, (c + 1) * LANES)
-                gate = gates[at, cols]
-                gated = ssd_all[full_at, cols] * (gate * sigmoid(gate))
-                gateds[at, cols] = gated
-                squares = squares + gated * gated
-            inverse = lax.rsqrt(jnp.sum(squares, axis=1, keepdims=True) / inner + EPS)
-            for c in range(inner // LANES):
-                cols = slice(c * LANES, (c + 1) * LANES)
-                unit = gateds[at, cols] * inverse
-                gateds[at, cols] = unit
+                gate = gates[full_at, cols]
+                unit = ssd_all[full_at, cols] * (gate * sigmoid(gate)) * inverse
                 mixed_ref[at, cols] = (unit * gain_ref[:, cols]).astype(BF16)
-            inverses[at, :] = jnp.broadcast_to(inverse, (sub, LANES))
             return carry
 
         lax.fori_loop(0, block_rows // sub, forward_part, 0)
+        results = gms.at[:, 0:d_model]
         results[...] = mm(mixed_ref[...], flat_out[...])
         scale = 2.0 * loss_weight / (counts[4, 0:1, :] * d_model)
 
@@ -1313,21 +1334,22 @@
             cross = jnp.zeros((sub, LANES), F32)
             for c in range(inner // LANES):
                 cols = slice(c * LANES, (c + 1) * LANES)
-                cross = cross + gms[at, cols] * gain_ref[:, cols] * gateds[at, cols]
-            inverse = inverses[at, :]
+                cross = cross + gms[at, cols] * mixed_ref[at, cols].astype(F32)
+            inverse = inverses[full_at, :]
             mean_cross = jnp.sum(cross, axis=1, keepdims=True) / inner
             for c in range(inner // LANES):
                 cols = slice(c * LANES, (c + 1) * LANES)
-                gate = gates[at, cols]
+                gate = gates[full_at, cols]
                 sig = sigmoid(gate)
                 silu = gate * sig
-                unit = gateds[at, cols]
+                ssd = ssd_all[full_at, cols]
+                unit = ssd * silu * inverse
                 grad_mixed = gms[at, cols]
                 dgain_ref[:, cols] += jnp.sum((grad_mixed * unit).reshape(sub // 8, 8, LANES), axis=0)
                 grad_gated = inverse * (grad_mixed * gain_ref[:, cols] - unit * mean_cross)
                 dy_ref[at, cols] = (grad_gated * silu).astype(BF16)
                 dz_ref[at, cols] = (
-                    grad_gated * ssd_all[full_at, cols] * (sig + silu * (1.0 - sig))
+                    grad_gated * ssd * (sig + silu * (1.0 - sig))
                 ).astype(BF16)
             return carry
 
@@ -1361,7 +1383,9 @@
         return s % chunks, s // chunks
 
     block = lambda h: pl.BlockSpec((h, wide), scan_block)
-    late = lambda w: pl.BlockSpec((tall, w), lambda s: (jnp.maximum(s - scan_steps, 0), 0))
+    late = lambda w, deep=2: pl.BlockSpec(
+        (tall, w), lambda s: (jnp.maximum(s - scan_steps, 0), 0), pipeline_mode=pl.Buffered(deep)
+    )
     whole = lambda a: pl.BlockSpec(a.shape, lambda s: (0,) * a.ndim, pipeline_mode=pl.Buffered(1))
     fixed = lambda *dims: pl.BlockSpec(dims, lambda s: (0,) * len(dims))
     anywhere = pl.BlockSpec(memory_space=pl.ANY)
@@ -1396,8 +1420,7 @@
             vm(wide_shape, BF16), vm(wide_shape, BF16), vm((levels, 2, 2, 2 * rows_f, d), BF16),
             vm((levels, 2, 2, rows_f, tcols), BF16),
             vm((length + 8, tcols), F32), vm((length + 8, wide), F32), vm((length, inner), F32),
-            vm((tall, inner), F32), vm((tall, inner), F32), vm((tall, inner), F32), vm((tall, d), F32),
-            vm((tall, LANES), F32),
+            vm((length, inner), F32), vm((tall, inner), F32), vm((length, LANES), F32),
             vm((3 * r, wide), F32), vm((n, wide), F32), vm((r, wide), F32), vm((r, wide), BF16), vm((r, wide), BF16),
             vm((chunks, r, 2 * n), BF16), vm((r, wide), F32), vm((chunks, r, LANES), F32), vm((chunks, r, r), F32),
             vm((chunks, 3 * r, 2 * heads), BF16),

time: 299 us -> 292 us (0.977)
  Pallas kernels: 282 us -> 275 us
    pallas_call x1, Pallas kernels: 144 us -> 136 us  [first(): pl.pallas_call(functools.partial(first_kernel, inner=inner, heads=heads,...]
where the time goes in v5:
time: 292 us
  Pallas kernels  275 us (94%)
  matrix products  15.7 us (5%)
    pallas_call x1, Pallas kernels, first(): pl.pallas_call(functools.partial(first_kernel, inner=inner, heads=heads,...  136 us
    pallas_call x1, Pallas kernels, back(): pl.pallas_call(functools.partial(back_kernel, inner=inner, heads=heads, w...  131 us
    dot_general x1, matrix products, mm_tn(): return lax.dot_general(a, b, TN, preferred_element_type=F32)  9.62 us
    dot_general x1, matrix products, mm(): return jnp.dot(a, b, preferred_element_type=F32)  6.08 us
    pallas_call x1, Pallas kernels, finish(): pl.pallas_call(finish_kernel, grid=(1,), in_specs=[*[anywhere] * 4, *[ful...  5.84 us

profile of v5, /device:TPU:0, one launch (start us, length us, event | category | flops | bytes accessed | tf_op | source)
XLA Modules:
  0.0 291.9 jit_solution(6931807482154275037)
XLA Ops:
  0.6 2.1 prepare.1
  2.8 136.1 %scan_forward.1 = (f32[1024,2048]{1,0:T(8,128)}, f32[1024,2048]{1,0:T(8,128)}, bf16[1024,2048]{1,0:T(8,128)(2,1)}, f32[1024,384]{1,0:T(8,128)}, bf16[1024,1024]{...) custom-call(bf16[1024,1024]{1,0:T(8,128)(2,1)} %bitcast.19, ...), custom_call_target="tpu_custom_call" | custom-call | tf_op jit(solution)/shard_map/scan_forward/pallas_call | solution.py:1395
  138.9 0.0 copy-start
  138.9 0.0 copy-start.2
  139.0 9.6 %convolution_convert_fusion = bf16[2048,1024]{1,0:T(8,128)(2,1)} fusion(bf16[1024,2048]{1,0:T(8,128)(2,1)} %get-tuple-element.81, bf16[1024,1024]{1,0:T(8,128)(2,1)} %get-tuple-element.79.gb_hbm), kind=kOutput, calls=%fused_computation | convolution fusion | flops 4297064448 | bytes 10485760 | tf_op jit(solution)/shard_map/dot_general | solution.py:28
  148.6 0.0 copy-done
  148.6 0.0 copy-done.2
  148.6 0.0 copy-start.1
  148.6 6.1 %convolution_convert_fusion.1 = bf16[1024,2048]{1,0:T(8,128)(2,1)} fusion(bf16[1024,1024]{1,0:T(8,128)(2,1)S(1)} %copy-done, bf16[1024,2048]{1,0:T(8,128)(2,1)S(1)} %copy-done.2), kind=kOutput, calls=%fused_computation.1 | convolution fusion | flops 4297064448 | bytes 10485760 | tf_op jit(solution)/shard_map/dot_general | solution.py:20
  154.7 0.0 copy-done.1
  154.7 0.6 slice.3.square_ref
  155.3 130.6 %scan_backward.1 = (f32[64,4384]{1,0:T(8,128)}, f32[128,1024]{1,0:T(8,128)}, bf16[1024,1024]{1,0:T(8,128)(2,1)}, f32[8,2560]{1,0:T(8,128)}, f32[8,128]{1,0:T(8,128)}) custom-call(f32[1024,2048]{1,0:T(8,128)} %get-tuple-element.67.px_ref.prev_ref, f32[1024,2048]{1,0:T(8,128)} %get-tuple-element.67.px_ref.prev_ref, f32[1024,2048]{1,0:T(8,128)} %get-tuple-element.68.y_ref, ...), custom_call_target="tpu_custom_call" | custom-call | tf_op jit(solution)/shard_map/scan_backward/pallas_call | solution.py:873
  285.9 5.8 %finish.1 = (bf16[1024,1024]{1,0:T(8,128)(2,1)}, f32[1,1]{1,0:T(1,128)}, bf16[1024,1024]{1,0:T(8,128)(2,1)}, f32[1024]{0:T(1024)}, f32[64,4384]{1,0:T(8,128)}, /...) custom-call(f32[64,4384]{1,0:T(8,128)} %get-tuple-element.82.gi_ref,, ...), custom_call_target="tpu_custom_call" | custom-call | tf_op jit(solution)/shard_map/finish/pallas_call | solution.py:202
Async XLA Ops:
  138.9 9.6 %copy-start = (bf16[1024,1024]{1,0:T(8,128)(2,1)S(1)}, bf16[1024,1024]{1,0:T(8,128)(2,1)}, u32[]{:S(2)}) copy-start(bf16[1024,1024]{1,0:T(8,128)(2,1)} %get-tuple-element.75.normed_t_hbm) | copy-start | bytes 6291460
  138.9 9.6 %copy-start.2 = (bf16[1024,2048]{1,0:T(8,128)(2,1)S(1)}, bf16[1024,2048]{1,0:T(8,128)(2,1)}, u32[]{:S(2)}) copy-start(bf16[1024,2048]{1,0:T(8,128)(2,1)} %get-tuple-element.80) | copy-start | bytes 12582916
  148.6 6.1 %copy-start.1 = (f32[16,128]{1,0:T(8,128)S(1)}, f32[16,128]{1,0:T(8,128)}, u32[]{:S(2)}) copy-start(f32[16,128]{1,0:T(8,128)} %get-tuple-element.74.sums_ref) | copy-start | bytes 24580

commit v6 on v5

--- a/solution.py
+++ b/solution.py
@@ -423,8 +423,8 @@
 
 GROUPS = 4
 STARTS = (0, 2, 4, 6, 8, 11, 13, 16, 18, 20, 24)
-UNIT_DELAYS = (0, 1, 5, 9, 11)
-SPLIT_DELAYS = (0, 1, 5, 8, 11, 13)
+UNIT_DELAYS = (0, 2, 6, 10, 12)
+SPLIT_DELAYS = (0, 2, 6, 9, 12, 14)
 
 
 def back_kernel(
@@ -611,15 +611,22 @@
     for c in range(tiles):
         cols = slice(c * LANES, (c + 1) * LANES)
         wcols = pl.ds(gcol + c * LANES, LANES)
-        pre = conv_pre(xbuf, cols, wcols)
-        sig = sigmoid(pre)
-        act = pre * sig
-        slope[:, cols] = sig + act * (1.0 - sig)
-        xs[:, cols] = act
-        scaled = act * ex[0:rows, cols]
-        xdt[:, cols] = scaled.astype(BF16)
-        xe[:, cols] = (scaled * ex[2 * rows : 3 * rows, cols]).astype(BF16)
-        dye[:, cols] = (dy_ref[:, cols].astype(F32) * ex[rows : 2 * rows, cols]).astype(BF16)
+        for at in range(0, rows, 64):
+            part_rows = slice(at, at + 64)
+            pre = cb_ref[:, wcols] + cw_ref[0:1, wcols] * xbuf[8 + at : 72 + at, cols]
+            for k in range(1, taps):
+                shifted = xbuf[8 + at - k : 72 + at - k, cols]
+                pre = pre + (cw_ref[k : k + 1, wcols] * shifted) * marks[k][part_rows]
+            sig = sigmoid(pre)
+            act = pre * sig
+            slope[part_rows, cols] = sig + act * (1.0 - sig)
+            xs[part_rows, cols] = act
+            scaled = act * ex[part_rows, cols]
+            xdt[part_rows, cols] = scaled.astype(BF16)
+            xe[part_rows, cols] = (scaled * ex[2 * rows + at : 2 * rows + at + 64, cols]).astype(BF16)
+            dye[part_rows, cols] = (
+                dy_ref[part_rows, cols].astype(F32) * ex[rows + at : rows + at + 64, cols]
+            ).astype(BF16)
     b, cc = bc[chunk, :, 0:n], bc[chunk, :, n:]
     state_low = state_ref[...]
     adj_low = adj[...].astype(BF16)

time: 292 us -> 288 us (0.986)
  Pallas kernels: 275 us -> 271 us
    pallas_call x1, Pallas kernels: 131 us -> 127 us  [back(): pl.pallas_call(functools.partial(back_kernel, inner=inner, heads=heads, w...]
where the time goes in v6:
time: 288 us
  Pallas kernels  271 us (94%)
  matrix products  15.7 us (5%)
    pallas_call x1, Pallas kernels, first(): pl.pallas_call(functools.partial(first_kernel, inner=inner, heads=heads,...  136 us
    pallas_call x1, Pallas kernels, back(): pl.pallas_call(functools.partial(back_kernel, inner=inner, heads=heads, w...  127 us
    dot_general x1, matrix products, mm_tn(): return lax.dot_general(a, b, TN, preferred_element_type=F32)  9.62 us
    dot_general x1, matrix products, mm(): return jnp.dot(a, b, preferred_element_type=F32)  6.08 us
    pallas_call x1, Pallas kernels, finish(): pl.pallas_call(finish_kernel, grid=(1,), in_specs=[*[anywhere] * 4, *[ful...  5.84 us

profile of v6, /device:TPU:0, one launch (start us, length us, event | category | flops | bytes accessed | tf_op | source)
XLA Modules:
  0.0 287.8 jit_solution(15564838302934943242)
XLA Ops:
  0.6 2.1 prepare.1
  2.8 136.1 %scan_forward.1 = (f32[1024,2048]{1,0:T(8,128)}, f32[1024,2048]{1,0:T(8,128)}, bf16[1024,2048]{1,0:T(8,128)(2,1)}, f32[1024,384]{1,0:T(8,128)}, bf16[1024,1024]{...) custom-call(bf16[1024,1024]{1,0:T(8,128)(2,1)} %bitcast.19, ...), custom_call_target="tpu_custom_call" | custom-call | tf_op jit(solution)/shard_map/scan_forward/pallas_call | solution.py:1402
  138.9 0.0 copy-start
  138.9 0.0 copy-start.2
  139.0 9.6 %convolution_convert_fusion = bf16[2048,1024]{1,0:T(8,128)(2,1)} fusion(bf16[1024,2048]{1,0:T(8,128)(2,1)} %get-tuple-element.81, bf16[1024,1024]{1,0:T(8,128)(2,1)} %get-tuple-element.79.gb_hbm), kind=kOutput, calls=%fused_computation | convolution fusion | flops 4297064448 | bytes 10485760 | tf_op jit(solution)/shard_map/dot_general | solution.py:28
  148.6 0.0 copy-done
  148.6 0.0 copy-done.2
  148.6 0.0 copy-start.1
  148.6 6.1 %convolution_convert_fusion.1 = bf16[1024,2048]{1,0:T(8,128)(2,1)} fusion(bf16[1024,1024]{1,0:T(8,128)(2,1)S(1)} %copy-done, bf16[1024,2048]{1,0:T(8,128)(2,1)S(1)} %copy-done.2), kind=kOutput, calls=%fused_computation.1 | convolution fusion | flops 4297064448 | bytes 10485760 | tf_op jit(solution)/shard_map/dot_general | solution.py:20
  154.7 0.0 copy-done.1
  154.7 0.6 slice.3.square_ref
  155.3 126.5 %scan_backward.1 = (f32[64,4384]{1,0:T(8,128)}, f32[128,1024]{1,0:T(8,128)}, bf16[1024,1024]{1,0:T(8,128)(2,1)}, f32[8,2560]{1,0:T(8,128)}, f32[8,128]{1,0:T(8,128)}) custom-call(f32[1024,2048]{1,0:T(8,128)} %get-tuple-element.67.px_ref.prev_ref, f32[1024,2048]{1,0:T(8,128)} %get-tuple-element.67.px_ref.prev_ref, f32[1024,2048]{1,0:T(8,128)} %get-tuple-element.68.y_ref, ...), custom_call_target="tpu_custom_call" | custom-call | tf_op jit(solution)/shard_map/scan_backward/pallas_call | solution.py:880
  281.8 5.8 %finish.1 = (bf16[1024,1024]{1,0:T(8,128)(2,1)}, f32[1,1]{1,0:T(1,128)}, bf16[1024,1024]{1,0:T(8,128)(2,1)}, f32[1024]{0:T(1024)}, f32[64,4384]{1,0:T(8,128)}, /...) custom-call(f32[64,4384]{1,0:T(8,128)} %get-tuple-element.82.gi_ref,, ...), custom_call_target="tpu_custom_call" | custom-call | tf_op jit(solution)/shard_map/finish/pallas_call | solution.py:202
Async XLA Ops:
  138.9 9.6 %copy-start = (bf16[1024,1024]{1,0:T(8,128)(2,1)S(1)}, bf16[1024,1024]{1,0:T(8,128)(2,1)}, u32[]{:S(2)}) copy-start(bf16[1024,1024]{1,0:T(8,128)(2,1)} %get-tuple-element.75.normed_t_hbm) | copy-start | bytes 6291460
  138.9 9.6 %copy-start.2 = (bf16[1024,2048]{1,0:T(8,128)(2,1)S(1)}, bf16[1024,2048]{1,0:T(8,128)(2,1)}, u32[]{:S(2)}) copy-start(bf16[1024,2048]{1,0:T(8,128)(2,1)} %get-tuple-element.80) | copy-start | bytes 12582916
  148.6 6.1 %copy-start.1 = (f32[16,128]{1,0:T(8,128)S(1)}, f32[16,128]{1,0:T(8,128)}, u32[]{:S(2)}) copy-start(f32[16,128]{1,0:T(8,128)} %get-tuple-element.74.sums_ref) | copy-start | bytes 24580

commit v7 on v6

--- a/solution.py
+++ b/solution.py
@@ -1255,11 +1255,19 @@
         px_ref[...] = pbuf[pl.ds(start + 8, rows), :]
         for c in range(tiles):
             cols = slice(c * LANES, (c + 1) * LANES)
-            act = conv(pbuf, start, cols, pl.ds(gcol + c * LANES, LANES), marks)
-            xs[:, cols] = act
-            scaled = act * ex[0:rows, cols]
-            xdt[:, cols] = scaled.astype(BF16)
-            xe[:, cols] = (scaled * ex[2 * rows : 3 * rows, cols]).astype(BF16)
+            wcols = pl.ds(gcol + c * LANES, LANES)
+            block = pbuf[pl.ds(start, rows + 8), cols]
+            for at in range(0, rows, 64):
+                part_rows = slice(at, at + 64)
+                pre = cb_ref[:, wcols] + cw_ref[0:1, wcols] * block[8 + at : 72 + at]
+                for k in range(1, taps):
+                    shifted = block[8 + at - k : 72 + at - k]
+                    pre = pre + (cw_ref[k : k + 1, wcols] * shifted) * marks[k][part_rows]
+                act = pre * sigmoid(pre)
+                xs[part_rows, cols] = act
+                scaled = act * ex[part_rows, cols]
+                xdt[part_rows, cols] = scaled.astype(BF16)
+                xe[part_rows, cols] = (scaled * ex[2 * rows + at : 2 * rows + at + 64, cols]).astype(BF16)
         b, cc = bc[chunk, :, 0:n], bc[chunk, :, n:]
         state_low = state[...].astype(BF16)
         state_out_ref[...] = state_low

time: 288 us -> 286 us (level)
  Pallas kernels: 271 us -> 268 us
where the time goes in v7:
time: 286 us
  Pallas kernels  268 us (94%)
  matrix products  15.7 us (5%)
    pallas_call x1, Pallas kernels, first(): pl.pallas_call(functools.partial(first_kernel, inner=inner, heads=heads,...  136 us
    pallas_call x1, Pallas kernels, back(): pl.pallas_call(functools.partial(back_kernel, inner=inner, heads=heads, w...  124 us
    dot_general x1, matrix products, mm_tn(): return lax.dot_general(a, b, TN, preferred_element_type=F32)  9.62 us
    dot_general x1, matrix products, mm(): return jnp.dot(a, b, preferred_element_type=F32)  6.08 us
    pallas_call x1, Pallas kernels, finish(): pl.pallas_call(finish_kernel, grid=(1,), in_specs=[*[anywhere] * 4, *[ful...  5.84 us

profile of v7, /device:TPU:0, one launch (start us, length us, event | category | flops | bytes accessed | tf_op | source)
XLA Modules:
  0.0 285.7 jit_solution(15485358518672604238)
XLA Ops:
  0.6 2.1 prepare.1
  2.8 136.2 %scan_forward.1 = (f32[1024,2048]{1,0:T(8,128)}, f32[1024,2048]{1,0:T(8,128)}, bf16[1024,2048]{1,0:T(8,128)(2,1)}, f32[1024,384]{1,0:T(8,128)}, bf16[1024,1024]{...) custom-call(bf16[1024,1024]{1,0:T(8,128)(2,1)} %bitcast.19, ...), custom_call_target="tpu_custom_call" | custom-call | tf_op jit(solution)/shard_map/scan_forward/pallas_call | solution.py:1410
  139.0 0.0 copy-start
  139.0 0.0 copy-start.2
  139.0 9.6 %convolution_convert_fusion = bf16[2048,1024]{1,0:T(8,128)(2,1)} fusion(bf16[1024,2048]{1,0:T(8,128)(2,1)} %get-tuple-element.81, bf16[1024,1024]{1,0:T(8,128)(2,1)} %get-tuple-element.79.gb_hbm), kind=kOutput, calls=%fused_computation | convolution fusion | flops 4297064448 | bytes 10485760 | tf_op jit(solution)/shard_map/dot_general | solution.py:28
  148.7 0.0 copy-done
  148.7 0.0 copy-done.2
  148.7 0.0 copy-start.1
  148.7 6.1 %convolution_convert_fusion.1 = bf16[1024,2048]{1,0:T(8,128)(2,1)} fusion(bf16[1024,1024]{1,0:T(8,128)(2,1)S(1)} %copy-done, bf16[1024,2048]{1,0:T(8,128)(2,1)S(1)} %copy-done.2), kind=kOutput, calls=%fused_computation.1 | convolution fusion | flops 4297064448 | bytes 10485760 | tf_op jit(solution)/shard_map/dot_general | solution.py:20
  154.7 0.0 copy-done.1
  154.7 0.6 slice.3.square_ref
  155.3 124.3 %scan_backward.1 = (f32[64,4384]{1,0:T(8,128)}, f32[128,1024]{1,0:T(8,128)}, bf16[1024,1024]{1,0:T(8,128)(2,1)}, f32[8,2560]{1,0:T(8,128)}, f32[8,128]{1,0:T(8,128)}) custom-call(f32[1024,2048]{1,0:T(8,128)} %get-tuple-element.67.px_ref.prev_ref, f32[1024,2048]{1,0:T(8,128)} %get-tuple-element.67.px_ref.prev_ref, f32[1024,2048]{1,0:T(8,128)} %get-tuple-element.68.y_ref, ...), custom_call_target="tpu_custom_call" | custom-call | tf_op jit(solution)/shard_map/scan_backward/pallas_call | solution.py:880
  279.7 5.8 %finish.1 = (bf16[1024,1024]{1,0:T(8,128)(2,1)}, f32[1,1]{1,0:T(1,128)}, bf16[1024,1024]{1,0:T(8,128)(2,1)}, f32[1024]{0:T(1024)}, f32[64,4384]{1,0:T(8,128)}, /...) custom-call(f32[64,4384]{1,0:T(8,128)} %get-tuple-element.82.gi_ref,, ...), custom_call_target="tpu_custom_call" | custom-call | tf_op jit(solution)/shard_map/finish/pallas_call | solution.py:202
Async XLA Ops:
  139.0 9.6 %copy-start = (bf16[1024,1024]{1,0:T(8,128)(2,1)S(1)}, bf16[1024,1024]{1,0:T(8,128)(2,1)}, u32[]{:S(2)}) copy-start(bf16[1024,1024]{1,0:T(8,128)(2,1)} %get-tuple-element.75.normed_t_hbm) | copy-start | bytes 6291460
  139.0 9.6 %copy-start.2 = (bf16[1024,2048]{1,0:T(8,128)(2,1)S(1)}, bf16[1024,2048]{1,0:T(8,128)(2,1)}, u32[]{:S(2)}) copy-start(bf16[1024,2048]{1,0:T(8,128)(2,1)} %get-tuple-element.80) | copy-start | bytes 12582916
  148.7 6.1 %copy-start.1 = (f32[16,128]{1,0:T(8,128)S(1)}, f32[16,128]{1,0:T(8,128)}, u32[]{:S(2)}) copy-start(f32[16,128]{1,0:T(8,128)} %get-tuple-element.74.sums_ref) | copy-start | bytes 24580
